TPU v7x, 32 devices: a whole 2x2x4 slice. The times are simulated.
32 devices in a mesh: grp: 2 (over y), seq: 8 (over z, x), mdl: 2 (over core).
Axes of the slice: x: 2, y: 2, z: 4, core: 2. Of those that a mesh axis runs over, the one named last changes fastest.
Arguments:
- tokens_in: bfloat16 [64, 8192], P(('grp', 'seq'), 'mdl'), parts along dimension 0, may hold values from -180 to 180
- norm_gain: float32 [8192], P('mdl'), may hold values from 0.5 to 1.5
- in_proj: bfloat16 [8, 3, 1024, 8192], P('seq', None, None, 'mdl'), may hold values from -0.0625 to 0.0625
- short_taps: float32 [7, 3, 8192], P(None, None, 'seq'), may hold values from -2.5 to 2.5
- long_taps: float32 [512, 128], replicated, may hold values from -0.5 to 0.5
- skip_bias: float32 [8192], P('seq'), may hold values from -6 to 6
- out_proj: bfloat16 [8192, 2, 4096], P('seq', 'mdl'), may hold values from -0.0625 to 0.0625
Outputs:
- mixed: bfloat16 [64, 8192], P('grp', 'seq'), parts along dimension 0
There are 2 independent parts, one for each index of `grp`. A program takes and returns all parts, laid end to end along the dimension named above; an argument that names none is the same for every part. Nothing has to cross between parts.
All inputs are finite; a program needn't handle non-finite values.
Results may differ from a plain program's by a relative error of at most 0.007.
Values may be sent and summed in bfloat16 or wider, within the bound.
No kernel may reach another device: no remote copies, remote signals or barrier semaphores. Data moves between devices by JAX's collectives and lax.ppermute only.
A program may use at most 320 MiB of HBM per device.

v0:
```python
import jax
import jax.numpy as jnp
from jax import lax
from jax.sharding import PartitionSpec as P

D = 8192


EPSILON = 1e-06


def build_toeplitz(channel_taps):
    chan_width, filt_len = channel_taps.shape
    blank = jnp.zeros((chan_width, filt_len), jnp.float32)
    framed = jnp.concatenate([blank, channel_taps, blank], axis=1)
    flipped = framed[:, ::-1]
    repeated = jnp.tile(flipped, (1, filt_len + 1))
    window = repeated[:, filt_len - 1 : filt_len - 1 + filt_len * (3 * filt_len - 1)]
    return window.reshape(chan_width, filt_len, 3 * filt_len - 1)[:, :, : 2 * filt_len]


def mix_channels(summed, short_local, bias_local, long_taps, first_channel, chan_width):
    token_count = summed.shape[0]
    taps_short = short_local.shape[0]
    padded = jnp.pad(summed, ((taps_short - 1, 0), (0, 0), (0, 0)))
    features = jnp.zeros(summed.shape, jnp.float32)
    for offset in range(taps_short):
        features = (
            features
            + short_local[offset][None, :, :]
            * padded[taps_short - 1 - offset : taps_short - 1 - offset + token_count]
        )
    gated_prod = features[:, 1, :] * features[:, 2, :]
    group_count = long_taps.shape[0]
    filt_len = long_taps.shape[1]
    group_width = D // group_count
    channel_ids = first_channel + jnp.arange(chan_width, dtype=jnp.int32)
    select_groups = (
        channel_ids[:, None] // group_width == jnp.arange(group_count, dtype=jnp.int32)[None, :]
    ).astype(jnp.float32)
    channel_taps = jnp.dot(select_groups, long_taps, precision=lax.Precision.HIGHEST)
    toeplitz = build_toeplitz(channel_taps)
    blocks = -(-token_count // filt_len)
    framed = jnp.pad(gated_prod, ((filt_len, blocks * filt_len - token_count), (0, 0))).reshape(
        blocks + 1, filt_len, chan_width
    )
    block_pairs = jnp.concatenate([framed[:-1], framed[1:]], axis=1)
    mixed_long = jnp.einsum("ctk,nkc->ntc", toeplitz, block_pairs, precision=lax.Precision.HIGHEST)
    mixed_long = mixed_long.reshape(blocks * filt_len, chan_width)[:token_count]
    mixed_long = mixed_long + bias_local[None, :] * gated_prod
    return (features[:, 0, :] * mixed_long).astype(jnp.bfloat16)


def contract_last(left, right):
    return lax.dot_general(
        left, right, (((1,), (1,)), ((), ())), preferred_element_type=jnp.float32
    )


def per_device(tokens_in, norm_gain, in_proj, short_taps, long_taps, skip_bias, out_proj):
    half_width = tokens_in.shape[1]
    chan_dev = in_proj.shape[2] // 2
    seq_index = lax.axis_index("seq")
    mdl_index = lax.axis_index("mdl")
    weights_in = in_proj.reshape(-1, half_width)
    values = tokens_in.astype(jnp.float32)
    squares = lax.psum(jnp.sum(values * values, axis=1), "mdl")
    scale_rows = lax.rsqrt(squares / D + EPSILON)
    normed = (values * scale_rows[:, None] * norm_gain[None, :]).astype(jnp.bfloat16)
    partial_value = contract_last(lax.all_gather(normed, "seq", axis=0, tiled=True), weights_in)
    token_count = partial_value.shape[0]
    partial_value = partial_value.reshape(token_count, 3, 2, chan_dev)
    summed = lax.psum_scatter(partial_value, "mdl", scatter_dimension=2, tiled=True).reshape(
        token_count, 3, chan_dev
    )
    short_local = lax.dynamic_slice_in_dim(short_taps, mdl_index * chan_dev, chan_dev, 2)
    bias_local = lax.dynamic_slice_in_dim(skip_bias, mdl_index * chan_dev, chan_dev, 0)
    own_mixed = mix_channels(
        summed,
        short_local,
        bias_local,
        long_taps,
        seq_index * 2 * chan_dev + mdl_index * chan_dev,
        chan_dev,
    )
    out_cols = out_proj.shape[0]
    out_rows = out_proj.reshape(out_cols, -1)
    folded = contract_last(lax.all_gather(own_mixed, "seq", axis=1, tiled=True), out_rows)
    return lax.psum(folded, "mdl").astype(jnp.bfloat16)


def solution(mesh):
    in_specs = (
        P(("grp", "seq"), "mdl"),
        P("mdl"),
        P("seq", None, None, "mdl"),
        P(None, None, "seq"),
        P(),
        P("seq"),
        P("seq", "mdl", None),
    )
    out_specs = P("grp", "seq")
    return jax.shard_map(
        per_device, mesh=mesh, in_specs=in_specs, out_specs=out_specs, check_vma=False
    )
```

profile of v0, /device:TPU:0, one launch (start us, length us, event | category | flops | bytes accessed | tf_op | source)
XLA Modules:
  0.0 439.3 jit_solution(12658814298557197857)
XLA Ops:
  6.5 0.0 copy-start
  6.5 0.0 all-reduce.7.cloned.1.call-start
  6.5 0.9 fusion.19
  7.5 2.6 psum.14
  10.1 0.8 fusion.26
  10.9 32.4 %all-gather = bf16[8,4,4096]{2,1,0:T(4,128)(2,1)S(1)} all-gather(bf16[1,4,4096]{2,1,0:T(4,128)(2,1)S(1)} %fusion.26), channel_id=1, replica_groups=mesh['grp'=2,'seq'=8,'mdl'=2] {'seq'}, dimensions={0}, use_global_device_ids=true | all-gather | bytes 294912 | tf_op jit(solution)/shard_map/all_gather | solution.py:70
  43.3 0.1 reshape.73
  43.4 13.0 %fusion.5 = f32[32,3,2,512]{3,0,2,1:T(8,128)} fusion(bf16[3,2,512,4096]{3,2,1,0:T(8,128)(2,1)} %bitcast.68, bf16[32,4096,1,1]{1,0,2,3:T(8,128)(2,1)S(1)} %reshape.73), kind=kOutput, calls=%fused_computation.16 | convolution fusion | flops 805306368 | bytes 25821184 | tf_op jit(solution)/shard_map/dot_general | solution.py:55
  56.4 0.0 all-reduce.7.cloned.1.call-update
  56.5 0.0 copy-done
  56.5 0.8 fusion.2
  57.3 0.1 pad_maximum_fusion
  57.4 0.4 rev.3
  57.8 31.7 %tile.4 = f32[512,129,384]{0,2,1:T(8,128)} broadcast(f32[512,384]{0,1:T(8,128)S(1)} %rev.3), dimensions={0,2} | broadcast | bytes 102236160 | tf_op jit(solution)/shard_map/tile | solution.py:17
  89.6 66.7 %slice.94 = f32[512,49024]{0,1:T(8,128)} slice(f32[512,49536]{0,1:T(8,128)} %bitcast.11), slice={[0:512], [127:49151]} | slice | bytes 200802304 | tf_op jit(solution)/shard_map/slice | solution.py:18
  156.3 98.7 %reshape.77 = f32[512,128,383]{0,2,1:T(8,128)} reshape(f32[512,49024]{0,1:T(8,128)} %slice.94) | data formatting | bytes 200802304 | tf_op jit(solution)/shard_map/reshape | solution.py:19
  255.0 44.1 %slice.95 = f32[512,128,256]{0,2,1:T(8,128)} slice(f32[512,128,383]{0,2,1:T(8,128)} %reshape.77), slice={[0:512], [0:128], [0:256]} | slice | bytes 134217728 | tf_op jit(solution)/shard_map/slice | solution.py:19
  299.1 66.8 %copy.28 = f32[512,128,256]{2,1,0:T(8,128)} copy(f32[512,128,256]{0,2,1:T(8,128)} %slice.95) | data formatting | bytes 134217728
  365.9 1.5 constant_dynamic-slice_fusion.5
  367.4 0.0 copy-done.1
  367.4 0.1 dynamic_slice.7
  367.5 0.0 copy-done.2
  367.5 0.6 dynamic-slice
  368.1 0.0 all-reduce.7.cloned.1.call-done
  368.1 1.6 dynamic-slice_bitcast_fusion
  369.7 0.2 fusion.13
  370.0 0.2 copy.29
  370.2 21.0 %multiply_reduce_fusion = f32[512,128]{1,0:T(8,128)S(1)} fusion(f32[512,128,256]{2,1,0:T(8,128)} %copy.28, f32[512,256]{1,0:T(8,128)S(1)} %copy.29), kind=kLoop, calls=%fused_computation | loop fusion | flops 33488896 | bytes 67895296
  391.3 0.1 copy.17
  391.4 30.7 %all_gather.7 = bf16[32,4096]{1,0:T(8,128)(2,1)S(1)} all-gather(bf16[32,512]{1,0:T(8,128)(2,1)S(1)} %fusion.24), channel_id=1, replica_groups=mesh['grp'=2,'seq'=8,'mdl'=2] {'seq'}, dimensions={1}, use_global_device_ids=true | all-gather | bytes 294912 | tf_op jit(solution)/shard_map/all_gather | solution.py:88
  422.2 6.0 %fusion = f32[32,1024]{1,0:T(8,128)S(1)} fusion(bf16[32,4096]{1,0:T(8,128)(2,1)S(1)} %all_gather.7, bf16[1024,1,4096]{2,0,1:T(8,128)(2,1)} %param.13), kind=kOutput, calls=%fused_computation.1 | convolution fusion | flops 268435456 | bytes 8781824 | tf_op jit(solution)/shard_map/dot_general | solution.py:55
  428.1 4.4 all-reduce.8
  (13 shorter events, 0.2 us)
Async XLA Ops:
  6.5 50.0 %copy-start = (f32[512,128]{1,0:T(8,128)S(1)}, f32[512,128]{1,0:T(8,128)}, u32[]{:S(2)}) copy-start(f32[512,128]{1,0:T(8,128)} %param.11) | copy-start | bytes 786436
  6.5 361.6 %all-reduce.7.cloned.1.call-start = ((), (), s32[]{:S(2)}) async-start(), calls=%async_computation | async-start | bytes 786432
  299.0 68.4 %copy-start.1 = (f32[1024]{0:T(1024)S(1)}, f32[1024]{0:T(1024)}, u32[]{:S(2)}) copy-start(f32[1024]{0:T(1024)} %param.12) | copy-start | bytes 12292
  299.1 68.4 %copy-start.2 = (u32[32]{0:T(128)S(1)}, u32[32]{0:T(128)}, u32[]{:S(2)}) copy-start(u32[32]{0:T(128)} %constant.52) | copy-start | bytes 388
Sparse Core Ops, SparseCore 0:
  56.6 19.3 all-reduce.6
where the time goes:
time: 441 us; the launch traced here: 439 us
  local copies, waits for them, and re-layouts  313 us (71%)
  blocking collectives  70.1 us (16%)
  other arithmetic  23.1 us (5%)
  matrix products  19.8 us (4%)
  between operations  13.6 us (3%)
    reshape x1, local copies, waits for them, and re-layouts, build_toeplitz(): window.reshape(chan_width, filt_len, 3 * filt_len - 1)[:, :, :2 * filt_len]  98.7 us
    unnamed x15, local copies, waits for them, and re-layouts  67.7 us
    slice x1, local copies, waits for them, and re-layouts, build_toeplitz(): repeated[:, filt_len - 1:filt_len - 1 + filt_len * (3 * filt_len - 1)]  66.7 us
    slice x1, local copies, waits for them, and re-layouts, build_toeplitz(): window.reshape(chan_width, filt_len, 3 * filt_len - 1)[:, :, :2 * filt_len]  44.1 us
    all_gather x1, blocking collectives, per_device(): lax.all_gather(normed, 'seq', axis=0, tiled=True)  32.4 us
    another operation x1, local copies, waits for them, and re-layouts, build_toeplitz(): repeated = jnp.tile(flipped, (1, filt_len + 1))  31.7 us
    all_gather x1, blocking collectives, per_device(): lax.all_gather(own_mixed, 'seq', axis=1, tiled=True)  30.7 us
    unnamed x2, other arithmetic  21.9 us
  transfers between devices with their start and end apart: 1, of which 0 were waited for; matrix products, arithmetic and copies ran while one was open for 71% of the time, Pallas kernels for 0%

commit v1 on v0

v1 whole, which is shorter than its diff:
```python
import jax
import jax.numpy as jnp
from jax import lax
from jax.experimental import pallas as pl
from jax.experimental.pallas import tpu as pltpu
from jax.sharding import PartitionSpec as P

EPSILON = 1e-06
F32 = jnp.float32
BF16 = jnp.bfloat16
VMEM = pl.BlockSpec(memory_space=pltpu.VMEM)
ANY = pl.BlockSpec(memory_space=pl.ANY)
MIB = 1 << 20
LANES = 128
ROWS = 8


def contract_last(left, right):
    return lax.dot_general(left, right, (((1,), (1,)), ((), ())), preferred_element_type=F32)


def cost(flops, nbytes):
    return pl.CostEstimate(flops=flops, bytes_accessed=nbytes, transcendentals=0)


def params(mib):
    return pltpu.CompilerParams(vmem_limit_bytes=mib * MIB)


def swap(x, bits):
    count = lax.axis_size("seq")
    return lax.ppermute(x, "seq", [(i, i ^ bits) for i in range(count)])


def gather_pieces(x):
    pair = jnp.concatenate([x, swap(x, 1)], axis=0)
    return [pair] + [swap(pair, bits) for bits in (2, 4, 6)]


def projection_partner_kernel(a_ref, b_ref, c_ref, d_ref, gain_ref, w_ref, out_ref, xg_ref):
    tokens = xg_ref.shape[0]
    chan = w_ref.shape[1] // 2
    me = lax.axis_index("seq")
    other = 1 - lax.axis_index("mdl")
    raw = jnp.concatenate([a_ref[...], b_ref[...], c_ref[...], d_ref[...]], axis=0)
    per = tokens // lax.axis_size("seq")
    row = lax.broadcasted_iota(jnp.int32, (tokens, tokens), 0)
    col = lax.broadcasted_iota(jnp.int32, (tokens, tokens), 1)
    order = ((row // per) ^ me == col // per) & (row % per == col % per)
    select = jnp.where(order, 1.0, 0.0).astype(BF16)
    values = jnp.dot(select, raw, preferred_element_type=F32)
    squares = jnp.sum(values * values, axis=1, keepdims=True)
    xg_ref[...] = (values * gain_ref[...]).astype(BF16)
    first = pl.multiple_of(other * chan, chan)
    for branch in range(3):
        out_ref[:, branch * chan : (branch + 1) * chan] = contract_last(
            xg_ref[...], w_ref[branch, pl.ds(first, chan), :]
        )
    out_ref[:, 3 * chan :] = jnp.broadcast_to(squares, (tokens, LANES))


def projection_own_kernel(xg_ref, w_ref, out_ref):
    chan = w_ref.shape[1] // 2
    first = pl.multiple_of(lax.axis_index("mdl") * chan, chan)
    for branch in range(3):
        out_ref[:, branch * chan : (branch + 1) * chan] = contract_last(
            xg_ref[...], w_ref[branch, pl.ds(first, chan), :]
        )


def project(pieces, gain, weights, tokens):
    chan = weights.shape[1] // 2
    half = weights.shape[2]
    partner, xg = pl.pallas_call(
        projection_partner_kernel,
        out_shape=(
            jax.ShapeDtypeStruct((tokens, 3 * chan + LANES), F32),
            jax.ShapeDtypeStruct((tokens, half), BF16),
        ),
        in_specs=[VMEM] * 6,
        out_specs=(VMEM, VMEM),
        compiler_params=params(8),
        cost_estimate=cost(2 * tokens * half * 3 * chan, 2 * half * 3 * chan),
        name="project_partner",
    )(*pieces, gain, weights)
    own = pl.pallas_call(
        projection_own_kernel,
        out_shape=jax.ShapeDtypeStruct((tokens, 3 * chan), F32),
        in_specs=[VMEM] * 2,
        out_specs=VMEM,
        compiler_params=params(8),
        cost_estimate=cost(2 * tokens * half * 3 * chan, 2 * half * 3 * chan),
        name="project_own",
    )(xg, weights)
    got = lax.ppermute(partner, "mdl", [(0, 1), (1, 0)])
    return own, got, partner


def taps_kernel(taps_ref, out_ref):
    groups = taps_ref.shape[0]
    reach, chan = out_ref.shape
    per_group = chan // groups
    grp = lax.broadcasted_iota(jnp.int32, (groups, chan), 0)
    ch = lax.broadcasted_iota(jnp.int32, (groups, chan), 1)
    spread = jnp.where(ch // per_group == grp, 1.0, 0.0)
    out_ref[...] = lax.dot_general(
        taps_ref[...],
        spread,
        (((0,), (0,)), ((), ())),
        preferred_element_type=F32,
        precision=lax.Precision.HIGHEST,
    )[:reach]


def delay(x, rows):
    if rows == 0:
        return x
    index = lax.broadcasted_iota(jnp.int32, x.shape, 0)
    return jnp.where(index >= rows, pltpu.roll(x, rows, axis=0), 0.0)


def mix_kernel(width, own_ref, got_ref, sent_ref, short_ref, bias_ref, taps_ref, out_ref):
    tokens, chan = out_ref.shape
    reach = taps_ref.shape[0]
    first = pl.multiple_of(lax.axis_index("mdl") * chan, chan)
    squares = sent_ref[:, 3 * chan : 3 * chan + 1] + got_ref[:, 3 * chan : 3 * chan + 1]
    scale = lax.rsqrt(squares / width + EPSILON)
    feats = []
    for branch in range(3):
        cut = slice(branch * chan, (branch + 1) * chan)
        total = (own_ref[:, cut] + got_ref[:, cut]) * scale
        feat = None
        for offset in range(short_ref.shape[0]):
            term = short_ref[offset, pl.ds(branch, 1), pl.ds(first, chan)] * delay(total, offset)
            feat = term if feat is None else feat + term
        feats.append(feat)
    gated = feats[1] * feats[2]
    mixed = bias_ref[:, pl.ds(first, chan)] * gated
    blocks = [mixed[b * ROWS : (b + 1) * ROWS] for b in range(tokens // ROWS)]
    for shift in range(ROWS):
        moved = delay(gated, shift)
        for lag in range(reach // ROWS):
            tap = taps_ref[pl.ds(lag * ROWS + shift, 1), :]
            for b in range(lag, tokens // ROWS):
                blocks[b] = blocks[b] + tap * moved[(b - lag) * ROWS : (b - lag + 1) * ROWS]
    out_ref[...] = (feats[0] * jnp.concatenate(blocks, axis=0)).astype(BF16)


def spread_taps(long_taps, first_channel, chan, width, tokens):
    group_width = width // long_taps.shape[0]
    groups = chan // group_width
    local = lax.dynamic_slice_in_dim(long_taps, first_channel // group_width, groups, 0)
    reach = min(tokens, long_taps.shape[1])
    return pl.pallas_call(
        taps_kernel,
        out_shape=jax.ShapeDtypeStruct((reach, chan), F32),
        in_specs=[VMEM],
        out_specs=VMEM,
        compiler_params=params(4),
        name="spread_taps",
    )(local)


def mix(own, got, sent, short_taps, bias, taps, width):
    tokens, chan = own.shape[0], own.shape[1] // 3
    return pl.pallas_call(
        lambda *refs: mix_kernel(width, *refs),
        out_shape=jax.ShapeDtypeStruct((tokens, chan), BF16),
        in_specs=[VMEM] * 6,
        out_specs=VMEM,
        compiler_params=params(8),
        name="mix",
    )(own, got, sent, short_taps, bias, taps)


def out_kernel(a_ref, b_ref, c_ref, d_ref, w_ref, out_ref):
    tokens = out_ref.shape[0]
    chan = a_ref.shape[1]
    me = lax.axis_index("seq")
    total = None
    for place, ref in enumerate((a_ref, b_ref, c_ref, d_ref)):
        for low in range(2):
            owner = me ^ (2 * place + low)
            cut = pl.ds(pl.multiple_of(owner * chan, chan), chan)
            term = contract_last(ref[low * tokens : (low + 1) * tokens, :], w_ref[:, cut])
            total = term if total is None else total + term
    out_ref[...] = total


def project_out(pieces, weights, tokens):
    return pl.pallas_call(
        out_kernel,
        out_shape=jax.ShapeDtypeStruct((tokens, weights.shape[0]), F32),
        in_specs=[VMEM] * 5,
        out_specs=VMEM,
        compiler_params=params(8),
        cost_estimate=cost(2 * tokens * weights.size, 2 * weights.size),
        name="project_out",
    )(*pieces, weights)


def per_device(tokens_in, norm_gain, in_proj, short_taps, long_taps, skip_bias, out_proj):
    own_tokens, half = tokens_in.shape
    width = 2 * half
    tokens = own_tokens * lax.axis_size("seq")
    chan = in_proj.shape[2] // 2
    weights_in = in_proj.reshape(3, 2 * chan, half)
    weights_out = out_proj.reshape(out_proj.shape[0], -1)
    first_channel = lax.axis_index("seq") * 2 * chan + lax.axis_index("mdl") * chan
    taps = spread_taps(long_taps, first_channel, chan, width, tokens)
    pieces = gather_pieces(tokens_in)
    own, got, sent = project(pieces, norm_gain[None, :], weights_in, tokens)
    gated = mix(own, got, sent, short_taps, skip_bias[None, :], taps, width)
    partial_out = project_out(gather_pieces(gated), weights_out, tokens)
    other = lax.ppermute(partial_out, "mdl", [(0, 1), (1, 0)])
    return (partial_out + other).astype(BF16)


def per_device_any(tokens_in, norm_gain, in_proj, short_taps, long_taps, skip_bias, out_proj):
    half = tokens_in.shape[1]
    width = 2 * half
    chan = in_proj.shape[2] // 2
    seq_index = lax.axis_index("seq")
    mdl_index = lax.axis_index("mdl")
    values = tokens_in.astype(F32)
    squares = lax.psum(jnp.sum(values * values, axis=1), "mdl")
    scale = lax.rsqrt(squares / width + EPSILON)
    normed = (values * scale[:, None] * norm_gain[None, :]).astype(BF16)
    part = contract_last(
        lax.all_gather(normed, "seq", axis=0, tiled=True), in_proj.reshape(-1, half)
    )
    tokens = part.shape[0]
    part = part.reshape(tokens, 3, 2, chan)
    summed = lax.psum_scatter(part, "mdl", scatter_dimension=2, tiled=True)
    summed = summed.reshape(tokens, 3, chan)
    short_local = lax.dynamic_slice_in_dim(short_taps, mdl_index * chan, chan, 2)
    bias_local = lax.dynamic_slice_in_dim(skip_bias, mdl_index * chan, chan, 0)
    short_count = short_local.shape[0]
    padded = jnp.pad(summed, ((short_count - 1, 0), (0, 0), (0, 0)))
    features = sum(
        short_local[i][None] * padded[short_count - 1 - i : short_count - 1 - i + tokens]
        for i in range(short_count)
    )
    gated = features[:, 1, :] * features[:, 2, :]
    group_width = width // long_taps.shape[0]
    groups = (seq_index * 2 * chan + mdl_index * chan + jnp.arange(chan)) // group_width
    taps = long_taps[groups].T
    reach = min(tokens, taps.shape[0])
    shifted = jnp.pad(gated, ((reach - 1, 0), (0, 0)))
    mixed = bias_local[None, :] * gated + sum(
        taps[i][None, :] * shifted[reach - 1 - i : reach - 1 - i + tokens] for i in range(reach)
    )
    gated_out = (features[:, 0, :] * mixed).astype(BF16)
    rows = out_proj.reshape(out_proj.shape[0], -1)
    folded = contract_last(lax.all_gather(gated_out, "seq", axis=1, tiled=True), rows)
    return lax.psum(folded, "mdl").astype(BF16)


def solution(mesh):
    seq = mesh.shape["seq"]
    in_specs = (
        P(("grp", "seq"), "mdl"),
        P("mdl"),
        P("seq", None, None, "mdl"),
        P(None, None, "seq"),
        P(),
        P("seq"),
        P("seq", "mdl", None),
    )
    body = per_device if seq == 8 and mesh.shape["mdl"] == 2 else per_device_any
    return jax.shard_map(
        body, mesh=mesh, in_specs=in_specs, out_specs=P("grp", "seq"), check_vma=False
    )
```

time: 441 us -> 62.5 us (0.14)
  local copies, waits for them, and re-layouts: 313 us -> 20.5 us
  blocking collectives: 70.1 us -> 0 us
  other arithmetic: 23.1 us -> 1.44 us
  matrix products: 19.8 us -> 0 us
  waiting for transfers between devices: 0.04 us -> 15.4 us
  starting transfers between devices: 0.01 us -> 13.7 us
  between operations: 13.6 us -> 0.14 us
  Pallas kernels: 0 us -> 11 us
    slice x4 -> x0, local copies, waits for them, and re-layouts: 112 us -> none  [the longest x1 66.7 us: build_toeplitz(): repeated[:, filt_len - 1:filt_len - 1 + filt_len * (3 * filt_len - 1)]]
    reshape x2 -> x0, local copies, waits for them, and re-layouts: 100 us -> none  [the longest x1 98.7 us: build_toeplitz(): window.reshape(chan_width, filt_len, 3 * filt_len - 1)[:, :, :2 * filt_len]]
    all_gather x2 -> x0, blocking collectives: 63.2 us -> none  [the longest x1 32.4 us: per_device(): lax.all_gather(normed, 'seq', axis=0, tiled=True)]
    unnamed x15, local copies, waits for them, and re-layouts: 67.7 us -> 20.5 us
    another operation x1 -> x0, local copies, waits for them, and re-layouts: 31.7 us -> none  [build_toeplitz(): repeated = jnp.tile(flipped, (1, filt_len + 1))]
    unnamed x2 -> x0, other arithmetic: 21.9 us -> none
    dot_general x3 -> x0, matrix products: 19.8 us -> none  [the longest x2 19 us: contract_last(): lax.dot_general(left, right, (((1,), (1,)), ((), ())), preferred_element_...]
    ppermute x0 -> x10, waiting for transfers between devices: none -> 15.4 us  [the longest x8 14 us: swap(): return lax.ppermute(x, 'seq', [(i, i ^ bits) for i in range(count)])]
  transfers between devices with their start and end apart: 1 -> 10, of which waited for: 0 -> 7; matrix products, arithmetic and copies ran while one was open for 71% -> 0% of each run, Pallas kernels for 0% -> 7%
where the time goes in v1:
time: 62.5 us; the launch traced here: 62.1 us
  local copies, waits for them, and re-layouts  20.5 us (33%)
  waiting for transfers between devices  15.4 us (25%)
  starting transfers between devices  13.7 us (22%)
  Pallas kernels  11 us (18%)
  other arithmetic  1.44 us (2%)
    unnamed x15, local copies, waits for them, and re-layouts  20.5 us
    ppermute x8, waiting for transfers between devices, swap(): return lax.ppermute(x, 'seq', [(i, i ^ bits) for i in range(count)])  14 us
    ppermute x8, starting transfers between devices, swap(): return lax.ppermute(x, 'seq', [(i, i ^ bits) for i in range(count)])  13.6 us
    pallas_call x1, Pallas kernels, project(): pl.pallas_call(projection_partner_kernel, out_shape=(jax.ShapeDtypeStruct...  3.88 us
    pallas_call x1, Pallas kernels, project(): pl.pallas_call(projection_own_kernel, out_shape=jax.ShapeDtypeStruct((tok...  3.8 us
    pallas_call x1, Pallas kernels, project_out(): pl.pallas_call(out_kernel, out_shape=jax.ShapeDtypeStruct((tokens, weight...  2.53 us
    ppermute x1, waiting for transfers between devices, per_device(): other = lax.ppermute(partial_out, 'mdl', [(0, 1), (1, 0)])  1.34 us
  transfers between devices with their start and end apart: 10, of which 7 were waited for; matrix products, arithmetic and copies ran while one was open for 0% of the time, Pallas kernels for 7%

profile of v1, /device:TPU:0, one launch (start us, length us, event | category | flops | bytes accessed | tf_op | source)
XLA Modules:
  0.0 62.1 jit_solution(9527286856342929359)
XLA Ops:
  0.0 2.9 %collective-permute-start = (bf16[4,4096]{1,0:T(4,128)(2,1)}, bf16[4,4096]{1,0:T(4,128)(2,1)S(1)}, u32[]{:S(2)}, u32[]{:S(2)}) collective-permute-start(bf16[4,4096]{1,0:T(4,128)(2,1)} %param.7), channel_id=1, source_target_pairs={{0,2},{2,0},{4,6},{6,4},{8,10},{10,8},{12,14},{14,12},{1,3},{3,1},... | collective-permute-start | bytes 98312 | tf_op jit(solution)/shard_map/ppermute | solution.py:32
  2.9 2.1 %collective-permute-done = bf16[4,4096]{1,0:T(4,128)(2,1)S(1)} collective-permute-done((bf16[4,4096]{1,0:T(4,128)(2,1)}, bf16[4,4096]{1,0:T(4,128)(2,1)S(1)}, u32[]{:S(2)}, u32[]{:S(2)}) %collective-permute-start) | collective-permute-done | bytes 32800 | tf_op jit(solution)/shard_map/ppermute | solution.py:32
  5.0 0.8 %pad_maximum_fusion.a_ref = bf16[8,4096]{1,0:T(8,128)(2,1)S(1)} fusion(bf16[4,4096]{1,0:T(4,128)(2,1)S(1)} %collective-permute-done, bf16[4,4096]{1,0:T(4,128)(2,1)} %param.7), kind=kLoop, calls=%fused_computation.1 | loop fusion | flops 131072 | bytes 131072 | tf_op jit(solution)/shard_map/concatenate | solution.py:36
  5.8 2.2 %collective-permute-start.1 = (bf16[8,4096]{1,0:T(8,128)(2,1)S(1)}, bf16[8,4096]{1,0:T(8,128)(2,1)S(1)}, u32[]{:S(2)}, u32[]{:S(2)}) collective-permute-start(bf16[8,4096]{1,0:T(8,128)(2,1)S(1)} %pad_maximum_fusion.a_ref), channel_id=1, source_target_pairs={{0,4},{2,6},{4,0},{6,2},{8,12},{10,14},{12,8},{14,10},{1,5},{3,7},... | collective-permute-start | bytes 196616 | tf_op jit(solution)/shard_map/ppermute | solution.py:32
  8.0 2.6 %collective-permute-start.2 = (bf16[8,4096]{1,0:T(8,128)(2,1)S(1)}, bf16[8,4096]{1,0:T(8,128)(2,1)S(1)}, u32[]{:S(2)}, u32[]{:S(2)}) collective-permute-start(bf16[8,4096]{1,0:T(8,128)(2,1)S(1)} %pad_maximum_fusion.a_ref), channel_id=1, source_target_pairs={{0,8},{2,10},{4,12},{6,14},{8,0},{10,2},{12,4},{14,6},{1,9},{3,11}... | collective-permute-start | bytes 196616 | tf_op jit(solution)/shard_map/ppermute | solution.py:32
  10.6 0.0 collective-permute-start.3
  10.6 0.3 collective-permute-done.1.b_ref
  10.9 3.7 %collective-permute-done.2.c_ref = bf16[8,4096]{1,0:T(8,128)(2,1)S(1)} collective-permute-done((bf16[8,4096]{1,0:T(8,128)(2,1)S(1)}, bf16[8,4096]{1,0:T(8,128)(2,1)S(1)}, u32[]{:S(2)}, u32[]{:S(2)}) %collective-permute-start.2) | collective-permute-done | bytes 65568 | tf_op jit(solution)/shard_map/ppermute | solution.py:32
  14.6 2.1 %collective-permute-done.3.d_ref = bf16[8,4096]{1,0:T(8,128)(2,1)S(1)} collective-permute-done((bf16[8,4096]{1,0:T(8,128)(2,1)S(1)}, bf16[8,4096]{1,0:T(8,128)(2,1)S(1)}, u32[]{:S(2)}, u32[]{:S(2)}) %collective-permute-start.3) | collective-permute-done | bytes 65568 | tf_op jit(solution)/shard_map/ppermute | solution.py:32
  16.7 8.2 %copy-done.1 = bf16[1,3,1024,4096]{3,2,1,0:T(8,128)(2,1)S(1)} copy-done((bf16[1,3,1024,4096]{3,2,1,0:T(8,128)(2,1)S(1)}, bf16[1,3,1024,4096]{3,2,1,0:T(8,128)(2,1)}, u32[]{:S(2)}) %copy-start.1) | copy-done | bytes 25165848
  24.8 0.7 %copy-done.4 = f32[4096]{0:T(1024)S(1)} copy-done((f32[4096]{0:T(1024)S(1)}, f32[4096]{0:T(1024)}, u32[]{:S(2)}) %copy-start.4) | copy-done | bytes 16408
  25.5 3.9 %project_partner.1 = (f32[32,1664]{1,0:T(8,128)S(1)}, bf16[32,4096]{1,0:T(8,128)(2,1)S(1)}) custom-call(bf16[8,4096]{1,0:T(8,128)(2,1)S(1)} %pad_maximum_fusion.a_ref, bf16[8,4096]{1,0:T(8,128)(2,1)S(1)} %collective-permute-done.1.b_ref, bf16[8,4096]{1,0:T(8,128)(2,1)S(1)} %collective-permute-done.2.c_ref, bf16[8,4096]{1,0:T(8,128)(2,1)S(1)} %collective-permute-done.3.d_ref, ...), custom_call_target="tpu_custom_call" | custom-call | flops 402653184 | bytes 12582912 | tf_op jit(solution)/shard_map/project_partner/pallas_call | solution.py:74
  29.4 0.0 collective-permute-start.4
  29.5 0.1 copy.8.refs_3_
  29.6 0.4 spread_taps.1.refs_5_
  30.0 0.0 copy-start.2
  30.0 8.2 %copy-done.2 = bf16[1,3,1024,4096]{3,2,1,0:T(8,128)(2,1)S(1)} copy-done((bf16[1,3,1024,4096]{3,2,1,0:T(8,128)(2,1)S(1)}, bf16[1,3,1024,4096]{3,2,1,0:T(8,128)(2,1)}, u32[]{:S(2)}) %copy-start.2) | copy-done | bytes 25165848
  38.2 3.8 %project_own.1.refs_0_ = f32[32,1536]{1,0:T(8,128)S(1)} custom-call(bf16[32,4096]{1,0:T(8,128)(2,1)S(1)} %get-tuple-element.7.xg_ref, bf16[3,1024,4096]{2,1,0:T(8,128)(2,1)S(1)} %bitcast.5), custom_call_target="tpu_custom_call" | custom-call | flops 402653184 | bytes 12582912 | tf_op jit(solution)/shard_map/project_own/pallas_call | solution.py:86
  42.0 0.0 collective-permute-done.4.refs_1_
  42.0 0.4 mix.1
  42.4 1.6 %collective-permute-start.5 = (bf16[32,512]{1,0:T(8,128)(2,1)S(1)}, bf16[32,512]{1,0:T(8,128)(2,1)S(1)}, u32[]{:S(2)}, u32[]{:S(2)}) collective-permute-start(bf16[32,512]{1,0:T(8,128)(2,1)S(1)} %mix.1), channel_id=1, source_target_pairs={{0,2},{2,0},{4,6},{6,4},{8,10},{10,8},{12,14},{14,12},{1,3},{3,1},... | collective-permute-start | bytes 98312 | tf_op jit(solution)/shard_map/ppermute | solution.py:32
  44.0 2.4 %collective-permute-done.5 = bf16[32,512]{1,0:T(8,128)(2,1)S(1)} collective-permute-done((bf16[32,512]{1,0:T(8,128)(2,1)S(1)}, bf16[32,512]{1,0:T(8,128)(2,1)S(1)}, u32[]{:S(2)}, u32[]{:S(2)}) %collective-permute-start.5) | collective-permute-done | bytes 32800 | tf_op jit(solution)/shard_map/ppermute | solution.py:32
  46.4 0.0 collective-permute-start.6
  46.4 1.5 %collective-permute-start.7 = (bf16[64,512]{1,0:T(8,128)(2,1)S(1)}, bf16[64,512]{1,0:T(8,128)(2,1)S(1)}, u32[]{:S(2)}, u32[]{:S(2)}) collective-permute-start(bf16[64,512]{1,0:T(8,128)(2,1)S(1)} %pad_maximum_fusion.1.a_ref), channel_id=1, source_target_pairs={{0,8},{2,10},{4,12},{6,14},{8,0},{10,2},{12,4},{14,6},{1,9},{3,11}... | collective-permute-start | bytes 196616 | tf_op jit(solution)/shard_map/ppermute | solution.py:32
  47.9 2.9 %collective-permute-start.8 = (bf16[64,512]{1,0:T(8,128)(2,1)S(1)}, bf16[64,512]{1,0:T(8,128)(2,1)S(1)}, u32[]{:S(2)}, u32[]{:S(2)}) collective-permute-start(bf16[64,512]{1,0:T(8,128)(2,1)S(1)} %pad_maximum_fusion.1.a_ref), channel_id=1, source_target_pairs={{0,12},{2,14},{4,8},{6,10},{8,4},{10,6},{12,0},{14,2},{1,13},{3,15... | collective-permute-start | bytes 196616 | tf_op jit(solution)/shard_map/ppermute | solution.py:32
  50.8 0.0 collective-permute-done.6.b_ref
  50.8 3.4 %collective-permute-done.7.c_ref = bf16[64,512]{1,0:T(8,128)(2,1)S(1)} collective-permute-done((bf16[64,512]{1,0:T(8,128)(2,1)S(1)}, bf16[64,512]{1,0:T(8,128)(2,1)S(1)}, u32[]{:S(2)}, u32[]{:S(2)}) %collective-permute-start.7) | collective-permute-done | bytes 65568 | tf_op jit(solution)/shard_map/ppermute | solution.py:32
  54.2 3.4 %copy-done.3 = bf16[1024,1,4096]{2,0,1:T(8,128)(2,1)S(1)} copy-done((bf16[1024,1,4096]{2,0,1:T(8,128)(2,1)S(1)}, bf16[1024,1,4096]{2,0,1:T(8,128)(2,1)}, u32[]{:S(2)}) %copy-start.3) | copy-done | bytes 8388632
  57.6 2.5 %project_out.1 = f32[32,1024]{1,0:T(8,128)S(1)} custom-call(bf16[64,512]{1,0:T(8,128)(2,1)S(1)} %pad_maximum_fusion.1.a_ref, bf16[64,512]{1,0:T(8,128)(2,1)S(1)} %collective-permute-done.6.b_ref, bf16[64,512]{1,0:T(8,128)(2,1)S(1)} %collective-permute-done.7.c_ref, bf16[64,512]{1,0:T(8,128)(2,1)S(1)} %collective-permute-done.8.d_ref, ...), custom_call_target="tpu_custom_call" | custom-call | flops 268435456 | bytes 8388608 | tf_op jit(solution)/shard_map/project_out/pallas_call | solution.py:191
  60.1 0.0 collective-permute-start.9
  60.1 1.3 %collective-permute-done.9 = f32[32,1024]{1,0:T(8,128)S(1)} collective-permute-done((f32[32,1024]{1,0:T(8,128)S(1)}, f32[32,1024]{1,0:T(8,128)S(1)}, u32[]{:S(2)}, u32[]{:S(2)}) %collective-permute-start.9) | collective-permute-done | bytes 131104 | tf_op jit(solution)/shard_map/ppermute | solution.py:215
  61.5 0.6 %add_convert_fusion = bf16[32,1024]{1,0:T(8,128)(2,1)} fusion(f32[32,1024]{1,0:T(8,128)S(1)} %project_out.1, f32[32,1024]{1,0:T(8,128)S(1)} %collective-permute-done.9), kind=kLoop, calls=%fused_computation | loop fusion | flops 65536 | bytes 327680 | tf_op jit(solution)/shard_map/convert_element_type | solution.py:216
  (12 shorter events, 0.0 us)
Async XLA Ops:
  0.0 29.6 %copy-start = (f32[512,128]{1,0:T(8,128)S(1)}, f32[512,128]{1,0:T(8,128)}, u32[]{:S(2)}) copy-start(f32[512,128]{1,0:T(8,128)} %param.11) | copy-start | bytes 786436
  0.0 29.5 %copy-start.6 = (f32[7,3,1024]{2,0,1:T(8,128)S(1)}, f32[7,3,1024]{2,0,1:T(8,128)}, u32[]{:S(2)}) copy-start(f32[7,3,1024]{2,0,1:T(8,128)} %param.10) | copy-start | bytes 258052
  0.0 5.0 %collective-permute-start = (bf16[4,4096]{1,0:T(4,128)(2,1)}, bf16[4,4096]{1,0:T(4,128)(2,1)S(1)}, u32[]{:S(2)}, u32[]{:S(2)}) collective-permute-start(bf16[4,4096]{1,0:T(4,128)(2,1)} %param.7), channel_id=1, source_target_pairs={{0,2},{2,0},{4,6},{6,4},{8,10},{10,8},{12,14},{14,12},{1,3},{3,1},... | collective-permute-start | bytes 98312 | tf_op jit(solution)/shard_map/ppermute | solution.py:32
  5.8 5.0 %collective-permute-start.1 = (bf16[8,4096]{1,0:T(8,128)(2,1)S(1)}, bf16[8,4096]{1,0:T(8,128)(2,1)S(1)}, u32[]{:S(2)}, u32[]{:S(2)}) collective-permute-start(bf16[8,4096]{1,0:T(8,128)(2,1)S(1)} %pad_maximum_fusion.a_ref), channel_id=1, source_target_pairs={{0,4},{2,6},{4,0},{6,2},{8,12},{10,14},{12,8},{14,10},{1,5},{3,7},... | collective-permute-start | bytes 196616 | tf_op jit(solution)/shard_map/ppermute | solution.py:32
  8.0 6.6 %collective-permute-start.2 = (bf16[8,4096]{1,0:T(8,128)(2,1)S(1)}, bf16[8,4096]{1,0:T(8,128)(2,1)S(1)}, u32[]{:S(2)}, u32[]{:S(2)}) collective-permute-start(bf16[8,4096]{1,0:T(8,128)(2,1)S(1)} %pad_maximum_fusion.a_ref), channel_id=1, source_target_pairs={{0,8},{2,10},{4,12},{6,14},{8,0},{10,2},{12,4},{14,6},{1,9},{3,11}... | collective-permute-start | bytes 196616 | tf_op jit(solution)/shard_map/ppermute | solution.py:32
  10.6 6.1 %collective-permute-start.3 = (bf16[8,4096]{1,0:T(8,128)(2,1)S(1)}, bf16[8,4096]{1,0:T(8,128)(2,1)S(1)}, u32[]{:S(2)}, u32[]{:S(2)}) collective-permute-start(bf16[8,4096]{1,0:T(8,128)(2,1)S(1)} %pad_maximum_fusion.a_ref), channel_id=1, source_target_pairs={{0,12},{2,14},{4,8},{6,10},{8,4},{10,6},{12,0},{14,2},{1,13},{3,15... | collective-permute-start | bytes 196616 | tf_op jit(solution)/shard_map/ppermute | solution.py:32
  16.7 8.2 %copy-start.1 = (bf16[1,3,1024,4096]{3,2,1,0:T(8,128)(2,1)S(1)}, bf16[1,3,1024,4096]{3,2,1,0:T(8,128)(2,1)}, u32[]{:S(2)}) copy-start(bf16[1,3,1024,4096]{3,2,1,0:T(8,128)(2,1)} %param.9) | copy-start | bytes 75497472
  24.8 0.7 %copy-start.4 = (f32[4096]{0:T(1024)S(1)}, f32[4096]{0:T(1024)}, u32[]{:S(2)}) copy-start(f32[4096]{0:T(1024)} %param.8) | copy-start | bytes 49156
  25.5 16.4 %copy-start.5 = (f32[1024]{0:T(1024)S(1)}, f32[1024]{0:T(1024)}, u32[]{:S(2)}) copy-start(f32[1024]{0:T(1024)} %param.12) | copy-start | bytes 12292
  29.4 12.5 %collective-permute-start.4 = (f32[32,1664]{1,0:T(8,128)S(1)}, f32[32,1664]{1,0:T(8,128)S(1)}, u32[]{:S(2)}, u32[]{:S(2)}) collective-permute-start(f32[32,1664]{1,0:T(8,128)S(1)} %get-tuple-element.8.refs_2_), channel_id=1, source_target_pairs={{0,1},{1,0},{2,3},{3,2},{4,5},{5,4},{6,7},{7,6},{8,9},{9,8},{10,11... | collective-permute-start | bytes 638984 | tf_op jit(solution)/shard_map/ppermute | solution.py:95
  30.0 8.2 %copy-start.2 = (bf16[1,3,1024,4096]{3,2,1,0:T(8,128)(2,1)S(1)}, bf16[1,3,1024,4096]{3,2,1,0:T(8,128)(2,1)}, u32[]{:S(2)}) copy-start(bf16[1,3,1024,4096]{3,2,1,0:T(8,128)(2,1)} %param.9) | copy-start | bytes 75497472
  42.4 4.0 %collective-permute-start.5 = (bf16[32,512]{1,0:T(8,128)(2,1)S(1)}, bf16[32,512]{1,0:T(8,128)(2,1)S(1)}, u32[]{:S(2)}, u32[]{:S(2)}) collective-permute-start(bf16[32,512]{1,0:T(8,128)(2,1)S(1)} %mix.1), channel_id=1, source_target_pairs={{0,2},{2,0},{4,6},{6,4},{8,10},{10,8},{12,14},{14,12},{1,3},{3,1},... | collective-permute-start | bytes 98312 | tf_op jit(solution)/shard_map/ppermute | solution.py:32
  46.4 4.4 %collective-permute-start.6 = (bf16[64,512]{1,0:T(8,128)(2,1)S(1)}, bf16[64,512]{1,0:T(8,128)(2,1)S(1)}, u32[]{:S(2)}, u32[]{:S(2)}) collective-permute-start(bf16[64,512]{1,0:T(8,128)(2,1)S(1)} %pad_maximum_fusion.1.a_ref), channel_id=1, source_target_pairs={{0,4},{2,6},{4,0},{6,2},{8,12},{10,14},{12,8},{14,10},{1,5},{3,7},... | collective-permute-start | bytes 196616 | tf_op jit(solution)/shard_map/ppermute | solution.py:32
  46.4 7.8 %collective-permute-start.7 = (bf16[64,512]{1,0:T(8,128)(2,1)S(1)}, bf16[64,512]{1,0:T(8,128)(2,1)S(1)}, u32[]{:S(2)}, u32[]{:S(2)}) collective-permute-start(bf16[64,512]{1,0:T(8,128)(2,1)S(1)} %pad_maximum_fusion.1.a_ref), channel_id=1, source_target_pairs={{0,8},{2,10},{4,12},{6,14},{8,0},{10,2},{12,4},{14,6},{1,9},{3,11}... | collective-permute-start | bytes 196616 | tf_op jit(solution)/shard_map/ppermute | solution.py:32
  47.9 6.3 %collective-permute-start.8 = (bf16[64,512]{1,0:T(8,128)(2,1)S(1)}, bf16[64,512]{1,0:T(8,128)(2,1)S(1)}, u32[]{:S(2)}, u32[]{:S(2)}) collective-permute-start(bf16[64,512]{1,0:T(8,128)(2,1)S(1)} %pad_maximum_fusion.1.a_ref), channel_id=1, source_target_pairs={{0,12},{2,14},{4,8},{6,10},{8,4},{10,6},{12,0},{14,2},{1,13},{3,15... | collective-permute-start | bytes 196616 | tf_op jit(solution)/shard_map/ppermute | solution.py:32
  54.2 3.4 %copy-start.3 = (bf16[1024,1,4096]{2,0,1:T(8,128)(2,1)S(1)}, bf16[1024,1,4096]{2,0,1:T(8,128)(2,1)}, u32[]{:S(2)}) copy-start(bf16[1024,1,4096]{2,0,1:T(8,128)(2,1)} %param.13) | copy-start | bytes 25165828
  60.1 1.4 %collective-permute-start.9 = (f32[32,1024]{1,0:T(8,128)S(1)}, f32[32,1024]{1,0:T(8,128)S(1)}, u32[]{:S(2)}, u32[]{:S(2)}) collective-permute-start(f32[32,1024]{1,0:T(8,128)S(1)} %project_out.1), channel_id=1, source_target_pairs={{0,1},{1,0},{2,3},{3,2},{4,5},{5,4},{6,7},{7,6},{8,9},{9,8},{10,11... | collective-permute-start | bytes 393224 | tf_op jit(solution)/shard_map/ppermute | solution.py:215

commit v2 on v1

v2 whole, which is shorter than its diff:
```python
import jax
import jax.numpy as jnp
from jax import lax
from jax.experimental import pallas as pl
from jax.experimental.pallas import tpu as pltpu
from jax.sharding import PartitionSpec as P

EPSILON = 1e-06
F32 = jnp.float32
BF16 = jnp.bfloat16
VMEM = pl.BlockSpec(memory_space=pltpu.VMEM)
ANY = pl.BlockSpec(memory_space=pl.ANY)
MIB = 1 << 20
LANES = 128
ROWS = 8


def contract_last(left, right):
    return lax.dot_general(left, right, (((1,), (1,)), ((), ())), preferred_element_type=F32)


def cost(flops, nbytes):
    return pl.CostEstimate(flops=flops, bytes_accessed=nbytes, transcendentals=0)


def params(mib):
    return pltpu.CompilerParams(vmem_limit_bytes=mib * MIB)


def swap(x, bits):
    count = lax.axis_size("seq")
    return lax.ppermute(x, "seq", [(i, i ^ bits) for i in range(count)])


def stack_kernel(*refs):
    parts = [ref[...].astype(F32) for ref in refs[:-1]]
    refs[-1][...] = jnp.concatenate(parts, axis=0).astype(refs[-1].dtype)


def stack(*parts):
    rows = sum(part.shape[0] for part in parts)
    return pl.pallas_call(
        stack_kernel,
        out_shape=jax.ShapeDtypeStruct((rows,) + parts[0].shape[1:], parts[0].dtype),
        in_specs=[VMEM] * len(parts),
        out_specs=VMEM,
        compiler_params=params(4),
        name="stack",
    )(*parts)


ORDER = (0, 1, 2, 3, 4, 5, 6, 7)


def gather_pieces(x, local):
    pair = stack(local, swap(x, 1))
    return [pair] + [swap(pair, bits) for bits in (2, 4, 6)]


def in_vmem(x):
    return pltpu.with_memory_space_constraint(x, pltpu.VMEM)


def in_hbm(x):
    return pltpu.with_memory_space_constraint(x, pltpu.HBM)


def rows_of(which, chan):
    mine = lax.axis_index("mdl")
    return pl.multiple_of((mine if which == "own" else 1 - mine) * chan, chan)


CUTS = 2
PRE = 1
MORE = 4
NEXT = 4


def chunk_copies(which, w_ref, out_ref, sems, first, count):
    rows = out_ref.shape[1]
    start = rows_of(which, rows * CUTS)
    return [
        pltpu.make_async_copy(
            w_ref.at[i // CUTS, pl.ds(start + i % CUTS * rows, rows)],
            out_ref.at[i - first],
            sems.at[i - first],
        )
        for i in range(first, first + count)
    ]


def start_all(copies):
    for copy in copies:
        copy.start()


def wait_all(copies):
    for copy in copies:
        copy.wait()


def prepare_kernel(x_ref, w_ref, taps_ref, local_ref, chunks_ref, spread_ref, group_taps, sems, small):
    chan = spread_ref.shape[1]
    groups = group_taps.shape[0]
    index = lax.axis_index("seq") * 2 + lax.axis_index("mdl")
    near = pl.ds(pl.multiple_of(index * groups, groups), groups)
    fetch = pltpu.make_async_copy(taps_ref.at[near], group_taps, small.at[0])
    move = pltpu.make_async_copy(x_ref, local_ref, small.at[1])
    copies = chunk_copies("partner", w_ref, chunks_ref, sems, 0, PRE)
    start_all([fetch, move] + copies)
    fetch.wait()
    grp = lax.broadcasted_iota(jnp.int32, (groups, chan), 0)
    ch = lax.broadcasted_iota(jnp.int32, (groups, chan), 1)
    spread = jnp.where(ch // (chan // groups) == grp, 1.0, 0.0)
    spread_ref[...] = lax.dot_general(
        group_taps[...],
        spread,
        (((0,), (0,)), ((), ())),
        preferred_element_type=F32,
        precision=lax.Precision.HIGHEST,
    )[: spread_ref.shape[0]]
    wait_all([move] + copies)


def prepare(x, weights, long_taps, tokens):
    chan, half = weights.shape[1] // 2, weights.shape[2]
    reach = min(tokens, long_taps.shape[1])
    groups = long_taps.shape[0] * chan // (2 * half)
    return pl.pallas_call(
        prepare_kernel,
        out_shape=(
            jax.ShapeDtypeStruct(x.shape, x.dtype),
            pltpu.VMEM((PRE, chan // CUTS, half), weights.dtype),
            jax.ShapeDtypeStruct((reach, chan), F32),
        ),
        in_specs=[ANY] * 3,
        out_specs=(VMEM,) * 3,
        scratch_shapes=[
            pltpu.VMEM((groups, long_taps.shape[1]), F32),
            pltpu.SemaphoreType.DMA((PRE,)),
            pltpu.SemaphoreType.DMA((2,)),
        ],
        compiler_params=params(4),
        cost_estimate=cost(0, 4 * PRE * chan // CUTS * half),
        name="prepare",
    )(in_hbm(x), weights, in_hbm(long_taps))


def load_kernel(w_ref, after_ref, out_ref, sems):
    copies = chunk_copies("partner", w_ref, out_ref, sems, PRE, MORE)
    start_all(copies)
    wait_all(copies)


def load_more(weights, after):
    rows, half = weights.shape[1] // 2 // CUTS, weights.shape[2]
    return pl.pallas_call(
        load_kernel,
        out_shape=pltpu.VMEM((MORE, rows, half), weights.dtype),
        in_specs=[ANY, ANY],
        out_specs=VMEM,
        scratch_shapes=[pltpu.SemaphoreType.DMA((MORE,))],
        compiler_params=params(4),
        cost_estimate=cost(0, 4 * MORE * rows * half),
        name="load_more",
    )(weights, after)


def ordered(pieces, order, tokens):
    raw = jnp.concatenate([piece[...].astype(F32) for piece in pieces], axis=0).astype(BF16)
    me = lax.axis_index("seq")
    per = tokens // len(order)
    row = lax.broadcasted_iota(jnp.int32, (tokens, tokens), 0)
    col = lax.broadcasted_iota(jnp.int32, (tokens, tokens), 1)
    place = col // per
    bits = jnp.zeros_like(place)
    for k, value in enumerate(order):
        bits = jnp.where(place == k, value, bits)
    hit = ((row // per) ^ me == bits) & (row % per == col % per)
    return jnp.dot(jnp.where(hit, 1.0, 0.0).astype(BF16), raw, preferred_element_type=F32)


def chunk_products(xg_ref, refs, out_ref, at):
    for ref in refs:
        for i in range(ref.shape[0]):
            out_ref[:, at : at + ref.shape[1]] = contract_last(xg_ref[...], ref[i])
            at += ref.shape[1]
    return at


def in_order(work):
    pl.when(lax.axis_index("mdl") >= 0)(work)


def partner_kernel(
    a_ref, b_ref, c_ref, d_ref, gain_ref, pre_ref, more_ref, w_ref,
    out_ref, xg_ref, next_ref, last_ref, sems,
):
    tokens = out_ref.shape[0]
    rows = last_ref.shape[1]
    last = chunk_copies("partner", w_ref, last_ref, sems.at[0], PRE + MORE, last_ref.shape[0])
    following = chunk_copies("own", w_ref, next_ref, sems.at[1], 0, NEXT)
    start_all(last + following)

    @in_order
    def _():
        values = ordered((a_ref, b_ref, c_ref, d_ref), ORDER, tokens)
        squares = jnp.sum(values * values, axis=1, keepdims=True)
        out_ref[:, -LANES:] = jnp.broadcast_to(squares, (tokens, LANES))
        xg_ref[...] = (values * gain_ref[...]).astype(BF16)
        chunk_products(xg_ref, (pre_ref, more_ref), out_ref, 0)

    wait_all(last)

    @in_order
    def _():
        chunk_products(xg_ref, (last_ref,), out_ref, (PRE + MORE) * rows)

    wait_all(following)


def own_kernel(xg_ref, next_ref, w_ref, out_ref, last_ref, sems):
    rows = last_ref.shape[1]
    copies = chunk_copies("own", w_ref, last_ref, sems, NEXT, last_ref.shape[0])
    start_all(copies)

    @in_order
    def _():
        chunk_products(xg_ref, (next_ref,), out_ref, 0)

    wait_all(copies)
    chunk_products(xg_ref, (last_ref,), out_ref, NEXT * rows)


def project(tokens_in, gain, weights, long_taps, tokens):
    chan = weights.shape[1] // 2
    half = weights.shape[2]
    rows = chan // CUTS
    weights = in_hbm(weights)
    local, pre, taps = prepare(tokens_in, weights, long_taps, tokens)
    pieces = gather_pieces(tokens_in, local)
    more = load_more(weights, pieces[0])
    work = cost(2 * tokens * chan * half * 3, 2 * chan * half * 3)
    partner, xg, following = pl.pallas_call(
        partner_kernel,
        out_shape=(
            jax.ShapeDtypeStruct((tokens, 3 * chan + LANES), F32),
            jax.ShapeDtypeStruct((tokens, half), BF16),
            pltpu.VMEM((NEXT, rows, half), weights.dtype),
        ),
        in_specs=[VMEM] * 7 + [ANY],
        out_specs=(VMEM,) * 3,
        scratch_shapes=[
            pltpu.VMEM((3 * CUTS - PRE - MORE, rows, half), weights.dtype),
            pltpu.SemaphoreType.DMA((2, 3 * CUTS)),
        ],
        compiler_params=params(8),
        cost_estimate=work,
        name="project_partner",
    )(*pieces, gain, in_vmem(pre), in_vmem(more), weights)
    got = lax.ppermute(partner, "mdl", [(0, 1), (1, 0)])
    own = pl.pallas_call(
        own_kernel,
        out_shape=jax.ShapeDtypeStruct((tokens, 3 * chan), F32),
        in_specs=[VMEM] * 2 + [ANY],
        out_specs=VMEM,
        scratch_shapes=[
            pltpu.VMEM((3 * CUTS - NEXT, rows, half), weights.dtype),
            pltpu.SemaphoreType.DMA((3 * CUTS,)),
        ],
        compiler_params=params(8),
        cost_estimate=work,
        name="project_own",
    )(xg, in_vmem(following), weights)
    return own, got, partner, taps


def delay(x, rows):
    if rows == 0:
        return x
    index = lax.broadcasted_iota(jnp.int32, x.shape, 0)
    return jnp.where(index >= rows, pltpu.roll(x, rows, axis=0), 0.0)


def mix_kernel(width, own_ref, got_ref, sent_ref, short_ref, bias_ref, taps_ref, out_ref):
    tokens, chan = out_ref.shape
    reach = taps_ref.shape[0]
    first = pl.multiple_of(lax.axis_index("mdl") * chan, chan)
    squares = sent_ref[:, 3 * chan : 3 * chan + 1] + got_ref[:, 3 * chan : 3 * chan + 1]
    scale = lax.rsqrt(squares / width + EPSILON)
    feats = []
    for branch in range(3):
        span = slice(branch * chan, (branch + 1) * chan)
        total = (own_ref[:, span] + got_ref[:, span]) * scale
        feat = None
        for offset in range(short_ref.shape[1]):
            term = short_ref[branch, pl.ds(offset, 1), pl.ds(first, chan)] * delay(total, offset)
            feat = term if feat is None else feat + term
        feats.append(feat)
    gated = feats[1] * feats[2]
    mixed = bias_ref[:, pl.ds(first, chan)] * gated
    blocks = [mixed[b * ROWS : (b + 1) * ROWS] for b in range(tokens // ROWS)]
    for shift in range(ROWS):
        moved = delay(gated, shift)
        for lag in range(reach // ROWS):
            tap = taps_ref[pl.ds(lag * ROWS + shift, 1), :]
            for b in range(lag, tokens // ROWS):
                blocks[b] = blocks[b] + tap * moved[(b - lag) * ROWS : (b - lag + 1) * ROWS]
    out_ref[...] = (feats[0] * jnp.concatenate(blocks, axis=0)).astype(BF16)


def mix(own, got, sent, short_taps, bias, taps, width):
    tokens, chan = own.shape[0], own.shape[1] // 3
    return pl.pallas_call(
        lambda *refs: mix_kernel(width, *refs),
        out_shape=jax.ShapeDtypeStruct((tokens, chan), BF16),
        in_specs=[VMEM] * 6,
        out_specs=VMEM,
        compiler_params=params(8),
        name="mix",
    )(own, got, sent, jnp.transpose(short_taps, (1, 0, 2)), bias, taps)


def out_kernel(first, piece_ref, w_ref, *refs):
    out_ref = refs[-1]
    tokens, chan = out_ref.shape[0], piece_ref.shape[1]
    total = refs[0][...] if len(refs) > 1 else None
    for k in range(piece_ref.shape[0] // tokens):
        owner = lax.axis_index("seq") ^ ORDER[first + k]
        span = pl.ds(pl.multiple_of(owner * chan, chan), chan)
        term = contract_last(piece_ref[k * tokens : (k + 1) * tokens, :], w_ref[:, span])
        total = term if total is None else total + term
    out_ref[...] = total


def add_kernel(a_ref, b_ref, out_ref):
    out_ref[...] = (a_ref[...] + b_ref[...]).astype(out_ref.dtype)


def project_out(pieces, weights, tokens):
    total, first = [], 0
    for piece in pieces:
        count = piece.shape[0] // tokens
        width = count * piece.shape[1]
        total = [
            pl.pallas_call(
                lambda *refs, first=first: out_kernel(first, *refs),
                out_shape=jax.ShapeDtypeStruct((tokens, weights.shape[0]), F32),
                in_specs=[VMEM] * (2 + len(total)),
                out_specs=VMEM,
                compiler_params=params(8),
                cost_estimate=cost(2 * tokens * weights.shape[0] * width, 2 * weights.shape[0] * width),
                name="project_out",
            )(piece, weights, *total)
        ]
        first += count
    return total[0]


def per_device(tokens_in, norm_gain, in_proj, short_taps, long_taps, skip_bias, out_proj):
    own_tokens, half = tokens_in.shape
    width = 2 * half
    tokens = own_tokens * lax.axis_size("seq")
    chan = in_proj.shape[2] // 2
    weights_in = in_proj.reshape(3, 2 * chan, half)
    weights_out = out_proj.reshape(out_proj.shape[0], -1)
    own, got, sent, taps = project(tokens_in, norm_gain[None, :], weights_in, long_taps, tokens)
    gated = mix(own, got, sent, short_taps, skip_bias[None, :], taps, width)
    partial_out = project_out(gather_pieces(gated, gated), weights_out, tokens)
    other = lax.ppermute(partial_out, "mdl", [(0, 1), (1, 0)])
    return pl.pallas_call(
        add_kernel,
        out_shape=jax.ShapeDtypeStruct(other.shape, BF16),
        in_specs=[VMEM] * 2,
        out_specs=VMEM,
        compiler_params=params(4),
        name="add",
    )(partial_out, other)


def per_device_any(tokens_in, norm_gain, in_proj, short_taps, long_taps, skip_bias, out_proj):
    half = tokens_in.shape[1]
    width = 2 * half
    chan = in_proj.shape[2] // 2
    seq_index = lax.axis_index("seq")
    mdl_index = lax.axis_index("mdl")
    values = tokens_in.astype(F32)
    squares = lax.psum(jnp.sum(values * values, axis=1), "mdl")
    scale = lax.rsqrt(squares / width + EPSILON)
    normed = (values * scale[:, None] * norm_gain[None, :]).astype(BF16)
    part = contract_last(
        lax.all_gather(normed, "seq", axis=0, tiled=True), in_proj.reshape(-1, half)
    )
    tokens = part.shape[0]
    part = part.reshape(tokens, 3, 2, chan)
    summed = lax.psum_scatter(part, "mdl", scatter_dimension=2, tiled=True)
    summed = summed.reshape(tokens, 3, chan)
    short_local = lax.dynamic_slice_in_dim(short_taps, mdl_index * chan, chan, 2)
    bias_local = lax.dynamic_slice_in_dim(skip_bias, mdl_index * chan, chan, 0)
    short_count = short_local.shape[0]
    padded = jnp.pad(summed, ((short_count - 1, 0), (0, 0), (0, 0)))
    features = sum(
        short_local[i][None] * padded[short_count - 1 - i : short_count - 1 - i + tokens]
        for i in range(short_count)
    )
    gated = features[:, 1, :] * features[:, 2, :]
    group_width = width // long_taps.shape[0]
    groups = (seq_index * 2 * chan + mdl_index * chan + jnp.arange(chan)) // group_width
    taps = long_taps[groups].T
    reach = min(tokens, taps.shape[0])
    shifted = jnp.pad(gated, ((reach - 1, 0), (0, 0)))
    mixed = bias_local[None, :] * gated + sum(
        taps[i][None, :] * shifted[reach - 1 - i : reach - 1 - i + tokens] for i in range(reach)
    )
    gated_out = (features[:, 0, :] * mixed).astype(BF16)
    rows = out_proj.reshape(out_proj.shape[0], -1)
    folded = contract_last(lax.all_gather(gated_out, "seq", axis=1, tiled=True), rows)
    return lax.psum(folded, "mdl").astype(BF16)


def solution(mesh):
    seq = mesh.shape["seq"]
    in_specs = (
        P(("grp", "seq"), "mdl"),
        P("mdl"),
        P("seq", None, None, "mdl"),
        P(None, None, "seq"),
        P(),
        P("seq"),
        P("seq", "mdl", None),
    )
    body = per_device if seq == 8 and mesh.shape["mdl"] == 2 else per_device_any
    return jax.shard_map(
        body, mesh=mesh, in_specs=in_specs, out_specs=P("grp", "seq"), check_vma=False
    )
```

time: 62.5 us -> 39.9 us (0.64)
  local copies, waits for them, and re-layouts: 20.5 us -> 0.03 us
  waiting for transfers between devices: 15.4 us -> 8.07 us
  Pallas kernels: 11 us -> 17.5 us
  other arithmetic: 1.44 us -> 0.01 us
    unnamed x15 -> x10, local copies, waits for them, and re-layouts: 20.5 us -> 0.03 us
    ppermute x8, waiting for transfers between devices: 14 us -> 6.73 us  [swap(): return lax.ppermute(x, 'seq', [(i, i ^ bits) for i in range(count)])]
    pallas_call x4 -> x11, Pallas kernels: 10.6 us -> 17.1 us  [the longest x1 4.32 us: project(): pl.pallas_call(partner_kernel, out_shape=(jax.ShapeDtypeStruct((tokens, 3...]
    concatenate x2 -> x0, other arithmetic: 0.8 us -> none  [gather_pieces(): pair = jnp.concatenate([x, swap(x, 1)], axis=0)]
    convert_element_type x1 -> x0, other arithmetic: 0.64 us -> none  [per_device(): return (partial_out + other).astype(BF16)]
  transfers between devices with their start and end apart: 10 -> 10, of which waited for: 7 -> 6; matrix products, arithmetic and copies ran while one was open for 0% -> 0% of each run, Pallas kernels for 7% -> 29%
where the time goes in v2:
time: 39.9 us; the launch traced here: 39.6 us
  Pallas kernels  17.5 us (44%)
  starting transfers between devices  13.9 us (35%)
  waiting for transfers between devices  8.07 us (20%)
    ppermute x8, starting transfers between devices, swap(): return lax.ppermute(x, 'seq', [(i, i ^ bits) for i in range(count)])  13.7 us
    ppermute x8, waiting for transfers between devices, swap(): return lax.ppermute(x, 'seq', [(i, i ^ bits) for i in range(count)])  6.73 us
    pallas_call x1, Pallas kernels, project(): pl.pallas_call(partner_kernel, out_shape=(jax.ShapeDtypeStruct((tokens, 3...  4.32 us
    pallas_call x1, Pallas kernels, project(): pl.pallas_call(own_kernel, out_shape=jax.ShapeDtypeStruct((tokens, 3 * ch...  4 us
    pallas_call x1, Pallas kernels, load_more(): pl.pallas_call(load_kernel, out_shape=pltpu.VMEM((MORE, rows, half), weig...  3.64 us
    pallas_call x4, Pallas kernels, project_out(): pl.pallas_call(lambda *refs, first=first: out_kernel(first, *refs), out_s...  2.85 us
    pallas_call x1, Pallas kernels, prepare(): pl.pallas_call(prepare_kernel, out_shape=(jax.ShapeDtypeStruct(x.shape, x...  1.65 us
    ppermute x1, waiting for transfers between devices, per_device(): other = lax.ppermute(partial_out, 'mdl', [(0, 1), (1, 0)])  1.33 us
  transfers between devices with their start and end apart: 10, of which 6 were waited for; matrix products, arithmetic and copies ran while one was open for 0% of the time, Pallas kernels for 29%

profile of v2, /device:TPU:0, one launch (start us, length us, event | category | flops | bytes accessed | tf_op | source)
XLA Modules:
  0.0 39.6 jit_solution(11038872219410388996)
XLA Ops:
  0.0 2.9 %collective-permute-start = (bf16[4,4096]{1,0:T(4,128)(2,1)}, bf16[4,4096]{1,0:T(4,128)(2,1)S(1)}, u32[]{:S(2)}, u32[]{:S(2)}) collective-permute-start(bf16[4,4096]{1,0:T(4,128)(2,1)} %x_ref.1), channel_id=1, source_target_pairs={{0,2},{2,0},{4,6},{6,4},{8,10},{10,8},{12,14},{14,12},{1,3},{3,1},... | collective-permute-start | bytes 98312 | tf_op jit(solution)/shard_map/ppermute | solution.py:32
  2.9 1.7 %prepare.1 = (bf16[4,4096]{1,0:T(4,128)(2,1)S(1)}, bf16[1,256,4096]{2,1,0:T(8,128)(2,1)S(1)}, f32[32,512]{1,0:T(8,128)S(1)}) custom-call(bf16[4,4096]{1,0:T(4,128)(2,1)} %x_ref.1, bf16[3,1024,4096]{2,1,0:T(8,128)(2,1)} %bitcast.14, f32[512,128]{1,0:T(8,128)} %taps_ref.1), custom_call_target="tpu_custom_call" | custom-call | bytes 4194304 | tf_op jit(solution)/shard_map/prepare/pallas_call | solution.py:129
  4.6 0.4 %collective-permute-done.refs_1_ = bf16[4,4096]{1,0:T(4,128)(2,1)S(1)} collective-permute-done((bf16[4,4096]{1,0:T(4,128)(2,1)}, bf16[4,4096]{1,0:T(4,128)(2,1)S(1)}, u32[]{:S(2)}, u32[]{:S(2)}) %collective-permute-start) | collective-permute-done | bytes 32800 | tf_op jit(solution)/shard_map/ppermute | solution.py:32
  5.1 0.0 copy-start.1
  5.1 4.2 %collective-permute-start.3 = (bf16[8,4096]{1,0:T(8,128)(2,1)S(1)}, bf16[8,4096]{1,0:T(8,128)(2,1)S(1)}, u32[]{:S(2)}, u32[]{:S(2)}) collective-permute-start(bf16[8,4096]{1,0:T(8,128)(2,1)S(1)} %stack.2.after_ref.a_ref), channel_id=1, source_target_pairs={{0,12},{2,14},{4,8},{6,10},{8,4},{10,6},{12,0},{14,2},{1,13},{3,15... | collective-permute-start | bytes 196616 | tf_op jit(solution)/shard_map/ppermute | solution.py:32
  9.3 0.0 collective-permute-start.2
  9.3 0.6 %collective-permute-start.1 = (bf16[8,4096]{1,0:T(8,128)(2,1)S(1)}, bf16[8,4096]{1,0:T(8,128)(2,1)S(1)}, u32[]{:S(2)}, u32[]{:S(2)}) collective-permute-start(bf16[8,4096]{1,0:T(8,128)(2,1)S(1)} %stack.2.after_ref.a_ref), channel_id=1, source_target_pairs={{0,4},{2,6},{4,0},{6,2},{8,12},{10,14},{12,8},{14,10},{1,5},{3,7},... | collective-permute-start | bytes 196616 | tf_op jit(solution)/shard_map/ppermute | solution.py:32
  9.9 3.6 %load_more.1.more_ref = bf16[4,256,4096]{2,1,0:T(8,128)(2,1)S(1)} custom-call(bf16[3,1024,4096]{2,1,0:T(8,128)(2,1)} %bitcast.15, bf16[8,4096]{1,0:T(8,128)(2,1)S(1)} %stack.2.after_ref.a_ref), custom_call_target="tpu_custom_call" | custom-call | bytes 16777216 | tf_op jit(solution)/shard_map/load_more/pallas_call | solution.py:157
  13.6 0.0 collective-permute-done.3.d_ref
  13.6 0.9 %collective-permute-done.2.c_ref = bf16[8,4096]{1,0:T(8,128)(2,1)S(1)} collective-permute-done((bf16[8,4096]{1,0:T(8,128)(2,1)S(1)}, bf16[8,4096]{1,0:T(8,128)(2,1)S(1)}, u32[]{:S(2)}, u32[]{:S(2)}) %collective-permute-start.2) | collective-permute-done | bytes 65568 | tf_op jit(solution)/shard_map/ppermute | solution.py:32
  14.5 0.0 collective-permute-done.1.b_ref
  14.5 4.3 %project_partner.1 = (f32[32,1664]{1,0:T(8,128)S(1)}, bf16[32,4096]{1,0:T(8,128)(2,1)S(1)}, bf16[4,256,4096]{2,1,0:T(8,128)(2,1)S(1)}) custom-call(bf16[8,4096]{1,0:T(8,128)(2,1)S(1)} %stack.2.after_ref.a_ref, bf16[8,4096]{1,0:T(8,128)(2,1)S(1)} %collective-permute-done.1.b_ref, bf16[8,4096]{1,0:T(8,128)(2,1)S(1)} %collective-permute-done.2.c_ref, ...), custom_call_target="tpu_custom_call" | custom-call | flops 402653184 | bytes 12582912 | tf_op jit(solution)/shard_map/project_partner/pallas_call | solution.py:244
  18.8 0.1 collective-permute-start.4
  18.9 0.0 copy-start
  18.9 0.0 copy-start.2
  18.9 4.0 %project_own.1.refs_0_ = f32[32,1536]{1,0:T(8,128)S(1)} custom-call(bf16[32,4096]{1,0:T(8,128)(2,1)S(1)} %get-tuple-element.13.xg_ref, bf16[4,256,4096]{2,1,0:T(8,128)(2,1)S(1)} %get-tuple-element.14.next_ref, bf16[3,1024,4096]{2,1,0:T(8,128)(2,1)} %bitcast.17), custom_call_target="tpu_custom_call" | custom-call | flops 402653184 | bytes 12582912 | tf_op jit(solution)/shard_map/project_own/pallas_call | solution.py:262
  22.9 0.4 %mix.1.refs_0_ = bf16[32,512]{1,0:T(8,128)(2,1)S(1)} custom-call(f32[32,1536]{1,0:T(8,128)S(1)} %project_own.1.refs_0_, f32[32,1664]{1,0:T(8,128)S(1)} %collective-permute-done.4.refs_1_, f32[32,1664]{1,0:T(8,128)S(1)} %get-tuple-element.15.refs_2_, f32[3,7,1024]{2,1,0:T(8,128)S(1)} %bitcast.11, f32[1,1024]{1,0:T(1,128)S(1)} %bitcast.13, ...), custom_call_target="tpu_custom_call" | custom-call | tf_op jit(solution)/shard_map/mix/pallas_call | solution.py:314
  23.4 1.6 %collective-permute-start.5 = (bf16[32,512]{1,0:T(8,128)(2,1)S(1)}, bf16[32,512]{1,0:T(8,128)(2,1)S(1)}, u32[]{:S(2)}, u32[]{:S(2)}) collective-permute-start(bf16[32,512]{1,0:T(8,128)(2,1)S(1)} %mix.1.refs_0_), channel_id=1, source_target_pairs={{0,2},{2,0},{4,6},{6,4},{8,10},{10,8},{12,14},{14,12},{1,3},{3,1},... | collective-permute-start | bytes 98312 | tf_op jit(solution)/shard_map/ppermute | solution.py:32
  24.9 2.4 %collective-permute-done.5.refs_1_ = bf16[32,512]{1,0:T(8,128)(2,1)S(1)} collective-permute-done((bf16[32,512]{1,0:T(8,128)(2,1)S(1)}, bf16[32,512]{1,0:T(8,128)(2,1)S(1)}, u32[]{:S(2)}, u32[]{:S(2)}) %collective-permute-start.5) | collective-permute-done | bytes 32800 | tf_op jit(solution)/shard_map/ppermute | solution.py:32
  27.3 0.5 %collective-permute-start.8 = (bf16[64,512]{1,0:T(8,128)(2,1)S(1)}, bf16[64,512]{1,0:T(8,128)(2,1)S(1)}, u32[]{:S(2)}, u32[]{:S(2)}) collective-permute-start(bf16[64,512]{1,0:T(8,128)(2,1)S(1)} %stack.3.refs_0_), channel_id=1, source_target_pairs={{0,4},{2,6},{4,0},{6,2},{8,12},{10,14},{12,8},{14,10},{1,5},{3,7},... | collective-permute-start | bytes 196616 | tf_op jit(solution)/shard_map/ppermute | solution.py:32
  27.9 2.9 %collective-permute-start.7 = (bf16[64,512]{1,0:T(8,128)(2,1)S(1)}, bf16[64,512]{1,0:T(8,128)(2,1)S(1)}, u32[]{:S(2)}, u32[]{:S(2)}) collective-permute-start(bf16[64,512]{1,0:T(8,128)(2,1)S(1)} %stack.3.refs_0_), channel_id=1, source_target_pairs={{0,8},{2,10},{4,12},{6,14},{8,0},{10,2},{12,4},{14,6},{1,9},{3,11}... | collective-permute-start | bytes 196616 | tf_op jit(solution)/shard_map/ppermute | solution.py:32
  30.8 0.9 %collective-permute-start.6 = (bf16[64,512]{1,0:T(8,128)(2,1)S(1)}, bf16[64,512]{1,0:T(8,128)(2,1)S(1)}, u32[]{:S(2)}, u32[]{:S(2)}) collective-permute-start(bf16[64,512]{1,0:T(8,128)(2,1)S(1)} %stack.3.refs_0_), channel_id=1, source_target_pairs={{0,12},{2,14},{4,8},{6,10},{8,4},{10,6},{12,0},{14,2},{1,13},{3,15... | collective-permute-start | bytes 196616 | tf_op jit(solution)/shard_map/ppermute | solution.py:32
  31.7 0.7 %project_out.4.refs_2_ = f32[32,1024]{1,0:T(8,128)S(1)} custom-call(bf16[64,512]{1,0:T(8,128)(2,1)S(1)} %stack.3.refs_0_, bf16[1024,4096]{1,0:T(8,128)(2,1)S(1)} %bitcast.7), custom_call_target="tpu_custom_call" | custom-call | flops 67108864 | bytes 2097152 | tf_op jit(solution)/shard_map/project_out/pallas_call | solution.py:346
  32.4 0.0 collective-permute-done.8.refs_0_
  32.5 0.7 %project_out.5.refs_2_ = f32[32,1024]{1,0:T(8,128)S(1)} custom-call(bf16[64,512]{1,0:T(8,128)(2,1)S(1)} %collective-permute-done.8.refs_0_, bf16[1024,4096]{1,0:T(8,128)(2,1)S(1)} %bitcast.8, f32[32,1024]{1,0:T(8,128)S(1)} %project_out.4.refs_2_), custom_call_target="tpu_custom_call" | custom-call | flops 67108864 | bytes 2097152 | tf_op jit(solution)/shard_map/project_out/pallas_call | solution.py:346
  33.2 1.8 %collective-permute-done.7.refs_0_ = bf16[64,512]{1,0:T(8,128)(2,1)S(1)} collective-permute-done((bf16[64,512]{1,0:T(8,128)(2,1)S(1)}, bf16[64,512]{1,0:T(8,128)(2,1)S(1)}, u32[]{:S(2)}, u32[]{:S(2)}) %collective-permute-start.7) | collective-permute-done | bytes 65568 | tf_op jit(solution)/shard_map/ppermute | solution.py:32
  34.9 0.7 %project_out.6.refs_2_ = f32[32,1024]{1,0:T(8,128)S(1)} custom-call(bf16[64,512]{1,0:T(8,128)(2,1)S(1)} %collective-permute-done.7.refs_0_, bf16[1024,4096]{1,0:T(8,128)(2,1)S(1)} %bitcast.9, f32[32,1024]{1,0:T(8,128)S(1)} %project_out.5.refs_2_), custom_call_target="tpu_custom_call" | custom-call | flops 67108864 | bytes 2097152 | tf_op jit(solution)/shard_map/project_out/pallas_call | solution.py:346
  35.7 1.2 %collective-permute-done.6.refs_0_ = bf16[64,512]{1,0:T(8,128)(2,1)S(1)} collective-permute-done((bf16[64,512]{1,0:T(8,128)(2,1)S(1)}, bf16[64,512]{1,0:T(8,128)(2,1)S(1)}, u32[]{:S(2)}, u32[]{:S(2)}) %collective-permute-start.6) | collective-permute-done | bytes 65568 | tf_op jit(solution)/shard_map/ppermute | solution.py:32
  36.9 0.7 %project_out.7.a_ref = f32[32,1024]{1,0:T(8,128)S(1)} custom-call(bf16[64,512]{1,0:T(8,128)(2,1)S(1)} %collective-permute-done.6.refs_0_, bf16[1024,4096]{1,0:T(8,128)(2,1)S(1)} %bitcast.10, f32[32,1024]{1,0:T(8,128)S(1)} %project_out.6.refs_2_), custom_call_target="tpu_custom_call" | custom-call | flops 67108864 | bytes 2097152 | tf_op jit(solution)/shard_map/project_out/pallas_call | solution.py:346
  37.6 0.1 collective-permute-start.9
  37.6 1.3 %collective-permute-done.9.b_ref = f32[32,1024]{1,0:T(8,128)S(1)} collective-permute-done((f32[32,1024]{1,0:T(8,128)S(1)}, f32[32,1024]{1,0:T(8,128)S(1)}, u32[]{:S(2)}, u32[]{:S(2)}) %collective-permute-start.9) | collective-permute-done | bytes 131104 | tf_op jit(solution)/shard_map/ppermute | solution.py:370
  39.0 0.6 %add.1 = bf16[32,1024]{1,0:T(8,128)(2,1)} custom-call(f32[32,1024]{1,0:T(8,128)S(1)} %project_out.7.a_ref, f32[32,1024]{1,0:T(8,128)S(1)} %collective-permute-done.9.b_ref), custom_call_target="tpu_custom_call" | custom-call | tf_op jit(solution)/shard_map/add/pallas_call | solution.py:371
  (11 shorter events, 0.0 us)
Async XLA Ops:
  0.0 5.0 %collective-permute-start = (bf16[4,4096]{1,0:T(4,128)(2,1)}, bf16[4,4096]{1,0:T(4,128)(2,1)S(1)}, u32[]{:S(2)}, u32[]{:S(2)}) collective-permute-start(bf16[4,4096]{1,0:T(4,128)(2,1)} %x_ref.1), channel_id=1, source_target_pairs={{0,2},{2,0},{4,6},{6,4},{8,10},{10,8},{12,14},{14,12},{1,3},{3,1},... | collective-permute-start | bytes 98312 | tf_op jit(solution)/shard_map/ppermute | solution.py:32
  5.1 9.4 %copy-start.1 = (f32[4096]{0:T(1024)S(1)}, f32[4096]{0:T(1024)}, u32[]{:S(2)}) copy-start(f32[4096]{0:T(1024)} %param.8) | copy-start | bytes 49156
  5.1 8.5 %collective-permute-start.3 = (bf16[8,4096]{1,0:T(8,128)(2,1)S(1)}, bf16[8,4096]{1,0:T(8,128)(2,1)S(1)}, u32[]{:S(2)}, u32[]{:S(2)}) collective-permute-start(bf16[8,4096]{1,0:T(8,128)(2,1)S(1)} %stack.2.after_ref.a_ref), channel_id=1, source_target_pairs={{0,12},{2,14},{4,8},{6,10},{8,4},{10,6},{12,0},{14,2},{1,13},{3,15... | collective-permute-start | bytes 196616 | tf_op jit(solution)/shard_map/ppermute | solution.py:32
  9.3 5.2 %collective-permute-start.2 = (bf16[8,4096]{1,0:T(8,128)(2,1)S(1)}, bf16[8,4096]{1,0:T(8,128)(2,1)S(1)}, u32[]{:S(2)}, u32[]{:S(2)}) collective-permute-start(bf16[8,4096]{1,0:T(8,128)(2,1)S(1)} %stack.2.after_ref.a_ref), channel_id=1, source_target_pairs={{0,8},{2,10},{4,12},{6,14},{8,0},{10,2},{12,4},{14,6},{1,9},{3,11}... | collective-permute-start | bytes 196616 | tf_op jit(solution)/shard_map/ppermute | solution.py:32
  9.3 5.2 %collective-permute-start.1 = (bf16[8,4096]{1,0:T(8,128)(2,1)S(1)}, bf16[8,4096]{1,0:T(8,128)(2,1)S(1)}, u32[]{:S(2)}, u32[]{:S(2)}) collective-permute-start(bf16[8,4096]{1,0:T(8,128)(2,1)S(1)} %stack.2.after_ref.a_ref), channel_id=1, source_target_pairs={{0,4},{2,6},{4,0},{6,2},{8,12},{10,14},{12,8},{14,10},{1,5},{3,7},... | collective-permute-start | bytes 196616 | tf_op jit(solution)/shard_map/ppermute | solution.py:32
  9.9 21.8 %slice-start = ((s8[8388608]{0:T(1024)(128)(4,1)}), s8[4194304]{0:T(1024)(128)(4,1)S(1)}, s32[]{:S(2)}) async-start(s8[8388608]{0:T(1024)(128)(4,1)} %bitcast.5), calls=%async_computation | async-start | bytes 8388608
  14.5 17.3 %slice-start.1 = ((s8[8388608]{0:T(1024)(128)(4,1)}), s8[4194304]{0:T(1024)(128)(4,1)S(1)}, s32[]{:S(2)}) async-start(s8[8388608]{0:T(1024)(128)(4,1)} %bitcast.5), calls=%async_computation.1 | async-start | bytes 8388608
  18.8 4.1 %collective-permute-start.4 = (f32[32,1664]{1,0:T(8,128)S(1)}, f32[32,1664]{1,0:T(8,128)S(1)}, u32[]{:S(2)}, u32[]{:S(2)}) collective-permute-start(f32[32,1664]{1,0:T(8,128)S(1)} %get-tuple-element.15.refs_2_), channel_id=1, source_target_pairs={{0,1},{1,0},{2,3},{3,2},{4,5},{5,4},{6,7},{7,6},{8,9},{9,8},{10,11... | collective-permute-start | bytes 638984 | tf_op jit(solution)/shard_map/ppermute | solution.py:261
  18.9 4.0 %copy-start = (f32[7,3,1024]{2,0,1:T(8,128)S(1)}, f32[7,3,1024]{2,0,1:T(8,128)}, u32[]{:S(2)}) copy-start(f32[7,3,1024]{2,0,1:T(8,128)} %param.10) | copy-start | bytes 258052
  18.9 4.0 %copy-start.2 = (f32[1024]{0:T(1024)S(1)}, f32[1024]{0:T(1024)}, u32[]{:S(2)}) copy-start(f32[1024]{0:T(1024)} %param.12) | copy-start | bytes 12292
  23.4 4.0 %collective-permute-start.5 = (bf16[32,512]{1,0:T(8,128)(2,1)S(1)}, bf16[32,512]{1,0:T(8,128)(2,1)S(1)}, u32[]{:S(2)}, u32[]{:S(2)}) collective-permute-start(bf16[32,512]{1,0:T(8,128)(2,1)S(1)} %mix.1.refs_0_), channel_id=1, source_target_pairs={{0,2},{2,0},{4,6},{6,4},{8,10},{10,8},{12,14},{14,12},{1,3},{3,1},... | collective-permute-start | bytes 98312 | tf_op jit(solution)/shard_map/ppermute | solution.py:32
  27.3 5.1 %collective-permute-start.8 = (bf16[64,512]{1,0:T(8,128)(2,1)S(1)}, bf16[64,512]{1,0:T(8,128)(2,1)S(1)}, u32[]{:S(2)}, u32[]{:S(2)}) collective-permute-start(bf16[64,512]{1,0:T(8,128)(2,1)S(1)} %stack.3.refs_0_), channel_id=1, source_target_pairs={{0,4},{2,6},{4,0},{6,2},{8,12},{10,14},{12,8},{14,10},{1,5},{3,7},... | collective-permute-start | bytes 196616 | tf_op jit(solution)/shard_map/ppermute | solution.py:32
  27.9 7.1 %collective-permute-start.7 = (bf16[64,512]{1,0:T(8,128)(2,1)S(1)}, bf16[64,512]{1,0:T(8,128)(2,1)S(1)}, u32[]{:S(2)}, u32[]{:S(2)}) collective-permute-start(bf16[64,512]{1,0:T(8,128)(2,1)S(1)} %stack.3.refs_0_), channel_id=1, source_target_pairs={{0,8},{2,10},{4,12},{6,14},{8,0},{10,2},{12,4},{14,6},{1,9},{3,11}... | collective-permute-start | bytes 196616 | tf_op jit(solution)/shard_map/ppermute | solution.py:32
  30.8 6.1 %collective-permute-start.6 = (bf16[64,512]{1,0:T(8,128)(2,1)S(1)}, bf16[64,512]{1,0:T(8,128)(2,1)S(1)}, u32[]{:S(2)}, u32[]{:S(2)}) collective-permute-start(bf16[64,512]{1,0:T(8,128)(2,1)S(1)} %stack.3.refs_0_), channel_id=1, source_target_pairs={{0,12},{2,14},{4,8},{6,10},{8,4},{10,6},{12,0},{14,2},{1,13},{3,15... | collective-permute-start | bytes 196616 | tf_op jit(solution)/shard_map/ppermute | solution.py:32
  37.6 1.4 %collective-permute-start.9 = (f32[32,1024]{1,0:T(8,128)S(1)}, f32[32,1024]{1,0:T(8,128)S(1)}, u32[]{:S(2)}, u32[]{:S(2)}) collective-permute-start(f32[32,1024]{1,0:T(8,128)S(1)} %project_out.7.a_ref), channel_id=1, source_target_pairs={{0,1},{1,0},{2,3},{3,2},{4,5},{5,4},{6,7},{7,6},{8,9},{9,8},{10,11... | collective-permute-start | bytes 393224 | tf_op jit(solution)/shard_map/ppermute | solution.py:370

commit v3 on v2

--- a/solution.py
+++ b/solution.py
@@ -1,3 +1,5 @@
+import functools
+
 import jax
 import jax.numpy as jnp
 from jax import lax
@@ -49,12 +51,13 @@
     )(*parts)
 
 
-ORDER = (0, 1, 2, 3, 4, 5, 6, 7)
+ORDER = (0, 1, 6, 7, 4, 5, 2, 3)
 
 
 def gather_pieces(x, local):
     pair = stack(local, swap(x, 1))
-    return [pair] + [swap(pair, bits) for bits in (2, 4, 6)]
+    far, mid, near = [swap(pair, bits) for bits in (6, 4, 2)]
+    return [pair, far, mid, near]
 
 
 def in_vmem(x):
@@ -70,44 +73,15 @@
     return pl.multiple_of((mine if which == "own" else 1 - mine) * chan, chan)
 
 
-CUTS = 2
-PRE = 1
-MORE = 4
-NEXT = 4
-
-
-def chunk_copies(which, w_ref, out_ref, sems, first, count):
-    rows = out_ref.shape[1]
-    start = rows_of(which, rows * CUTS)
-    return [
-        pltpu.make_async_copy(
-            w_ref.at[i // CUTS, pl.ds(start + i % CUTS * rows, rows)],
-            out_ref.at[i - first],
-            sems.at[i - first],
-        )
-        for i in range(first, first + count)
-    ]
-
-
-def start_all(copies):
-    for copy in copies:
-        copy.start()
-
-
-def wait_all(copies):
-    for copy in copies:
-        copy.wait()
-
-
-def prepare_kernel(x_ref, w_ref, taps_ref, local_ref, chunks_ref, spread_ref, group_taps, sems, small):
+def prepare_kernel(x_ref, taps_ref, local_ref, spread_ref, group_taps, sems):
     chan = spread_ref.shape[1]
     groups = group_taps.shape[0]
     index = lax.axis_index("seq") * 2 + lax.axis_index("mdl")
     near = pl.ds(pl.multiple_of(index * groups, groups), groups)
-    fetch = pltpu.make_async_copy(taps_ref.at[near], group_taps, small.at[0])
-    move = pltpu.make_async_copy(x_ref, local_ref, small.at[1])
-    copies = chunk_copies("partner", w_ref, chunks_ref, sems, 0, PRE)
-    start_all([fetch, move] + copies)
+    fetch = pltpu.make_async_copy(taps_ref.at[near], group_taps, sems.at[0])
+    move = pltpu.make_async_copy(x_ref, local_ref, sems.at[1])
+    fetch.start()
+    move.start()
     fetch.wait()
     grp = lax.broadcasted_iota(jnp.int32, (groups, chan), 0)
     ch = lax.broadcasted_iota(jnp.int32, (groups, chan), 1)
@@ -119,51 +93,28 @@
         preferred_element_type=F32,
         precision=lax.Precision.HIGHEST,
     )[: spread_ref.shape[0]]
-    wait_all([move] + copies)
-
-
-def prepare(x, weights, long_taps, tokens):
-    chan, half = weights.shape[1] // 2, weights.shape[2]
+    move.wait()
+
+
+def prepare(x, long_taps, tokens, chan):
     reach = min(tokens, long_taps.shape[1])
-    groups = long_taps.shape[0] * chan // (2 * half)
+    groups = long_taps.shape[0] * chan // (2 * x.shape[1])
     return pl.pallas_call(
         prepare_kernel,
         out_shape=(
             jax.ShapeDtypeStruct(x.shape, x.dtype),
-            pltpu.VMEM((PRE, chan // CUTS, half), weights.dtype),
             jax.ShapeDtypeStruct((reach, chan), F32),
         ),
-        in_specs=[ANY] * 3,
-        out_specs=(VMEM,) * 3,
+        in_specs=[ANY] * 2,
+        out_specs=(VMEM,) * 2,
         scratch_shapes=[
             pltpu.VMEM((groups, long_taps.shape[1]), F32),
-            pltpu.SemaphoreType.DMA((PRE,)),
             pltpu.SemaphoreType.DMA((2,)),
         ],
         compiler_params=params(4),
-        cost_estimate=cost(0, 4 * PRE * chan // CUTS * half),
+        cost_estimate=cost(12 * 10**9, 4 * MIB),
         name="prepare",
-    )(in_hbm(x), weights, in_hbm(long_taps))
-
-
-def load_kernel(w_ref, after_ref, out_ref, sems):
-    copies = chunk_copies("partner", w_ref, out_ref, sems, PRE, MORE)
-    start_all(copies)
-    wait_all(copies)
-
-
-def load_more(weights, after):
-    rows, half = weights.shape[1] // 2 // CUTS, weights.shape[2]
-    return pl.pallas_call(
-        load_kernel,
-        out_shape=pltpu.VMEM((MORE, rows, half), weights.dtype),
-        in_specs=[ANY, ANY],
-        out_specs=VMEM,
-        scratch_shapes=[pltpu.SemaphoreType.DMA((MORE,))],
-        compiler_params=params(4),
-        cost_estimate=cost(0, 4 * MORE * rows * half),
-        name="load_more",
-    )(weights, after)
+    )(in_hbm(x), in_hbm(long_taps))
 
 
 def ordered(pieces, order, tokens):
@@ -180,99 +131,76 @@
     return jnp.dot(jnp.where(hit, 1.0, 0.0).astype(BF16), raw, preferred_element_type=F32)
 
 
-def chunk_products(xg_ref, refs, out_ref, at):
-    for ref in refs:
-        for i in range(ref.shape[0]):
-            out_ref[:, at : at + ref.shape[1]] = contract_last(xg_ref[...], ref[i])
-            at += ref.shape[1]
-    return at
-
-
-def in_order(work):
-    pl.when(lax.axis_index("mdl") >= 0)(work)
-
-
 def partner_kernel(
-    a_ref, b_ref, c_ref, d_ref, gain_ref, pre_ref, more_ref, w_ref,
-    out_ref, xg_ref, next_ref, last_ref, sems,
+    a_ref, b_ref, c_ref, d_ref, gain_ref, w_ref, wo_ref, out_ref, xg_ref, load_ref, sem
 ):
+    load = pltpu.make_async_copy(wo_ref.at[pl.ds(0, load_ref.shape[0])], load_ref, sem)
+    load.start()
     tokens = out_ref.shape[0]
-    rows = last_ref.shape[1]
-    last = chunk_copies("partner", w_ref, last_ref, sems.at[0], PRE + MORE, last_ref.shape[0])
-    following = chunk_copies("own", w_ref, next_ref, sems.at[1], 0, NEXT)
-    start_all(last + following)
-
-    @in_order
-    def _():
-        values = ordered((a_ref, b_ref, c_ref, d_ref), ORDER, tokens)
-        squares = jnp.sum(values * values, axis=1, keepdims=True)
-        out_ref[:, -LANES:] = jnp.broadcast_to(squares, (tokens, LANES))
-        xg_ref[...] = (values * gain_ref[...]).astype(BF16)
-        chunk_products(xg_ref, (pre_ref, more_ref), out_ref, 0)
-
-    wait_all(last)
-
-    @in_order
-    def _():
-        chunk_products(xg_ref, (last_ref,), out_ref, (PRE + MORE) * rows)
-
-    wait_all(following)
-
-
-def own_kernel(xg_ref, next_ref, w_ref, out_ref, last_ref, sems):
-    rows = last_ref.shape[1]
-    copies = chunk_copies("own", w_ref, last_ref, sems, NEXT, last_ref.shape[0])
-    start_all(copies)
-
-    @in_order
-    def _():
-        chunk_products(xg_ref, (next_ref,), out_ref, 0)
-
-    wait_all(copies)
-    chunk_products(xg_ref, (last_ref,), out_ref, NEXT * rows)
-
-
-def project(tokens_in, gain, weights, long_taps, tokens):
-    chan = weights.shape[1] // 2
-    half = weights.shape[2]
-    rows = chan // CUTS
-    weights = in_hbm(weights)
-    local, pre, taps = prepare(tokens_in, weights, long_taps, tokens)
+    chan = w_ref.shape[2] // 2
+    values = ordered((a_ref, b_ref, c_ref, d_ref), ORDER, tokens)
+    squares = jnp.sum(values * values, axis=1, keepdims=True)
+    out_ref[:, 3 * chan :] = jnp.broadcast_to(squares, (tokens, LANES))
+    xg_ref[...] = (values * gain_ref[...]).astype(BF16)
+    first = rows_of("partner", chan)
+    for p in range(3):
+        out_ref[:, p * chan : (p + 1) * chan] = contract_last(
+            xg_ref[...], w_ref[0, p, pl.ds(first, chan), :]
+        )
+    load.wait()
+
+
+def own_kernel(xg_ref, w_ref, wo_ref, out_ref, load_ref, sem):
+    rows = load_ref.shape[0]
+    load = pltpu.make_async_copy(wo_ref.at[pl.ds(wo_ref.shape[0] - rows, rows)], load_ref, sem)
+    load.start()
+    chan = w_ref.shape[2] // 2
+    first = rows_of("own", chan)
+    for p in range(3):
+        out_ref[:, p * chan : (p + 1) * chan] = contract_last(
+            xg_ref[...], w_ref[0, p, pl.ds(first, chan), :]
+        )
+    load.wait()
+
+
+def project(tokens_in, gain, weights, weights_out, long_taps, tokens):
+    chan = weights.shape[2] // 2
+    half = weights.shape[3]
+    local, taps = prepare(tokens_in, long_taps, tokens, chan)
     pieces = gather_pieces(tokens_in, local)
-    more = load_more(weights, pieces[0])
-    work = cost(2 * tokens * chan * half * 3, 2 * chan * half * 3)
-    partner, xg, following = pl.pallas_call(
+    work = cost(2 * tokens * chan * half * 3, weights.size)
+    rows = weights_out.shape[0] // 2
+    half_out = pltpu.VMEM((rows, weights_out.shape[1]), weights_out.dtype)
+    weights_out = in_hbm(weights_out)
+    partner, xg, low = pl.pallas_call(
         partner_kernel,
         out_shape=(
             jax.ShapeDtypeStruct((tokens, 3 * chan + LANES), F32),
             jax.ShapeDtypeStruct((tokens, half), BF16),
-            pltpu.VMEM((NEXT, rows, half), weights.dtype),
+            half_out,
         ),
-        in_specs=[VMEM] * 7 + [ANY],
+        in_specs=[VMEM] * 6 + [ANY],
         out_specs=(VMEM,) * 3,
-        scratch_shapes=[
-            pltpu.VMEM((3 * CUTS - PRE - MORE, rows, half), weights.dtype),
-            pltpu.SemaphoreType.DMA((2, 3 * CUTS)),
-        ],
+        scratch_shapes=[pltpu.SemaphoreType.DMA],
         compiler_params=params(8),
         cost_estimate=work,
         name="project_partner",
-    )(*pieces, gain, in_vmem(pre), in_vmem(more), weights)
+    )(*pieces, gain, weights, weights_out)
     got = lax.ppermute(partner, "mdl", [(0, 1), (1, 0)])
-    own = pl.pallas_call(
+    own, high = pl.pallas_call(
         own_kernel,
-        out_shape=jax.ShapeDtypeStruct((tokens, 3 * chan), F32),
+        out_shape=(
+            jax.ShapeDtypeStruct((tokens, 3 * chan), F32),
+            half_out,
+        ),
         in_specs=[VMEM] * 2 + [ANY],
-        out_specs=VMEM,
-        scratch_shapes=[
-            pltpu.VMEM((3 * CUTS - NEXT, rows, half), weights.dtype),
-            pltpu.SemaphoreType.DMA((3 * CUTS,)),
-        ],
+        out_specs=(VMEM,) * 2,
+        scratch_shapes=[pltpu.SemaphoreType.DMA],
         compiler_params=params(8),
         cost_estimate=work,
         name="project_own",
-    )(xg, in_vmem(following), weights)
-    return own, got, partner, taps
+    )(xg, weights, weights_out)
+    return own, got, partner, taps, (in_vmem(low), in_vmem(high))
 
 
 def delay(x, rows):
@@ -321,37 +249,41 @@
     )(own, got, sent, jnp.transpose(short_taps, (1, 0, 2)), bias, taps)
 
 
-def out_kernel(first, piece_ref, w_ref, *refs):
+def out_kernel(piece_ref, low_ref, high_ref, *refs, first):
     out_ref = refs[-1]
     tokens, chan = out_ref.shape[0], piece_ref.shape[1]
-    total = refs[0][...] if len(refs) > 1 else None
-    for k in range(piece_ref.shape[0] // tokens):
-        owner = lax.axis_index("seq") ^ ORDER[first + k]
-        span = pl.ds(pl.multiple_of(owner * chan, chan), chan)
-        term = contract_last(piece_ref[k * tokens : (k + 1) * tokens, :], w_ref[:, span])
-        total = term if total is None else total + term
-    out_ref[...] = total
+    rows = low_ref.shape[0]
+    for at, w_ref in ((0, low_ref), (rows, high_ref)):
+        total = refs[0][:, at : at + rows] if len(refs) > 1 else None
+        for k in range(piece_ref.shape[0] // tokens):
+            owner = lax.axis_index("seq") ^ ORDER[first + k]
+            span = pl.ds(pl.multiple_of(owner * chan, chan), chan)
+            term = contract_last(piece_ref[k * tokens : (k + 1) * tokens, :], w_ref[:, span])
+            total = term if total is None else total + term
+        out_ref[:, at : at + rows] = total
 
 
 def add_kernel(a_ref, b_ref, out_ref):
     out_ref[...] = (a_ref[...] + b_ref[...]).astype(out_ref.dtype)
 
 
-def project_out(pieces, weights, tokens):
+def project_out(gated, low, high):
+    tokens, rows = gated.shape[0], low.shape[0]
+    pieces = gather_pieces(gated, gated)
     total, first = [], 0
     for piece in pieces:
         count = piece.shape[0] // tokens
-        width = count * piece.shape[1]
+        work = 2 * rows * count * piece.shape[1]
         total = [
             pl.pallas_call(
-                lambda *refs, first=first: out_kernel(first, *refs),
-                out_shape=jax.ShapeDtypeStruct((tokens, weights.shape[0]), F32),
-                in_specs=[VMEM] * (2 + len(total)),
+                functools.partial(out_kernel, first=first),
+                out_shape=jax.ShapeDtypeStruct((tokens, 2 * rows), F32),
+                in_specs=[VMEM] * (3 + len(total)),
                 out_specs=VMEM,
                 compiler_params=params(8),
-                cost_estimate=cost(2 * tokens * weights.shape[0] * width, 2 * weights.shape[0] * width),
+                cost_estimate=cost(2 * tokens * work, 2 * work),
                 name="project_out",
-            )(piece, weights, *total)
+            )(piece, low, high, *total)
         ]
         first += count
     return total[0]
@@ -362,11 +294,12 @@
     width = 2 * half
     tokens = own_tokens * lax.axis_size("seq")
     chan = in_proj.shape[2] // 2
-    weights_in = in_proj.reshape(3, 2 * chan, half)
     weights_out = out_proj.reshape(out_proj.shape[0], -1)
-    own, got, sent, taps = project(tokens_in, norm_gain[None, :], weights_in, long_taps, tokens)
+    own, got, sent, taps, loaded = project(
+        tokens_in, norm_gain[None, :], in_proj, weights_out, long_taps, tokens
+    )
     gated = mix(own, got, sent, short_taps, skip_bias[None, :], taps, width)
-    partial_out = project_out(gather_pieces(gated, gated), weights_out, tokens)
+    partial_out = project_out(gated, *loaded)
     other = lax.ppermute(partial_out, "mdl", [(0, 1), (1, 0)])
     return pl.pallas_call(
         add_kernel,

time: 39.9 us -> 38.9 us (0.975)
  Pallas kernels: 17.5 us -> 13 us
  waiting for transfers between devices: 8.07 us -> 11.7 us
    pallas_call x6 -> x5, Pallas kernels: 10.5 us -> 6.71 us  [the longest x1 3.84 us: project(): pl.pallas_call(own_kernel, out_shape=(jax.ShapeDtypeStruct((tokens, 3 * c...]
    ppermute x8, waiting for transfers between devices: 6.73 us -> 10.4 us  [swap(): return lax.ppermute(x, 'seq', [(i, i ^ bits) for i in range(count)])]
    pallas_call x1, Pallas kernels: 4.32 us -> 3.91 us  [project(): pl.pallas_call(partner_kernel, out_shape=(jax.ShapeDtypeStruct((tokens, 3...]
  transfers between devices with their start and end apart: 10 -> 10, of which waited for: 6 -> 7; matrix products, arithmetic and copies ran while one was open for 0% -> 0% of each run, Pallas kernels for 29% -> 19%
where the time goes in v3:
time: 38.9 us; the launch traced here: 38.7 us
  starting transfers between devices  13.9 us (36%)
  Pallas kernels  13 us (33%)
  waiting for transfers between devices  11.7 us (30%)
    ppermute x8, starting transfers between devices, swap(): return lax.ppermute(x, 'seq', [(i, i ^ bits) for i in range(count)])  13.7 us
    ppermute x8, waiting for transfers between devices, swap(): return lax.ppermute(x, 'seq', [(i, i ^ bits) for i in range(count)])  10.4 us
    pallas_call x1, Pallas kernels, project(): pl.pallas_call(partner_kernel, out_shape=(jax.ShapeDtypeStruct((tokens, 3...  3.91 us
    pallas_call x1, Pallas kernels, project(): pl.pallas_call(own_kernel, out_shape=(jax.ShapeDtypeStruct((tokens, 3 * c...  3.84 us
    pallas_call x4, Pallas kernels, project_out(): pl.pallas_call(functools.partial(out_kernel, first=first), out_shape=jax....  2.87 us
    ppermute x1, waiting for transfers between devices, per_device(): other = lax.ppermute(partial_out, 'mdl', [(0, 1), (1, 0)])  1.33 us
    pallas_call x1, Pallas kernels, prepare(): pl.pallas_call(prepare_kernel, out_shape=(jax.ShapeDtypeStruct(x.shape, x...  1.3 us
  transfers between devices with their start and end apart: 10, of which 7 were waited for; matrix products, arithmetic and copies ran while one was open for 0% of the time, Pallas kernels for 19%

profile of v3, /device:TPU:0, one launch (start us, length us, event | category | flops | bytes accessed | tf_op | source)
XLA Modules:
  0.0 38.7 jit_solution(15761466168693808560)
XLA Ops:
  0.0 2.9 %collective-permute-start = (bf16[4,4096]{1,0:T(4,128)(2,1)}, bf16[4,4096]{1,0:T(4,128)(2,1)S(1)}, u32[]{:S(2)}, u32[]{:S(2)}) collective-permute-start(bf16[4,4096]{1,0:T(4,128)(2,1)} %x_ref.1), channel_id=1, source_target_pairs={{0,2},{2,0},{4,6},{6,4},{8,10},{10,8},{12,14},{14,12},{1,3},{3,1},... | collective-permute-start | bytes 98312 | tf_op jit(solution)/shard_map/ppermute | solution.py:34
  2.9 1.3 %prepare.1 = (bf16[4,4096]{1,0:T(4,128)(2,1)S(1)}, f32[32,512]{1,0:T(8,128)S(1)}) custom-call(bf16[4,4096]{1,0:T(4,128)(2,1)} %x_ref.1, f32[512,128]{1,0:T(8,128)} %taps_ref.1), custom_call_target="tpu_custom_call" | custom-call | flops 12000000000 | bytes 4194304 | tf_op jit(solution)/shard_map/prepare/pallas_call | solution.py:102
  4.3 0.8 %collective-permute-done.refs_1_ = bf16[4,4096]{1,0:T(4,128)(2,1)S(1)} collective-permute-done((bf16[4,4096]{1,0:T(4,128)(2,1)}, bf16[4,4096]{1,0:T(4,128)(2,1)S(1)}, u32[]{:S(2)}, u32[]{:S(2)}) %collective-permute-start) | collective-permute-done | bytes 32800 | tf_op jit(solution)/shard_map/ppermute | solution.py:34
  5.1 4.2 %collective-permute-start.1 = (bf16[8,4096]{1,0:T(8,128)(2,1)S(1)}, bf16[8,4096]{1,0:T(8,128)(2,1)S(1)}, u32[]{:S(2)}, u32[]{:S(2)}) collective-permute-start(bf16[8,4096]{1,0:T(8,128)(2,1)S(1)} %stack.2.a_ref), channel_id=1, source_target_pairs={{0,12},{2,14},{4,8},{6,10},{8,4},{10,6},{12,0},{14,2},{1,13},{3,15... | collective-permute-start | bytes 196616 | tf_op jit(solution)/shard_map/ppermute | solution.py:34
  9.3 0.0 collective-permute-start.2
  9.3 0.6 %collective-permute-start.3 = (bf16[8,4096]{1,0:T(8,128)(2,1)S(1)}, bf16[8,4096]{1,0:T(8,128)(2,1)S(1)}, u32[]{:S(2)}, u32[]{:S(2)}) collective-permute-start(bf16[8,4096]{1,0:T(8,128)(2,1)S(1)} %stack.2.a_ref), channel_id=1, source_target_pairs={{0,4},{2,6},{4,0},{6,2},{8,12},{10,14},{12,8},{14,10},{1,5},{3,7},... | collective-permute-start | bytes 196616 | tf_op jit(solution)/shard_map/ppermute | solution.py:34
  9.9 1.8 %collective-permute-done.1.b_ref = bf16[8,4096]{1,0:T(8,128)(2,1)S(1)} collective-permute-done((bf16[8,4096]{1,0:T(8,128)(2,1)S(1)}, bf16[8,4096]{1,0:T(8,128)(2,1)S(1)}, u32[]{:S(2)}, u32[]{:S(2)}) %collective-permute-start.1) | collective-permute-done | bytes 65568 | tf_op jit(solution)/shard_map/ppermute | solution.py:34
  11.7 2.8 %collective-permute-done.2.c_ref = bf16[8,4096]{1,0:T(8,128)(2,1)S(1)} collective-permute-done((bf16[8,4096]{1,0:T(8,128)(2,1)S(1)}, bf16[8,4096]{1,0:T(8,128)(2,1)S(1)}, u32[]{:S(2)}, u32[]{:S(2)}) %collective-permute-start.2) | collective-permute-done | bytes 65568 | tf_op jit(solution)/shard_map/ppermute | solution.py:34
  14.5 0.0 collective-permute-done.3.d_ref
  14.5 0.0 copy-done.2
  14.5 3.9 %project_partner.1 = (f32[32,1664]{1,0:T(8,128)S(1)}, bf16[32,4096]{1,0:T(8,128)(2,1)S(1)}, bf16[512,4096]{1,0:T(8,128)(2,1)S(1)}) custom-call(bf16[8,4096]{1,0:T(8,128)(2,1)S(1)} %stack.2.a_ref, bf16[8,4096]{1,0:T(8,128)(2,1)S(1)} %collective-permute-done.1.b_ref, bf16[8,4096]{1,0:T(8,128)(2,1)S(1)} %collective-permute-done.2.c_ref, ...), custom_call_target="tpu_custom_call" | custom-call | flops 402653184 | bytes 12582912 | tf_op jit(solution)/shard_map/project_partner/pallas_call | solution.py:175
  18.4 0.1 collective-permute-start.4
  18.5 0.0 copy-start.1
  18.5 0.0 copy-start.3
  18.5 3.8 %project_own.1 = (f32[32,1536]{1,0:T(8,128)S(1)}, bf16[512,4096]{1,0:T(8,128)(2,1)S(1)}) custom-call(bf16[32,4096]{1,0:T(8,128)(2,1)S(1)} %get-tuple-element.13.xg_ref, bf16[1,3,1024,4096]{3,2,1,0:T(8,128)(2,1)S(1)} %copy-done, bf16[1024,4096]{1,0:T(8,128)(2,1)} %bitcast.8), custom_call_target="tpu_custom_call" | custom-call | flops 402653184 | bytes 12582912 | tf_op jit(solution)/shard_map/project_own/pallas_call | solution.py:190
  22.3 0.0 collective-permute-done.4.refs_1_
  22.4 0.4 %mix.1.refs_0_ = bf16[32,512]{1,0:T(8,128)(2,1)S(1)} custom-call(f32[32,1536]{1,0:T(8,128)S(1)} %get-tuple-element.14.refs_0_, f32[32,1664]{1,0:T(8,128)S(1)} %collective-permute-done.4.refs_1_, f32[32,1664]{1,0:T(8,128)S(1)} %get-tuple-element.15.refs_2_, f32[3,7,1024]{2,1,0:T(8,128)S(1)} %bitcast.4, f32[1,1024]{1,0:T(1,128)S(1)} %bitcast.6, ...), custom_call_target="tpu_custom_call" | custom-call | tf_op jit(solution)/shard_map/mix/pallas_call | solution.py:242
  22.8 1.6 %collective-permute-start.5 = (bf16[32,512]{1,0:T(8,128)(2,1)S(1)}, bf16[32,512]{1,0:T(8,128)(2,1)S(1)}, u32[]{:S(2)}, u32[]{:S(2)}) collective-permute-start(bf16[32,512]{1,0:T(8,128)(2,1)S(1)} %mix.1.refs_0_), channel_id=1, source_target_pairs={{0,2},{2,0},{4,6},{6,4},{8,10},{10,8},{12,14},{14,12},{1,3},{3,1},... | collective-permute-start | bytes 98312 | tf_op jit(solution)/shard_map/ppermute | solution.py:34
  24.3 2.4 %collective-permute-done.5.refs_1_ = bf16[32,512]{1,0:T(8,128)(2,1)S(1)} collective-permute-done((bf16[32,512]{1,0:T(8,128)(2,1)S(1)}, bf16[32,512]{1,0:T(8,128)(2,1)S(1)}, u32[]{:S(2)}, u32[]{:S(2)}) %collective-permute-start.5) | collective-permute-done | bytes 32800 | tf_op jit(solution)/shard_map/ppermute | solution.py:34
  26.8 2.1 %collective-permute-start.8 = (bf16[64,512]{1,0:T(8,128)(2,1)S(1)}, bf16[64,512]{1,0:T(8,128)(2,1)S(1)}, u32[]{:S(2)}, u32[]{:S(2)}) collective-permute-start(bf16[64,512]{1,0:T(8,128)(2,1)S(1)} %stack.3.piece_ref), channel_id=1, source_target_pairs={{0,12},{2,14},{4,8},{6,10},{8,4},{10,6},{12,0},{14,2},{1,13},{3,15... | collective-permute-start | bytes 196616 | tf_op jit(solution)/shard_map/ppermute | solution.py:34
  28.9 0.0 collective-permute-start.7
  28.9 2.3 %collective-permute-start.6 = (bf16[64,512]{1,0:T(8,128)(2,1)S(1)}, bf16[64,512]{1,0:T(8,128)(2,1)S(1)}, u32[]{:S(2)}, u32[]{:S(2)}) collective-permute-start(bf16[64,512]{1,0:T(8,128)(2,1)S(1)} %stack.3.piece_ref), channel_id=1, source_target_pairs={{0,4},{2,6},{4,0},{6,2},{8,12},{10,14},{12,8},{14,10},{1,5},{3,7},... | collective-permute-start | bytes 196616 | tf_op jit(solution)/shard_map/ppermute | solution.py:34
  31.2 0.7 %project_out.4.refs_0_ = f32[32,1024]{1,0:T(8,128)S(1)} custom-call(bf16[64,512]{1,0:T(8,128)(2,1)S(1)} %stack.3.piece_ref, bf16[512,4096]{1,0:T(8,128)(2,1)S(1)} %get-tuple-element.17.low_ref, bf16[512,4096]{1,0:T(8,128)(2,1)S(1)} %get-tuple-element.18.high_ref), custom_call_target="tpu_custom_call" | custom-call | flops 67108864 | bytes 2097152 | tf_op jit(solution)/shard_map/project_out/pallas_call | solution.py:278
  31.9 1.3 %collective-permute-done.8.piece_ref = bf16[64,512]{1,0:T(8,128)(2,1)S(1)} collective-permute-done((bf16[64,512]{1,0:T(8,128)(2,1)S(1)}, bf16[64,512]{1,0:T(8,128)(2,1)S(1)}, u32[]{:S(2)}, u32[]{:S(2)}) %collective-permute-start.8) | collective-permute-done | bytes 65568 | tf_op jit(solution)/shard_map/ppermute | solution.py:34
  33.2 0.7 %project_out.5.refs_0_ = f32[32,1024]{1,0:T(8,128)S(1)} custom-call(bf16[64,512]{1,0:T(8,128)(2,1)S(1)} %collective-permute-done.8.piece_ref, bf16[512,4096]{1,0:T(8,128)(2,1)S(1)} %get-tuple-element.17.low_ref, bf16[512,4096]{1,0:T(8,128)(2,1)S(1)} %get-tuple-element.18.high_ref, f32[32,1024]{1,0:T(8,128)S(1)} %project_out.4.refs_0_), custom_call_target="tpu_custom_call" | custom-call | flops 67108864 | bytes 2097152 | tf_op jit(solution)/shard_map/project_out/pallas_call | solution.py:278
  33.9 1.3 %collective-permute-done.7.piece_ref = bf16[64,512]{1,0:T(8,128)(2,1)S(1)} collective-permute-done((bf16[64,512]{1,0:T(8,128)(2,1)S(1)}, bf16[64,512]{1,0:T(8,128)(2,1)S(1)}, u32[]{:S(2)}, u32[]{:S(2)}) %collective-permute-start.7) | collective-permute-done | bytes 65568 | tf_op jit(solution)/shard_map/ppermute | solution.py:34
  35.2 0.7 %project_out.6.refs_0_ = f32[32,1024]{1,0:T(8,128)S(1)} custom-call(bf16[64,512]{1,0:T(8,128)(2,1)S(1)} %collective-permute-done.7.piece_ref, bf16[512,4096]{1,0:T(8,128)(2,1)S(1)} %get-tuple-element.17.low_ref, bf16[512,4096]{1,0:T(8,128)(2,1)S(1)} %get-tuple-element.18.high_ref, f32[32,1024]{1,0:T(8,128)S(1)} %project_out.5.refs_0_), custom_call_target="tpu_custom_call" | custom-call | flops 67108864 | bytes 2097152 | tf_op jit(solution)/shard_map/project_out/pallas_call | solution.py:278
  35.9 0.0 collective-permute-done.6.piece_ref
  36.0 0.7 %project_out.7.a_ref = f32[32,1024]{1,0:T(8,128)S(1)} custom-call(bf16[64,512]{1,0:T(8,128)(2,1)S(1)} %collective-permute-done.6.piece_ref, bf16[512,4096]{1,0:T(8,128)(2,1)S(1)} %get-tuple-element.17.low_ref, bf16[512,4096]{1,0:T(8,128)(2,1)S(1)} %get-tuple-element.18.high_ref, f32[32,1024]{1,0:T(8,128)S(1)} %project_out.6.refs_0_), custom_call_target="tpu_custom_call" | custom-call | flops 67108864 | bytes 2097152 | tf_op jit(solution)/shard_map/project_out/pallas_call | solution.py:278
  36.7 0.1 collective-permute-start.9
  36.8 1.3 %collective-permute-done.9.b_ref = f32[32,1024]{1,0:T(8,128)S(1)} collective-permute-done((f32[32,1024]{1,0:T(8,128)S(1)}, f32[32,1024]{1,0:T(8,128)S(1)}, u32[]{:S(2)}, u32[]{:S(2)}) %collective-permute-start.9) | collective-permute-done | bytes 131104 | tf_op jit(solution)/shard_map/ppermute | solution.py:303
  38.1 0.6 %add.1 = bf16[32,1024]{1,0:T(8,128)(2,1)} custom-call(f32[32,1024]{1,0:T(8,128)S(1)} %project_out.7.a_ref, f32[32,1024]{1,0:T(8,128)S(1)} %collective-permute-done.9.b_ref), custom_call_target="tpu_custom_call" | custom-call | tf_op jit(solution)/shard_map/add/pallas_call | solution.py:304
  (7 shorter events, 0.0 us)
Async XLA Ops:
  0.0 14.5 %copy-start.2 = (f32[4096]{0:T(1024)S(1)}, f32[4096]{0:T(1024)}, u32[]{:S(2)}) copy-start(f32[4096]{0:T(1024)} %param.8) | copy-start | bytes 49156
  0.0 5.0 %collective-permute-start = (bf16[4,4096]{1,0:T(4,128)(2,1)}, bf16[4,4096]{1,0:T(4,128)(2,1)S(1)}, u32[]{:S(2)}, u32[]{:S(2)}) collective-permute-start(bf16[4,4096]{1,0:T(4,128)(2,1)} %x_ref.1), channel_id=1, source_target_pairs={{0,2},{2,0},{4,6},{6,4},{8,10},{10,8},{12,14},{14,12},{1,3},{3,1},... | collective-permute-start | bytes 98312 | tf_op jit(solution)/shard_map/ppermute | solution.py:34
  2.9 11.5 %copy-start = (bf16[1,3,1024,4096]{3,2,1,0:T(8,128)(2,1)S(1)}, bf16[1,3,1024,4096]{3,2,1,0:T(8,128)(2,1)}, u32[]{:S(2)}) copy-start(bf16[1,3,1024,4096]{3,2,1,0:T(8,128)(2,1)} %w_ref.3) | copy-start | bytes 75497472
  5.1 6.6 %collective-permute-start.1 = (bf16[8,4096]{1,0:T(8,128)(2,1)S(1)}, bf16[8,4096]{1,0:T(8,128)(2,1)S(1)}, u32[]{:S(2)}, u32[]{:S(2)}) collective-permute-start(bf16[8,4096]{1,0:T(8,128)(2,1)S(1)} %stack.2.a_ref), channel_id=1, source_target_pairs={{0,12},{2,14},{4,8},{6,10},{8,4},{10,6},{12,0},{14,2},{1,13},{3,15... | collective-permute-start | bytes 196616 | tf_op jit(solution)/shard_map/ppermute | solution.py:34
  9.3 5.2 %collective-permute-start.2 = (bf16[8,4096]{1,0:T(8,128)(2,1)S(1)}, bf16[8,4096]{1,0:T(8,128)(2,1)S(1)}, u32[]{:S(2)}, u32[]{:S(2)}) collective-permute-start(bf16[8,4096]{1,0:T(8,128)(2,1)S(1)} %stack.2.a_ref), channel_id=1, source_target_pairs={{0,8},{2,10},{4,12},{6,14},{8,0},{10,2},{12,4},{14,6},{1,9},{3,11}... | collective-permute-start | bytes 196616 | tf_op jit(solution)/shard_map/ppermute | solution.py:34
  9.3 5.2 %collective-permute-start.3 = (bf16[8,4096]{1,0:T(8,128)(2,1)S(1)}, bf16[8,4096]{1,0:T(8,128)(2,1)S(1)}, u32[]{:S(2)}, u32[]{:S(2)}) collective-permute-start(bf16[8,4096]{1,0:T(8,128)(2,1)S(1)} %stack.2.a_ref), channel_id=1, source_target_pairs={{0,4},{2,6},{4,0},{6,2},{8,12},{10,14},{12,8},{14,10},{1,5},{3,7},... | collective-permute-start | bytes 196616 | tf_op jit(solution)/shard_map/ppermute | solution.py:34
  18.4 4.0 %collective-permute-start.4 = (f32[32,1664]{1,0:T(8,128)S(1)}, f32[32,1664]{1,0:T(8,128)S(1)}, u32[]{:S(2)}, u32[]{:S(2)}) collective-permute-start(f32[32,1664]{1,0:T(8,128)S(1)} %get-tuple-element.15.refs_2_), channel_id=1, source_target_pairs={{0,1},{1,0},{2,3},{3,2},{4,5},{5,4},{6,7},{7,6},{8,9},{9,8},{10,11... | collective-permute-start | bytes 638984 | tf_op jit(solution)/shard_map/ppermute | solution.py:189
  18.5 3.9 %copy-start.1 = (f32[7,3,1024]{2,0,1:T(8,128)S(1)}, f32[7,3,1024]{2,0,1:T(8,128)}, u32[]{:S(2)}) copy-start(f32[7,3,1024]{2,0,1:T(8,128)} %param.10) | copy-start | bytes 258052
  18.5 3.9 %copy-start.3 = (f32[1024]{0:T(1024)S(1)}, f32[1024]{0:T(1024)}, u32[]{:S(2)}) copy-start(f32[1024]{0:T(1024)} %param.12) | copy-start | bytes 12292
  22.8 4.0 %collective-permute-start.5 = (bf16[32,512]{1,0:T(8,128)(2,1)S(1)}, bf16[32,512]{1,0:T(8,128)(2,1)S(1)}, u32[]{:S(2)}, u32[]{:S(2)}) collective-permute-start(bf16[32,512]{1,0:T(8,128)(2,1)S(1)} %mix.1.refs_0_), channel_id=1, source_target_pairs={{0,2},{2,0},{4,6},{6,4},{8,10},{10,8},{12,14},{14,12},{1,3},{3,1},... | collective-permute-start | bytes 98312 | tf_op jit(solution)/shard_map/ppermute | solution.py:34
  26.8 6.4 %collective-permute-start.8 = (bf16[64,512]{1,0:T(8,128)(2,1)S(1)}, bf16[64,512]{1,0:T(8,128)(2,1)S(1)}, u32[]{:S(2)}, u32[]{:S(2)}) collective-permute-start(bf16[64,512]{1,0:T(8,128)(2,1)S(1)} %stack.3.piece_ref), channel_id=1, source_target_pairs={{0,12},{2,14},{4,8},{6,10},{8,4},{10,6},{12,0},{14,2},{1,13},{3,15... | collective-permute-start | bytes 196616 | tf_op jit(solution)/shard_map/ppermute | solution.py:34
  28.9 6.4 %collective-permute-start.7 = (bf16[64,512]{1,0:T(8,128)(2,1)S(1)}, bf16[64,512]{1,0:T(8,128)(2,1)S(1)}, u32[]{:S(2)}, u32[]{:S(2)}) collective-permute-start(bf16[64,512]{1,0:T(8,128)(2,1)S(1)} %stack.3.piece_ref), channel_id=1, source_target_pairs={{0,8},{2,10},{4,12},{6,14},{8,0},{10,2},{12,4},{14,6},{1,9},{3,11}... | collective-permute-start | bytes 196616 | tf_op jit(solution)/shard_map/ppermute | solution.py:34
  28.9 7.1 %collective-permute-start.6 = (bf16[64,512]{1,0:T(8,128)(2,1)S(1)}, bf16[64,512]{1,0:T(8,128)(2,1)S(1)}, u32[]{:S(2)}, u32[]{:S(2)}) collective-permute-start(bf16[64,512]{1,0:T(8,128)(2,1)S(1)} %stack.3.piece_ref), channel_id=1, source_target_pairs={{0,4},{2,6},{4,0},{6,2},{8,12},{10,14},{12,8},{14,10},{1,5},{3,7},... | collective-permute-start | bytes 196616 | tf_op jit(solution)/shard_map/ppermute | solution.py:34
  36.7 1.4 %collective-permute-start.9 = (f32[32,1024]{1,0:T(8,128)S(1)}, f32[32,1024]{1,0:T(8,128)S(1)}, u32[]{:S(2)}, u32[]{:S(2)}) collective-permute-start(f32[32,1024]{1,0:T(8,128)S(1)} %project_out.7.a_ref), channel_id=1, source_target_pairs={{0,1},{1,0},{2,3},{3,2},{4,5},{5,4},{6,7},{7,6},{8,9},{9,8},{10,11... | collective-permute-start | bytes 393224 | tf_op jit(solution)/shard_map/ppermute | solution.py:303

commit v4 on v3

--- a/solution.py
+++ b/solution.py
@@ -51,13 +51,15 @@
     )(*parts)
 
 
-ORDER = (0, 1, 6, 7, 4, 5, 2, 3)
-
-
-def gather_pieces(x, local):
+def gather_tokens(x, local):
     pair = stack(local, swap(x, 1))
-    far, mid, near = [swap(pair, bits) for bits in (6, 4, 2)]
-    return [pair, far, mid, near]
+    return [pair] + [swap(pair, b) for b in (6, 4, 2)], (0, 1, 6, 7, 4, 5, 2, 3)
+
+
+def gather_groups(x):
+    far, mid, close = [swap(x, b) for b in (6, 4, 2)]
+    one, two = stack(x, far), stack(mid, close)
+    return [([one, two], (0, 6, 4, 2)), ([swap(one, 1)], (1, 7)), ([swap(two, 1)], (5, 3))]
 
 
 def in_vmem(x):
@@ -131,14 +133,13 @@
     return jnp.dot(jnp.where(hit, 1.0, 0.0).astype(BF16), raw, preferred_element_type=F32)
 
 
-def partner_kernel(
-    a_ref, b_ref, c_ref, d_ref, gain_ref, w_ref, wo_ref, out_ref, xg_ref, load_ref, sem
-):
+def partner_kernel(*refs, owners):
+    pieces, (gain_ref, w_ref, wo_ref, out_ref, xg_ref, load_ref, sem) = refs[:-7], refs[-7:]
     load = pltpu.make_async_copy(wo_ref.at[pl.ds(0, load_ref.shape[0])], load_ref, sem)
     load.start()
     tokens = out_ref.shape[0]
     chan = w_ref.shape[2] // 2
-    values = ordered((a_ref, b_ref, c_ref, d_ref), ORDER, tokens)
+    values = ordered(pieces, owners, tokens)
     squares = jnp.sum(values * values, axis=1, keepdims=True)
     out_ref[:, 3 * chan :] = jnp.broadcast_to(squares, (tokens, LANES))
     xg_ref[...] = (values * gain_ref[...]).astype(BF16)
@@ -167,19 +168,19 @@
     chan = weights.shape[2] // 2
     half = weights.shape[3]
     local, taps = prepare(tokens_in, long_taps, tokens, chan)
-    pieces = gather_pieces(tokens_in, local)
+    pieces, owners = gather_tokens(tokens_in, local)
     work = cost(2 * tokens * chan * half * 3, weights.size)
     rows = weights_out.shape[0] // 2
     half_out = pltpu.VMEM((rows, weights_out.shape[1]), weights_out.dtype)
     weights_out = in_hbm(weights_out)
     partner, xg, low = pl.pallas_call(
-        partner_kernel,
+        functools.partial(partner_kernel, owners=owners),
         out_shape=(
             jax.ShapeDtypeStruct((tokens, 3 * chan + LANES), F32),
             jax.ShapeDtypeStruct((tokens, half), BF16),
             half_out,
         ),
-        in_specs=[VMEM] * 6 + [ANY],
+        in_specs=[VMEM] * (2 + len(pieces)) + [ANY],
         out_specs=(VMEM,) * 3,
         scratch_shapes=[pltpu.SemaphoreType.DMA],
         compiler_params=params(8),
@@ -249,16 +250,17 @@
     )(own, got, sent, jnp.transpose(short_taps, (1, 0, 2)), bias, taps)
 
 
-def out_kernel(piece_ref, low_ref, high_ref, *refs, first):
-    out_ref = refs[-1]
-    tokens, chan = out_ref.shape[0], piece_ref.shape[1]
+def out_kernel(*refs, count, owners):
+    pieces, (low_ref, high_ref, *acc, out_ref) = refs[:count], refs[count:]
+    tokens, chan = out_ref.shape[0], pieces[0].shape[1]
     rows = low_ref.shape[0]
+    shards = [ref[i : i + tokens, :] for ref in pieces for i in range(0, ref.shape[0], tokens)]
     for at, w_ref in ((0, low_ref), (rows, high_ref)):
-        total = refs[0][:, at : at + rows] if len(refs) > 1 else None
-        for k in range(piece_ref.shape[0] // tokens):
-            owner = lax.axis_index("seq") ^ ORDER[first + k]
+        total = acc[0][:, at : at + rows] if acc else None
+        for shard, bits in zip(shards, owners, strict=True):
+            owner = lax.axis_index("seq") ^ bits
             span = pl.ds(pl.multiple_of(owner * chan, chan), chan)
-            term = contract_last(piece_ref[k * tokens : (k + 1) * tokens, :], w_ref[:, span])
+            term = contract_last(shard, w_ref[:, span])
             total = term if total is None else total + term
         out_ref[:, at : at + rows] = total
 
@@ -269,23 +271,20 @@
 
 def project_out(gated, low, high):
     tokens, rows = gated.shape[0], low.shape[0]
-    pieces = gather_pieces(gated, gated)
-    total, first = [], 0
-    for piece in pieces:
-        count = piece.shape[0] // tokens
-        work = 2 * rows * count * piece.shape[1]
+    total = []
+    for pieces, owners in gather_groups(gated):
+        work = 2 * rows * len(owners) * gated.shape[1]
         total = [
             pl.pallas_call(
-                functools.partial(out_kernel, first=first),
+                functools.partial(out_kernel, count=len(pieces), owners=owners),
                 out_shape=jax.ShapeDtypeStruct((tokens, 2 * rows), F32),
-                in_specs=[VMEM] * (3 + len(total)),
+                in_specs=[VMEM] * (len(pieces) + 2 + len(total)),
                 out_specs=VMEM,
                 compiler_params=params(8),
                 cost_estimate=cost(2 * tokens * work, 2 * work),
                 name="project_out",
-            )(piece, low, high, *total)
+            )(*pieces, low, high, *total)
         ]
-        first += count
     return total[0]
 
 

time: 38.9 us -> 37.3 us (0.959)
  waiting for transfers between devices: 11.7 us -> 8.87 us
  starting transfers between devices: 13.9 us -> 15.3 us
    ppermute x8 -> x9, waiting for transfers between devices: 10.4 us -> 7.53 us  [swap(): return lax.ppermute(x, 'seq', [(i, i ^ bits) for i in range(count)])]
    ppermute x8 -> x9, starting transfers between devices: 13.7 us -> 15.2 us  [swap(): return lax.ppermute(x, 'seq', [(i, i ^ bits) for i in range(count)])]
    pallas_call x5 -> x4, Pallas kernels: 6.78 us -> 6.67 us  [the longest x1 3.91 us: project(): pl.pallas_call(functools.partial(partner_kernel, owners=owners), out_shap...]
  transfers between devices with their start and end apart: 10 -> 11, of which waited for: 7 -> 7; matrix products, arithmetic and copies ran while one was open for 0% -> 0% of each run, Pallas kernels for 19% -> 19%
where the time goes in v4:
time: 37.3 us; the launch traced here: 37.2 us
  starting transfers between devices  15.3 us (41%)
  Pallas kernels  12.9 us (35%)
  waiting for transfers between devices  8.87 us (24%)
    ppermute x9, starting transfers between devices, swap(): return lax.ppermute(x, 'seq', [(i, i ^ bits) for i in range(count)])  15.2 us
    ppermute x9, waiting for transfers between devices, swap(): return lax.ppermute(x, 'seq', [(i, i ^ bits) for i in range(count)])  7.53 us
    pallas_call x1, Pallas kernels, project(): pl.pallas_call(functools.partial(partner_kernel, owners=owners), out_shap...  3.91 us
    pallas_call x1, Pallas kernels, project(): pl.pallas_call(own_kernel, out_shape=(jax.ShapeDtypeStruct((tokens, 3 * c...  3.84 us
    pallas_call x3, Pallas kernels, project_out(): pl.pallas_call(functools.partial(out_kernel, count=len(pieces), owners=ow...  2.76 us
    ppermute x1, waiting for transfers between devices, per_device(): other = lax.ppermute(partial_out, 'mdl', [(0, 1), (1, 0)])  1.33 us
    pallas_call x1, Pallas kernels, prepare(): pl.pallas_call(prepare_kernel, out_shape=(jax.ShapeDtypeStruct(x.shape, x...  1.3 us
  transfers between devices with their start and end apart: 11, of which 7 were waited for; matrix products, arithmetic and copies ran while one was open for 0% of the time, Pallas kernels for 19%

profile of v4, /device:TPU:0, one launch (start us, length us, event | category | flops | bytes accessed | tf_op | source)
XLA Modules:
  0.0 37.2 jit_solution(17159469188259845405)
XLA Ops:
  0.0 2.9 %collective-permute-start = (bf16[4,4096]{1,0:T(4,128)(2,1)}, bf16[4,4096]{1,0:T(4,128)(2,1)S(1)}, u32[]{:S(2)}, u32[]{:S(2)}) collective-permute-start(bf16[4,4096]{1,0:T(4,128)(2,1)} %x_ref.1), channel_id=1, source_target_pairs={{0,2},{2,0},{4,6},{6,4},{8,10},{10,8},{12,14},{14,12},{1,3},{3,1},... | collective-permute-start | bytes 98312 | tf_op jit(solution)/shard_map/ppermute | solution.py:34
  2.9 1.3 %prepare.1 = (bf16[4,4096]{1,0:T(4,128)(2,1)S(1)}, f32[32,512]{1,0:T(8,128)S(1)}) custom-call(bf16[4,4096]{1,0:T(4,128)(2,1)} %x_ref.1, f32[512,128]{1,0:T(8,128)} %taps_ref.1), custom_call_target="tpu_custom_call" | custom-call | flops 12000000000 | bytes 4194304 | tf_op jit(solution)/shard_map/prepare/pallas_call | solution.py:104
  4.3 0.8 %collective-permute-done.refs_1_ = bf16[4,4096]{1,0:T(4,128)(2,1)S(1)} collective-permute-done((bf16[4,4096]{1,0:T(4,128)(2,1)}, bf16[4,4096]{1,0:T(4,128)(2,1)S(1)}, u32[]{:S(2)}, u32[]{:S(2)}) %collective-permute-start) | collective-permute-done | bytes 32800 | tf_op jit(solution)/shard_map/ppermute | solution.py:34
  5.1 4.2 %collective-permute-start.1 = (bf16[8,4096]{1,0:T(8,128)(2,1)S(1)}, bf16[8,4096]{1,0:T(8,128)(2,1)S(1)}, u32[]{:S(2)}, u32[]{:S(2)}) collective-permute-start(bf16[8,4096]{1,0:T(8,128)(2,1)S(1)} %stack.3.refs_0_), channel_id=1, source_target_pairs={{0,12},{2,14},{4,8},{6,10},{8,4},{10,6},{12,0},{14,2},{1,13},{3,15... | collective-permute-start | bytes 196616 | tf_op jit(solution)/shard_map/ppermute | solution.py:34
  9.3 0.0 collective-permute-start.2
  9.3 0.6 %collective-permute-start.3 = (bf16[8,4096]{1,0:T(8,128)(2,1)S(1)}, bf16[8,4096]{1,0:T(8,128)(2,1)S(1)}, u32[]{:S(2)}, u32[]{:S(2)}) collective-permute-start(bf16[8,4096]{1,0:T(8,128)(2,1)S(1)} %stack.3.refs_0_), channel_id=1, source_target_pairs={{0,4},{2,6},{4,0},{6,2},{8,12},{10,14},{12,8},{14,10},{1,5},{3,7},... | collective-permute-start | bytes 196616 | tf_op jit(solution)/shard_map/ppermute | solution.py:34
  9.9 1.8 %collective-permute-done.1.refs_1_ = bf16[8,4096]{1,0:T(8,128)(2,1)S(1)} collective-permute-done((bf16[8,4096]{1,0:T(8,128)(2,1)S(1)}, bf16[8,4096]{1,0:T(8,128)(2,1)S(1)}, u32[]{:S(2)}, u32[]{:S(2)}) %collective-permute-start.1) | collective-permute-done | bytes 65568 | tf_op jit(solution)/shard_map/ppermute | solution.py:34
  11.7 2.8 %collective-permute-done.2.refs_2_ = bf16[8,4096]{1,0:T(8,128)(2,1)S(1)} collective-permute-done((bf16[8,4096]{1,0:T(8,128)(2,1)S(1)}, bf16[8,4096]{1,0:T(8,128)(2,1)S(1)}, u32[]{:S(2)}, u32[]{:S(2)}) %collective-permute-start.2) | collective-permute-done | bytes 65568 | tf_op jit(solution)/shard_map/ppermute | solution.py:34
  14.5 0.0 collective-permute-done.3.refs_3_
  14.5 3.9 %project_partner.1 = (f32[32,1664]{1,0:T(8,128)S(1)}, bf16[32,4096]{1,0:T(8,128)(2,1)S(1)}, bf16[512,4096]{1,0:T(8,128)(2,1)S(1)}) custom-call(bf16[8,4096]{1,0:T(8,128)(2,1)S(1)} %stack.3.refs_0_, bf16[8,4096]{1,0:T(8,128)(2,1)S(1)} %collective-permute-done.1.refs_1_, bf16[8,4096]{1,0:T(8,128)(2,1)S(1)} %collective-permute-done.2.refs_2_, ...), custom_call_target="tpu_custom_call" | custom-call | flops 402653184 | bytes 12582912 | tf_op jit(solution)/shard_map/project_partner/pallas_call | solution.py:176
  18.4 0.1 collective-permute-start.4
  18.5 0.0 copy-start.1
  18.5 0.0 copy-start.3
  18.5 3.8 %project_own.1 = (f32[32,1536]{1,0:T(8,128)S(1)}, bf16[512,4096]{1,0:T(8,128)(2,1)S(1)}) custom-call(bf16[32,4096]{1,0:T(8,128)(2,1)S(1)} %get-tuple-element.13.xg_ref, bf16[1,3,1024,4096]{3,2,1,0:T(8,128)(2,1)S(1)} %copy-done, bf16[1024,4096]{1,0:T(8,128)(2,1)} %bitcast.8), custom_call_target="tpu_custom_call" | custom-call | flops 402653184 | bytes 12582912 | tf_op jit(solution)/shard_map/project_own/pallas_call | solution.py:191
  22.3 0.0 collective-permute-done.4.refs_1_
  22.4 0.4 %mix.1.refs_0_ = bf16[32,512]{1,0:T(8,128)(2,1)S(1)} custom-call(f32[32,1536]{1,0:T(8,128)S(1)} %get-tuple-element.14.refs_0_, f32[32,1664]{1,0:T(8,128)S(1)} %collective-permute-done.4.refs_1_, f32[32,1664]{1,0:T(8,128)S(1)} %get-tuple-element.15.refs_2_, f32[3,7,1024]{2,1,0:T(8,128)S(1)} %bitcast.4, f32[1,1024]{1,0:T(1,128)S(1)} %bitcast.6, ...), custom_call_target="tpu_custom_call" | custom-call | tf_op jit(solution)/shard_map/mix/pallas_call | solution.py:243
  22.8 2.2 %collective-permute-start.8 = (bf16[32,512]{1,0:T(8,128)(2,1)S(1)}, bf16[32,512]{1,0:T(8,128)(2,1)S(1)}, u32[]{:S(2)}, u32[]{:S(2)}) collective-permute-start(bf16[32,512]{1,0:T(8,128)(2,1)S(1)} %mix.1.refs_0_), channel_id=1, source_target_pairs={{0,12},{2,14},{4,8},{6,10},{8,4},{10,6},{12,0},{14,2},{1,13},{3,15... | collective-permute-start | bytes 98312 | tf_op jit(solution)/shard_map/ppermute | solution.py:34
  24.9 0.0 collective-permute-start.5
  24.9 2.3 %collective-permute-start.6 = (bf16[32,512]{1,0:T(8,128)(2,1)S(1)}, bf16[32,512]{1,0:T(8,128)(2,1)S(1)}, u32[]{:S(2)}, u32[]{:S(2)}) collective-permute-start(bf16[32,512]{1,0:T(8,128)(2,1)S(1)} %mix.1.refs_0_), channel_id=1, source_target_pairs={{0,4},{2,6},{4,0},{6,2},{8,12},{10,14},{12,8},{14,10},{1,5},{3,7},... | collective-permute-start | bytes 98312 | tf_op jit(solution)/shard_map/ppermute | solution.py:34
  27.2 1.4 %collective-permute-done.8.refs_1_ = bf16[32,512]{1,0:T(8,128)(2,1)S(1)} collective-permute-done((bf16[32,512]{1,0:T(8,128)(2,1)S(1)}, bf16[32,512]{1,0:T(8,128)(2,1)S(1)}, u32[]{:S(2)}, u32[]{:S(2)}) %collective-permute-start.8) | collective-permute-done | bytes 32800 | tf_op jit(solution)/shard_map/ppermute | solution.py:34
  28.6 1.5 %collective-permute-start.9 = (bf16[64,512]{1,0:T(8,128)(2,1)S(1)}, bf16[64,512]{1,0:T(8,128)(2,1)S(1)}, u32[]{:S(2)}, u32[]{:S(2)}) collective-permute-start(bf16[64,512]{1,0:T(8,128)(2,1)S(1)} %stack.5.refs_0_), channel_id=1, source_target_pairs={{0,2},{2,0},{4,6},{6,4},{8,10},{10,8},{12,14},{14,12},{1,3},{3,1},... | collective-permute-start | bytes 196616 | tf_op jit(solution)/shard_map/ppermute | solution.py:34
  30.1 0.0 collective-permute-done.5.refs_0_
  30.1 0.0 collective-permute-done.6.refs_1_
  30.1 1.5 %collective-permute-start.7 = (bf16[64,512]{1,0:T(8,128)(2,1)S(1)}, bf16[64,512]{1,0:T(8,128)(2,1)S(1)}, u32[]{:S(2)}, u32[]{:S(2)}) collective-permute-start(bf16[64,512]{1,0:T(8,128)(2,1)S(1)} %stack.4.refs_1_), channel_id=1, source_target_pairs={{0,2},{2,0},{4,6},{6,4},{8,10},{10,8},{12,14},{14,12},{1,3},{3,1},... | collective-permute-start | bytes 196616 | tf_op jit(solution)/shard_map/ppermute | solution.py:34
  31.6 1.3 %project_out.3.refs_3_ = f32[32,1024]{1,0:T(8,128)S(1)} custom-call(bf16[64,512]{1,0:T(8,128)(2,1)S(1)} %stack.5.refs_0_, bf16[64,512]{1,0:T(8,128)(2,1)S(1)} %stack.4.refs_1_, bf16[512,4096]{1,0:T(8,128)(2,1)S(1)} %get-tuple-element.17.refs_2_.refs_1_, bf16[512,4096]{1,0:T(8,128)(2,1)S(1)} %get-tuple-element.18.refs_3_.refs_2_), custom_call_target="tpu_custom_call" | custom-call | flops 134217728 | bytes 4194304 | tf_op jit(solution)/shard_map/project_out/pallas_call | solution.py:278
  32.9 0.3 collective-permute-done.9.refs_0_
  33.2 0.7 %project_out.4.refs_3_ = f32[32,1024]{1,0:T(8,128)S(1)} custom-call(bf16[64,512]{1,0:T(8,128)(2,1)S(1)} %collective-permute-done.9.refs_0_, bf16[512,4096]{1,0:T(8,128)(2,1)S(1)} %get-tuple-element.17.refs_2_.refs_1_, bf16[512,4096]{1,0:T(8,128)(2,1)S(1)} %get-tuple-element.18.refs_3_.refs_2_, f32[32,1024]{1,0:T(8,128)S(1)} %project_out.3.refs_3_), custom_call_target="tpu_custom_call" | custom-call | flops 67108864 | bytes 2097152 | tf_op jit(solution)/shard_map/project_out/pallas_call | solution.py:278
  33.9 0.5 %collective-permute-done.7.refs_0_ = bf16[64,512]{1,0:T(8,128)(2,1)S(1)} collective-permute-done((bf16[64,512]{1,0:T(8,128)(2,1)S(1)}, bf16[64,512]{1,0:T(8,128)(2,1)S(1)}, u32[]{:S(2)}, u32[]{:S(2)}) %collective-permute-start.7) | collective-permute-done | bytes 65568 | tf_op jit(solution)/shard_map/ppermute | solution.py:34
  34.4 0.7 %project_out.5.a_ref = f32[32,1024]{1,0:T(8,128)S(1)} custom-call(bf16[64,512]{1,0:T(8,128)(2,1)S(1)} %collective-permute-done.7.refs_0_, bf16[512,4096]{1,0:T(8,128)(2,1)S(1)} %get-tuple-element.17.refs_2_.refs_1_, bf16[512,4096]{1,0:T(8,128)(2,1)S(1)} %get-tuple-element.18.refs_3_.refs_2_, f32[32,1024]{1,0:T(8,128)S(1)} %project_out.4.refs_3_), custom_call_target="tpu_custom_call" | custom-call | flops 67108864 | bytes 2097152 | tf_op jit(solution)/shard_map/project_out/pallas_call | solution.py:278
  35.2 0.1 collective-permute-start.10
  35.2 1.3 %collective-permute-done.10.b_ref = f32[32,1024]{1,0:T(8,128)S(1)} collective-permute-done((f32[32,1024]{1,0:T(8,128)S(1)}, f32[32,1024]{1,0:T(8,128)S(1)}, u32[]{:S(2)}, u32[]{:S(2)}) %collective-permute-start.10) | collective-permute-done | bytes 131104 | tf_op jit(solution)/shard_map/ppermute | solution.py:302
  36.6 0.6 %add.1 = bf16[32,1024]{1,0:T(8,128)(2,1)} custom-call(f32[32,1024]{1,0:T(8,128)S(1)} %project_out.5.a_ref, f32[32,1024]{1,0:T(8,128)S(1)} %collective-permute-done.10.b_ref), custom_call_target="tpu_custom_call" | custom-call | tf_op jit(solution)/shard_map/add/pallas_call | solution.py:303
  (9 shorter events, 0.0 us)
Async XLA Ops:
  0.0 14.5 %copy-start.2 = (f32[4096]{0:T(1024)S(1)}, f32[4096]{0:T(1024)}, u32[]{:S(2)}) copy-start(f32[4096]{0:T(1024)} %param.8) | copy-start | bytes 49156
  0.0 5.0 %collective-permute-start = (bf16[4,4096]{1,0:T(4,128)(2,1)}, bf16[4,4096]{1,0:T(4,128)(2,1)S(1)}, u32[]{:S(2)}, u32[]{:S(2)}) collective-permute-start(bf16[4,4096]{1,0:T(4,128)(2,1)} %x_ref.1), channel_id=1, source_target_pairs={{0,2},{2,0},{4,6},{6,4},{8,10},{10,8},{12,14},{14,12},{1,3},{3,1},... | collective-permute-start | bytes 98312 | tf_op jit(solution)/shard_map/ppermute | solution.py:34
  2.9 11.5 %copy-start = (bf16[1,3,1024,4096]{3,2,1,0:T(8,128)(2,1)S(1)}, bf16[1,3,1024,4096]{3,2,1,0:T(8,128)(2,1)}, u32[]{:S(2)}) copy-start(bf16[1,3,1024,4096]{3,2,1,0:T(8,128)(2,1)} %w_ref.1) | copy-start | bytes 75497472
  5.1 6.6 %collective-permute-start.1 = (bf16[8,4096]{1,0:T(8,128)(2,1)S(1)}, bf16[8,4096]{1,0:T(8,128)(2,1)S(1)}, u32[]{:S(2)}, u32[]{:S(2)}) collective-permute-start(bf16[8,4096]{1,0:T(8,128)(2,1)S(1)} %stack.3.refs_0_), channel_id=1, source_target_pairs={{0,12},{2,14},{4,8},{6,10},{8,4},{10,6},{12,0},{14,2},{1,13},{3,15... | collective-permute-start | bytes 196616 | tf_op jit(solution)/shard_map/ppermute | solution.py:34
  9.3 5.2 %collective-permute-start.2 = (bf16[8,4096]{1,0:T(8,128)(2,1)S(1)}, bf16[8,4096]{1,0:T(8,128)(2,1)S(1)}, u32[]{:S(2)}, u32[]{:S(2)}) collective-permute-start(bf16[8,4096]{1,0:T(8,128)(2,1)S(1)} %stack.3.refs_0_), channel_id=1, source_target_pairs={{0,8},{2,10},{4,12},{6,14},{8,0},{10,2},{12,4},{14,6},{1,9},{3,11}... | collective-permute-start | bytes 196616 | tf_op jit(solution)/shard_map/ppermute | solution.py:34
  9.3 5.2 %collective-permute-start.3 = (bf16[8,4096]{1,0:T(8,128)(2,1)S(1)}, bf16[8,4096]{1,0:T(8,128)(2,1)S(1)}, u32[]{:S(2)}, u32[]{:S(2)}) collective-permute-start(bf16[8,4096]{1,0:T(8,128)(2,1)S(1)} %stack.3.refs_0_), channel_id=1, source_target_pairs={{0,4},{2,6},{4,0},{6,2},{8,12},{10,14},{12,8},{14,10},{1,5},{3,7},... | collective-permute-start | bytes 196616 | tf_op jit(solution)/shard_map/ppermute | solution.py:34
  18.4 4.0 %collective-permute-start.4 = (f32[32,1664]{1,0:T(8,128)S(1)}, f32[32,1664]{1,0:T(8,128)S(1)}, u32[]{:S(2)}, u32[]{:S(2)}) collective-permute-start(f32[32,1664]{1,0:T(8,128)S(1)} %get-tuple-element.15.refs_2_), channel_id=1, source_target_pairs={{0,1},{1,0},{2,3},{3,2},{4,5},{5,4},{6,7},{7,6},{8,9},{9,8},{10,11... | collective-permute-start | bytes 638984 | tf_op jit(solution)/shard_map/ppermute | solution.py:190
  18.5 3.9 %copy-start.1 = (f32[7,3,1024]{2,0,1:T(8,128)S(1)}, f32[7,3,1024]{2,0,1:T(8,128)}, u32[]{:S(2)}) copy-start(f32[7,3,1024]{2,0,1:T(8,128)} %param.10) | copy-start | bytes 258052
  18.5 3.9 %copy-start.3 = (f32[1024]{0:T(1024)S(1)}, f32[1024]{0:T(1024)}, u32[]{:S(2)}) copy-start(f32[1024]{0:T(1024)} %param.12) | copy-start | bytes 12292
  22.8 5.8 %collective-permute-start.8 = (bf16[32,512]{1,0:T(8,128)(2,1)S(1)}, bf16[32,512]{1,0:T(8,128)(2,1)S(1)}, u32[]{:S(2)}, u32[]{:S(2)}) collective-permute-start(bf16[32,512]{1,0:T(8,128)(2,1)S(1)} %mix.1.refs_0_), channel_id=1, source_target_pairs={{0,12},{2,14},{4,8},{6,10},{8,4},{10,6},{12,0},{14,2},{1,13},{3,15... | collective-permute-start | bytes 98312 | tf_op jit(solution)/shard_map/ppermute | solution.py:34
  24.9 5.2 %collective-permute-start.5 = (bf16[32,512]{1,0:T(8,128)(2,1)S(1)}, bf16[32,512]{1,0:T(8,128)(2,1)S(1)}, u32[]{:S(2)}, u32[]{:S(2)}) collective-permute-start(bf16[32,512]{1,0:T(8,128)(2,1)S(1)} %mix.1.refs_0_), channel_id=1, source_target_pairs={{0,8},{2,10},{4,12},{6,14},{8,0},{10,2},{12,4},{14,6},{1,9},{3,11}... | collective-permute-start | bytes 98312 | tf_op jit(solution)/shard_map/ppermute | solution.py:34
  24.9 5.2 %collective-permute-start.6 = (bf16[32,512]{1,0:T(8,128)(2,1)S(1)}, bf16[32,512]{1,0:T(8,128)(2,1)S(1)}, u32[]{:S(2)}, u32[]{:S(2)}) collective-permute-start(bf16[32,512]{1,0:T(8,128)(2,1)S(1)} %mix.1.refs_0_), channel_id=1, source_target_pairs={{0,4},{2,6},{4,0},{6,2},{8,12},{10,14},{12,8},{14,10},{1,5},{3,7},... | collective-permute-start | bytes 98312 | tf_op jit(solution)/shard_map/ppermute | solution.py:34
  28.6 4.6 %collective-permute-start.9 = (bf16[64,512]{1,0:T(8,128)(2,1)S(1)}, bf16[64,512]{1,0:T(8,128)(2,1)S(1)}, u32[]{:S(2)}, u32[]{:S(2)}) collective-permute-start(bf16[64,512]{1,0:T(8,128)(2,1)S(1)} %stack.5.refs_0_), channel_id=1, source_target_pairs={{0,2},{2,0},{4,6},{6,4},{8,10},{10,8},{12,14},{14,12},{1,3},{3,1},... | collective-permute-start | bytes 196616 | tf_op jit(solution)/shard_map/ppermute | solution.py:34
  30.1 4.3 %collective-permute-start.7 = (bf16[64,512]{1,0:T(8,128)(2,1)S(1)}, bf16[64,512]{1,0:T(8,128)(2,1)S(1)}, u32[]{:S(2)}, u32[]{:S(2)}) collective-permute-start(bf16[64,512]{1,0:T(8,128)(2,1)S(1)} %stack.4.refs_1_), channel_id=1, source_target_pairs={{0,2},{2,0},{4,6},{6,4},{8,10},{10,8},{12,14},{14,12},{1,3},{3,1},... | collective-permute-start | bytes 196616 | tf_op jit(solution)/shard_map/ppermute | solution.py:34
  35.2 1.4 %collective-permute-start.10 = (f32[32,1024]{1,0:T(8,128)S(1)}, f32[32,1024]{1,0:T(8,128)S(1)}, u32[]{:S(2)}, u32[]{:S(2)}) collective-permute-start(f32[32,1024]{1,0:T(8,128)S(1)} %project_out.5.a_ref), channel_id=1, source_target_pairs={{0,1},{1,0},{2,3},{3,2},{4,5},{5,4},{6,7},{7,6},{8,9},{9,8},{10,11... | collective-permute-start | bytes 393224 | tf_op jit(solution)/shard_map/ppermute | solution.py:302

commit v5 on v4

--- a/solution.py
+++ b/solution.py
@@ -133,34 +133,51 @@
     return jnp.dot(jnp.where(hit, 1.0, 0.0).astype(BF16), raw, preferred_element_type=F32)
 
 
+PUSH = 128
+STREAM = 128
+DEPTH = 512
+
+
+def channel_sums(xg_ref, xt_ref, w_ref, which, out_ref, chan):
+    tokens, half = xg_ref.shape
+    first = rows_of(which, chan)
+    for p in range(3):
+        for at in range(0, chan, PUSH + STREAM):
+            low = pl.ds(pl.multiple_of(first + at, PUSH), PUSH)
+            high = pl.ds(pl.multiple_of(first + at + PUSH, STREAM), STREAM)
+            pushed = streamed = None
+            for depth in range(0, half, DEPTH):
+                cut = slice(depth, depth + DEPTH)
+                term = contract_last(xg_ref[:, cut], w_ref[0, p, low, cut])
+                pushed = term if pushed is None else pushed + term
+                term = jnp.dot(w_ref[0, p, high, cut], xt_ref[cut, :], preferred_element_type=F32)
+                streamed = term if streamed is None else streamed + term
+            to = p * chan + at
+            out_ref[:, to : to + PUSH] = pushed
+            out_ref[:, to + PUSH : to + PUSH + STREAM] = streamed.T
+
+
 def partner_kernel(*refs, owners):
-    pieces, (gain_ref, w_ref, wo_ref, out_ref, xg_ref, load_ref, sem) = refs[:-7], refs[-7:]
+    pieces, refs = refs[:-8], refs[-8:]
+    gain_ref, w_ref, wo_ref, out_ref, xg_ref, xt_ref, load_ref, sem = refs
     load = pltpu.make_async_copy(wo_ref.at[pl.ds(0, load_ref.shape[0])], load_ref, sem)
     load.start()
     tokens = out_ref.shape[0]
-    chan = w_ref.shape[2] // 2
     values = ordered(pieces, owners, tokens)
     squares = jnp.sum(values * values, axis=1, keepdims=True)
-    out_ref[:, 3 * chan :] = jnp.broadcast_to(squares, (tokens, LANES))
-    xg_ref[...] = (values * gain_ref[...]).astype(BF16)
-    first = rows_of("partner", chan)
-    for p in range(3):
-        out_ref[:, p * chan : (p + 1) * chan] = contract_last(
-            xg_ref[...], w_ref[0, p, pl.ds(first, chan), :]
-        )
+    out_ref[:, -LANES:] = jnp.broadcast_to(squares, (tokens, LANES))
+    gained = (values * gain_ref[...]).astype(BF16)
+    xg_ref[...] = gained
+    xt_ref[...] = gained.astype(F32).T.astype(BF16)
+    channel_sums(xg_ref, xt_ref, w_ref, "partner", out_ref, w_ref.shape[2] // 2)
     load.wait()
 
 
-def own_kernel(xg_ref, w_ref, wo_ref, out_ref, load_ref, sem):
+def own_kernel(xg_ref, xt_ref, w_ref, wo_ref, out_ref, load_ref, sem):
     rows = load_ref.shape[0]
     load = pltpu.make_async_copy(wo_ref.at[pl.ds(wo_ref.shape[0] - rows, rows)], load_ref, sem)
     load.start()
-    chan = w_ref.shape[2] // 2
-    first = rows_of("own", chan)
-    for p in range(3):
-        out_ref[:, p * chan : (p + 1) * chan] = contract_last(
-            xg_ref[...], w_ref[0, p, pl.ds(first, chan), :]
-        )
+    channel_sums(xg_ref, xt_ref, w_ref, "own", out_ref, w_ref.shape[2] // 2)
     load.wait()
 
 
@@ -173,15 +190,16 @@
     rows = weights_out.shape[0] // 2
     half_out = pltpu.VMEM((rows, weights_out.shape[1]), weights_out.dtype)
     weights_out = in_hbm(weights_out)
-    partner, xg, low = pl.pallas_call(
+    partner, xg, xt, low = pl.pallas_call(
         functools.partial(partner_kernel, owners=owners),
         out_shape=(
             jax.ShapeDtypeStruct((tokens, 3 * chan + LANES), F32),
             jax.ShapeDtypeStruct((tokens, half), BF16),
+            jax.ShapeDtypeStruct((half, tokens), BF16),
             half_out,
         ),
         in_specs=[VMEM] * (2 + len(pieces)) + [ANY],
-        out_specs=(VMEM,) * 3,
+        out_specs=(VMEM,) * 4,
         scratch_shapes=[pltpu.SemaphoreType.DMA],
         compiler_params=params(8),
         cost_estimate=work,
@@ -194,13 +212,13 @@
             jax.ShapeDtypeStruct((tokens, 3 * chan), F32),
             half_out,
         ),
-        in_specs=[VMEM] * 2 + [ANY],
+        in_specs=[VMEM] * 3 + [ANY],
         out_specs=(VMEM,) * 2,
         scratch_shapes=[pltpu.SemaphoreType.DMA],
         compiler_params=params(8),
         cost_estimate=work,
         name="project_own",
-    )(xg, weights, weights_out)
+    )(xg, xt, weights, weights_out)
     return own, got, partner, taps, (in_vmem(low), in_vmem(high))
 
 
@@ -361,7 +379,14 @@
         P("seq"),
         P("seq", "mdl", None),
     )
-    body = per_device if seq == 8 and mesh.shape["mdl"] == 2 else per_device_any
+
+    def body(tokens_in, norm_gain, in_proj, *others):
+        half, chan = tokens_in.shape[1], in_proj.shape[2] // 2
+        fits = seq == 8 and mesh.shape["mdl"] == 2
+        fits = fits and chan % (PUSH + STREAM) == 0 and half % DEPTH == 0
+        path = per_device if fits else per_device_any
+        return path(tokens_in, norm_gain, in_proj, *others)
+
     return jax.shard_map(
         body, mesh=mesh, in_specs=in_specs, out_specs=P("grp", "seq"), check_vma=False
     )

time: 37.3 us -> 36.7 us (0.984)
  Pallas kernels: 12.9 us -> 12.2 us
    pallas_call x1, Pallas kernels: 3.84 us -> 3.36 us  [project(): pl.pallas_call(own_kernel, out_shape=(jax.ShapeDtypeStruct((tokens, 3 * c...]
  transfers between devices with their start and end apart: 11 -> 11, of which waited for: 7 -> 7; matrix products, arithmetic and copies ran while one was open for 0% -> 0% of each run, Pallas kernels for 19% -> 18%
where the time goes in v5:
time: 36.7 us; the launch traced here: 36.5 us
  starting transfers between devices  15.3 us (42%)
  Pallas kernels  12.2 us (33%)
  waiting for transfers between devices  8.86 us (24%)
    ppermute x9, starting transfers between devices, swap(): return lax.ppermute(x, 'seq', [(i, i ^ bits) for i in range(count)])  15.2 us
    ppermute x9, waiting for transfers between devices, swap(): return lax.ppermute(x, 'seq', [(i, i ^ bits) for i in range(count)])  7.53 us
    pallas_call x1, Pallas kernels, project(): pl.pallas_call(functools.partial(partner_kernel, owners=owners), out_shap...  3.72 us
    pallas_call x1, Pallas kernels, project(): pl.pallas_call(own_kernel, out_shape=(jax.ShapeDtypeStruct((tokens, 3 * c...  3.36 us
    pallas_call x3, Pallas kernels, project_out(): pl.pallas_call(functools.partial(out_kernel, count=len(pieces), owners=ow...  2.76 us
    ppermute x1, waiting for transfers between devices, per_device(): other = lax.ppermute(partial_out, 'mdl', [(0, 1), (1, 0)])  1.33 us
    pallas_call x1, Pallas kernels, prepare(): pl.pallas_call(prepare_kernel, out_shape=(jax.ShapeDtypeStruct(x.shape, x...  1.3 us
  transfers between devices with their start and end apart: 11, of which 7 were waited for; matrix products, arithmetic and copies ran while one was open for 0% of the time, Pallas kernels for 18%

profile of v5, /device:TPU:0, one launch (start us, length us, event | category | flops | bytes accessed | tf_op | source)
XLA Modules:
  0.0 36.5 jit_solution(8566499590608106113)
XLA Ops:
  0.0 2.9 %collective-permute-start = (bf16[4,4096]{1,0:T(4,128)(2,1)}, bf16[4,4096]{1,0:T(4,128)(2,1)S(1)}, u32[]{:S(2)}, u32[]{:S(2)}) collective-permute-start(bf16[4,4096]{1,0:T(4,128)(2,1)} %x_ref.1), channel_id=1, source_target_pairs={{0,2},{2,0},{4,6},{6,4},{8,10},{10,8},{12,14},{14,12},{1,3},{3,1},... | collective-permute-start | bytes 98312 | tf_op jit(solution)/shard_map/ppermute | solution.py:34
  2.9 1.3 %prepare.1 = (bf16[4,4096]{1,0:T(4,128)(2,1)S(1)}, f32[32,512]{1,0:T(8,128)S(1)}) custom-call(bf16[4,4096]{1,0:T(4,128)(2,1)} %x_ref.1, f32[512,128]{1,0:T(8,128)} %taps_ref.1), custom_call_target="tpu_custom_call" | custom-call | flops 12000000000 | bytes 4194304 | tf_op jit(solution)/shard_map/prepare/pallas_call | solution.py:104
  4.3 0.8 %collective-permute-done.refs_1_ = bf16[4,4096]{1,0:T(4,128)(2,1)S(1)} collective-permute-done((bf16[4,4096]{1,0:T(4,128)(2,1)}, bf16[4,4096]{1,0:T(4,128)(2,1)S(1)}, u32[]{:S(2)}, u32[]{:S(2)}) %collective-permute-start) | collective-permute-done | bytes 32800 | tf_op jit(solution)/shard_map/ppermute | solution.py:34
  5.1 4.2 %collective-permute-start.1 = (bf16[8,4096]{1,0:T(8,128)(2,1)S(1)}, bf16[8,4096]{1,0:T(8,128)(2,1)S(1)}, u32[]{:S(2)}, u32[]{:S(2)}) collective-permute-start(bf16[8,4096]{1,0:T(8,128)(2,1)S(1)} %stack.3.refs_0_), channel_id=1, source_target_pairs={{0,12},{2,14},{4,8},{6,10},{8,4},{10,6},{12,0},{14,2},{1,13},{3,15... | collective-permute-start | bytes 196616 | tf_op jit(solution)/shard_map/ppermute | solution.py:34
  9.3 0.0 collective-permute-start.2
  9.3 0.6 %collective-permute-start.3 = (bf16[8,4096]{1,0:T(8,128)(2,1)S(1)}, bf16[8,4096]{1,0:T(8,128)(2,1)S(1)}, u32[]{:S(2)}, u32[]{:S(2)}) collective-permute-start(bf16[8,4096]{1,0:T(8,128)(2,1)S(1)} %stack.3.refs_0_), channel_id=1, source_target_pairs={{0,4},{2,6},{4,0},{6,2},{8,12},{10,14},{12,8},{14,10},{1,5},{3,7},... | collective-permute-start | bytes 196616 | tf_op jit(solution)/shard_map/ppermute | solution.py:34
  9.9 1.8 %collective-permute-done.1.refs_1_ = bf16[8,4096]{1,0:T(8,128)(2,1)S(1)} collective-permute-done((bf16[8,4096]{1,0:T(8,128)(2,1)S(1)}, bf16[8,4096]{1,0:T(8,128)(2,1)S(1)}, u32[]{:S(2)}, u32[]{:S(2)}) %collective-permute-start.1) | collective-permute-done | bytes 65568 | tf_op jit(solution)/shard_map/ppermute | solution.py:34
  11.7 2.8 %collective-permute-done.2.refs_2_ = bf16[8,4096]{1,0:T(8,128)(2,1)S(1)} collective-permute-done((bf16[8,4096]{1,0:T(8,128)(2,1)S(1)}, bf16[8,4096]{1,0:T(8,128)(2,1)S(1)}, u32[]{:S(2)}, u32[]{:S(2)}) %collective-permute-start.2) | collective-permute-done | bytes 65568 | tf_op jit(solution)/shard_map/ppermute | solution.py:34
  14.5 0.0 collective-permute-done.3.refs_3_
  14.5 3.7 %project_partner.1 = (f32[32,1664]{1,0:T(8,128)S(1)}, bf16[32,4096]{1,0:T(8,128)(2,1)S(1)}, bf16[4096,32]{1,0:T(8,128)(2,1)S(1)}, bf16[512,4096]{1,0:T(8,128)(2,1)S(1)}) custom-call(bf16[8,4096]{1,0:T(8,128)(2,1)S(1)} %stack.3.refs_0_, bf16[8,4096]{1,0:T(8,128)(2,1)S(1)} %collective-permute-done.1.refs_1_, ...), custom_call_target="tpu_custom_call" | custom-call | flops 402653184 | bytes 12582912 | tf_op jit(solution)/shard_map/project_partner/pallas_call | solution.py:193
  18.2 0.1 collective-permute-start.4
  18.3 0.0 copy-start.1
  18.3 0.0 copy-start.3
  18.3 3.4 %project_own.1 = (f32[32,1536]{1,0:T(8,128)S(1)}, bf16[512,4096]{1,0:T(8,128)(2,1)S(1)}) custom-call(bf16[32,4096]{1,0:T(8,128)(2,1)S(1)} %get-tuple-element.14.xg_ref, bf16[4096,32]{1,0:T(8,128)(2,1)S(1)} %get-tuple-element.15.xt_ref, bf16[1,3,1024,4096]{3,2,1,0:T(8,128)(2,1)S(1)} %copy-done, bf16[1024,4096]{1,0:T(8,128)(2,1)} %bitcast.8), custom_call_target="tpu_custom_call" | custom-call | flops 402653184 | bytes 12582912 | tf_op jit(solution)/shard_map/project_own/pallas_call | solution.py:209
  21.7 0.0 collective-permute-done.4.refs_1_
  21.7 0.4 %mix.1.refs_0_ = bf16[32,512]{1,0:T(8,128)(2,1)S(1)} custom-call(f32[32,1536]{1,0:T(8,128)S(1)} %get-tuple-element.16.refs_0_, f32[32,1664]{1,0:T(8,128)S(1)} %collective-permute-done.4.refs_1_, f32[32,1664]{1,0:T(8,128)S(1)} %get-tuple-element.17.refs_2_, f32[3,7,1024]{2,1,0:T(8,128)S(1)} %bitcast.4, f32[1,1024]{1,0:T(1,128)S(1)} %bitcast.6, ...), custom_call_target="tpu_custom_call" | custom-call | tf_op jit(solution)/shard_map/mix/pallas_call | solution.py:261
  22.1 2.2 %collective-permute-start.8 = (bf16[32,512]{1,0:T(8,128)(2,1)S(1)}, bf16[32,512]{1,0:T(8,128)(2,1)S(1)}, u32[]{:S(2)}, u32[]{:S(2)}) collective-permute-start(bf16[32,512]{1,0:T(8,128)(2,1)S(1)} %mix.1.refs_0_), channel_id=1, source_target_pairs={{0,12},{2,14},{4,8},{6,10},{8,4},{10,6},{12,0},{14,2},{1,13},{3,15... | collective-permute-start | bytes 98312 | tf_op jit(solution)/shard_map/ppermute | solution.py:34
  24.3 0.0 collective-permute-start.5
  24.3 2.3 %collective-permute-start.6 = (bf16[32,512]{1,0:T(8,128)(2,1)S(1)}, bf16[32,512]{1,0:T(8,128)(2,1)S(1)}, u32[]{:S(2)}, u32[]{:S(2)}) collective-permute-start(bf16[32,512]{1,0:T(8,128)(2,1)S(1)} %mix.1.refs_0_), channel_id=1, source_target_pairs={{0,4},{2,6},{4,0},{6,2},{8,12},{10,14},{12,8},{14,10},{1,5},{3,7},... | collective-permute-start | bytes 98312 | tf_op jit(solution)/shard_map/ppermute | solution.py:34
  26.6 1.4 %collective-permute-done.8.refs_1_ = bf16[32,512]{1,0:T(8,128)(2,1)S(1)} collective-permute-done((bf16[32,512]{1,0:T(8,128)(2,1)S(1)}, bf16[32,512]{1,0:T(8,128)(2,1)S(1)}, u32[]{:S(2)}, u32[]{:S(2)}) %collective-permute-start.8) | collective-permute-done | bytes 32800 | tf_op jit(solution)/shard_map/ppermute | solution.py:34
  27.9 1.5 %collective-permute-start.9 = (bf16[64,512]{1,0:T(8,128)(2,1)S(1)}, bf16[64,512]{1,0:T(8,128)(2,1)S(1)}, u32[]{:S(2)}, u32[]{:S(2)}) collective-permute-start(bf16[64,512]{1,0:T(8,128)(2,1)S(1)} %stack.5.refs_0_), channel_id=1, source_target_pairs={{0,2},{2,0},{4,6},{6,4},{8,10},{10,8},{12,14},{14,12},{1,3},{3,1},... | collective-permute-start | bytes 196616 | tf_op jit(solution)/shard_map/ppermute | solution.py:34
  29.4 0.0 collective-permute-done.5.refs_0_
  29.4 0.0 collective-permute-done.6.refs_1_
  29.4 1.5 %collective-permute-start.7 = (bf16[64,512]{1,0:T(8,128)(2,1)S(1)}, bf16[64,512]{1,0:T(8,128)(2,1)S(1)}, u32[]{:S(2)}, u32[]{:S(2)}) collective-permute-start(bf16[64,512]{1,0:T(8,128)(2,1)S(1)} %stack.4.refs_1_), channel_id=1, source_target_pairs={{0,2},{2,0},{4,6},{6,4},{8,10},{10,8},{12,14},{14,12},{1,3},{3,1},... | collective-permute-start | bytes 196616 | tf_op jit(solution)/shard_map/ppermute | solution.py:34
  30.9 1.3 %project_out.3.refs_3_ = f32[32,1024]{1,0:T(8,128)S(1)} custom-call(bf16[64,512]{1,0:T(8,128)(2,1)S(1)} %stack.5.refs_0_, bf16[64,512]{1,0:T(8,128)(2,1)S(1)} %stack.4.refs_1_, bf16[512,4096]{1,0:T(8,128)(2,1)S(1)} %get-tuple-element.19.refs_2_.refs_1_, bf16[512,4096]{1,0:T(8,128)(2,1)S(1)} %get-tuple-element.20.refs_3_.refs_2_), custom_call_target="tpu_custom_call" | custom-call | flops 134217728 | bytes 4194304 | tf_op jit(solution)/shard_map/project_out/pallas_call | solution.py:296
  32.2 0.3 collective-permute-done.9.refs_0_
  32.5 0.7 %project_out.4.refs_3_ = f32[32,1024]{1,0:T(8,128)S(1)} custom-call(bf16[64,512]{1,0:T(8,128)(2,1)S(1)} %collective-permute-done.9.refs_0_, bf16[512,4096]{1,0:T(8,128)(2,1)S(1)} %get-tuple-element.19.refs_2_.refs_1_, bf16[512,4096]{1,0:T(8,128)(2,1)S(1)} %get-tuple-element.20.refs_3_.refs_2_, f32[32,1024]{1,0:T(8,128)S(1)} %project_out.3.refs_3_), custom_call_target="tpu_custom_call" | custom-call | flops 67108864 | bytes 2097152 | tf_op jit(solution)/shard_map/project_out/pallas_call | solution.py:296
  33.2 0.5 %collective-permute-done.7.refs_0_ = bf16[64,512]{1,0:T(8,128)(2,1)S(1)} collective-permute-done((bf16[64,512]{1,0:T(8,128)(2,1)S(1)}, bf16[64,512]{1,0:T(8,128)(2,1)S(1)}, u32[]{:S(2)}, u32[]{:S(2)}) %collective-permute-start.7) | collective-permute-done | bytes 65568 | tf_op jit(solution)/shard_map/ppermute | solution.py:34
  33.8 0.7 %project_out.5.a_ref = f32[32,1024]{1,0:T(8,128)S(1)} custom-call(bf16[64,512]{1,0:T(8,128)(2,1)S(1)} %collective-permute-done.7.refs_0_, bf16[512,4096]{1,0:T(8,128)(2,1)S(1)} %get-tuple-element.19.refs_2_.refs_1_, bf16[512,4096]{1,0:T(8,128)(2,1)S(1)} %get-tuple-element.20.refs_3_.refs_2_, f32[32,1024]{1,0:T(8,128)S(1)} %project_out.4.refs_3_), custom_call_target="tpu_custom_call" | custom-call | flops 67108864 | bytes 2097152 | tf_op jit(solution)/shard_map/project_out/pallas_call | solution.py:296
  34.5 0.1 collective-permute-start.10
  34.6 1.3 %collective-permute-done.10.b_ref = f32[32,1024]{1,0:T(8,128)S(1)} collective-permute-done((f32[32,1024]{1,0:T(8,128)S(1)}, f32[32,1024]{1,0:T(8,128)S(1)}, u32[]{:S(2)}, u32[]{:S(2)}) %collective-permute-start.10) | collective-permute-done | bytes 131104 | tf_op jit(solution)/shard_map/ppermute | solution.py:320
  35.9 0.6 %add.1 = bf16[32,1024]{1,0:T(8,128)(2,1)} custom-call(f32[32,1024]{1,0:T(8,128)S(1)} %project_out.5.a_ref, f32[32,1024]{1,0:T(8,128)S(1)} %collective-permute-done.10.b_ref), custom_call_target="tpu_custom_call" | custom-call | tf_op jit(solution)/shard_map/add/pallas_call | solution.py:321
  (9 shorter events, 0.0 us)
Async XLA Ops:
  0.0 14.5 %copy-start.2 = (f32[4096]{0:T(1024)S(1)}, f32[4096]{0:T(1024)}, u32[]{:S(2)}) copy-start(f32[4096]{0:T(1024)} %param.8) | copy-start | bytes 49156
  0.0 5.0 %collective-permute-start = (bf16[4,4096]{1,0:T(4,128)(2,1)}, bf16[4,4096]{1,0:T(4,128)(2,1)S(1)}, u32[]{:S(2)}, u32[]{:S(2)}) collective-permute-start(bf16[4,4096]{1,0:T(4,128)(2,1)} %x_ref.1), channel_id=1, source_target_pairs={{0,2},{2,0},{4,6},{6,4},{8,10},{10,8},{12,14},{14,12},{1,3},{3,1},... | collective-permute-start | bytes 98312 | tf_op jit(solution)/shard_map/ppermute | solution.py:34
  2.9 11.5 %copy-start = (bf16[1,3,1024,4096]{3,2,1,0:T(8,128)(2,1)S(1)}, bf16[1,3,1024,4096]{3,2,1,0:T(8,128)(2,1)}, u32[]{:S(2)}) copy-start(bf16[1,3,1024,4096]{3,2,1,0:T(8,128)(2,1)} %w_ref.1) | copy-start | bytes 75497472
  5.1 6.6 %collective-permute-start.1 = (bf16[8,4096]{1,0:T(8,128)(2,1)S(1)}, bf16[8,4096]{1,0:T(8,128)(2,1)S(1)}, u32[]{:S(2)}, u32[]{:S(2)}) collective-permute-start(bf16[8,4096]{1,0:T(8,128)(2,1)S(1)} %stack.3.refs_0_), channel_id=1, source_target_pairs={{0,12},{2,14},{4,8},{6,10},{8,4},{10,6},{12,0},{14,2},{1,13},{3,15... | collective-permute-start | bytes 196616 | tf_op jit(solution)/shard_map/ppermute | solution.py:34
  9.3 5.2 %collective-permute-start.2 = (bf16[8,4096]{1,0:T(8,128)(2,1)S(1)}, bf16[8,4096]{1,0:T(8,128)(2,1)S(1)}, u32[]{:S(2)}, u32[]{:S(2)}) collective-permute-start(bf16[8,4096]{1,0:T(8,128)(2,1)S(1)} %stack.3.refs_0_), channel_id=1, source_target_pairs={{0,8},{2,10},{4,12},{6,14},{8,0},{10,2},{12,4},{14,6},{1,9},{3,11}... | collective-permute-start | bytes 196616 | tf_op jit(solution)/shard_map/ppermute | solution.py:34
  9.3 5.2 %collective-permute-start.3 = (bf16[8,4096]{1,0:T(8,128)(2,1)S(1)}, bf16[8,4096]{1,0:T(8,128)(2,1)S(1)}, u32[]{:S(2)}, u32[]{:S(2)}) collective-permute-start(bf16[8,4096]{1,0:T(8,128)(2,1)S(1)} %stack.3.refs_0_), channel_id=1, source_target_pairs={{0,4},{2,6},{4,0},{6,2},{8,12},{10,14},{12,8},{14,10},{1,5},{3,7},... | collective-permute-start | bytes 196616 | tf_op jit(solution)/shard_map/ppermute | solution.py:34
  18.2 3.5 %collective-permute-start.4 = (f32[32,1664]{1,0:T(8,128)S(1)}, f32[32,1664]{1,0:T(8,128)S(1)}, u32[]{:S(2)}, u32[]{:S(2)}) collective-permute-start(f32[32,1664]{1,0:T(8,128)S(1)} %get-tuple-element.17.refs_2_), channel_id=1, source_target_pairs={{0,1},{1,0},{2,3},{3,2},{4,5},{5,4},{6,7},{7,6},{8,9},{9,8},{10,11... | collective-permute-start | bytes 638984 | tf_op jit(solution)/shard_map/ppermute | solution.py:208
  18.3 3.4 %copy-start.1 = (f32[7,3,1024]{2,0,1:T(8,128)S(1)}, f32[7,3,1024]{2,0,1:T(8,128)}, u32[]{:S(2)}) copy-start(f32[7,3,1024]{2,0,1:T(8,128)} %param.10) | copy-start | bytes 258052
  18.3 3.4 %copy-start.3 = (f32[1024]{0:T(1024)S(1)}, f32[1024]{0:T(1024)}, u32[]{:S(2)}) copy-start(f32[1024]{0:T(1024)} %param.12) | copy-start | bytes 12292
  22.1 5.8 %collective-permute-start.8 = (bf16[32,512]{1,0:T(8,128)(2,1)S(1)}, bf16[32,512]{1,0:T(8,128)(2,1)S(1)}, u32[]{:S(2)}, u32[]{:S(2)}) collective-permute-start(bf16[32,512]{1,0:T(8,128)(2,1)S(1)} %mix.1.refs_0_), channel_id=1, source_target_pairs={{0,12},{2,14},{4,8},{6,10},{8,4},{10,6},{12,0},{14,2},{1,13},{3,15... | collective-permute-start | bytes 98312 | tf_op jit(solution)/shard_map/ppermute | solution.py:34
  24.3 5.2 %collective-permute-start.5 = (bf16[32,512]{1,0:T(8,128)(2,1)S(1)}, bf16[32,512]{1,0:T(8,128)(2,1)S(1)}, u32[]{:S(2)}, u32[]{:S(2)}) collective-permute-start(bf16[32,512]{1,0:T(8,128)(2,1)S(1)} %mix.1.refs_0_), channel_id=1, source_target_pairs={{0,8},{2,10},{4,12},{6,14},{8,0},{10,2},{12,4},{14,6},{1,9},{3,11}... | collective-permute-start | bytes 98312 | tf_op jit(solution)/shard_map/ppermute | solution.py:34
  24.3 5.2 %collective-permute-start.6 = (bf16[32,512]{1,0:T(8,128)(2,1)S(1)}, bf16[32,512]{1,0:T(8,128)(2,1)S(1)}, u32[]{:S(2)}, u32[]{:S(2)}) collective-permute-start(bf16[32,512]{1,0:T(8,128)(2,1)S(1)} %mix.1.refs_0_), channel_id=1, source_target_pairs={{0,4},{2,6},{4,0},{6,2},{8,12},{10,14},{12,8},{14,10},{1,5},{3,7},... | collective-permute-start | bytes 98312 | tf_op jit(solution)/shard_map/ppermute | solution.py:34
  27.9 4.6 %collective-permute-start.9 = (bf16[64,512]{1,0:T(8,128)(2,1)S(1)}, bf16[64,512]{1,0:T(8,128)(2,1)S(1)}, u32[]{:S(2)}, u32[]{:S(2)}) collective-permute-start(bf16[64,512]{1,0:T(8,128)(2,1)S(1)} %stack.5.refs_0_), channel_id=1, source_target_pairs={{0,2},{2,0},{4,6},{6,4},{8,10},{10,8},{12,14},{14,12},{1,3},{3,1},... | collective-permute-start | bytes 196616 | tf_op jit(solution)/shard_map/ppermute | solution.py:34
  29.4 4.3 %collective-permute-start.7 = (bf16[64,512]{1,0:T(8,128)(2,1)S(1)}, bf16[64,512]{1,0:T(8,128)(2,1)S(1)}, u32[]{:S(2)}, u32[]{:S(2)}) collective-permute-start(bf16[64,512]{1,0:T(8,128)(2,1)S(1)} %stack.4.refs_1_), channel_id=1, source_target_pairs={{0,2},{2,0},{4,6},{6,4},{8,10},{10,8},{12,14},{14,12},{1,3},{3,1},... | collective-permute-start | bytes 196616 | tf_op jit(solution)/shard_map/ppermute | solution.py:34
  34.5 1.4 %collective-permute-start.10 = (f32[32,1024]{1,0:T(8,128)S(1)}, f32[32,1024]{1,0:T(8,128)S(1)}, u32[]{:S(2)}, u32[]{:S(2)}) collective-permute-start(f32[32,1024]{1,0:T(8,128)S(1)} %project_out.5.a_ref), channel_id=1, source_target_pairs={{0,1},{1,0},{2,3},{3,2},{4,5},{5,4},{6,7},{7,6},{8,9},{9,8},{10,11... | collective-permute-start | bytes 393224 | tf_op jit(solution)/shard_map/ppermute | solution.py:320

commit v6 on v5

--- a/solution.py
+++ b/solution.py
@@ -119,18 +119,15 @@
     )(in_hbm(x), in_hbm(long_taps))
 
 
-def ordered(pieces, order, tokens):
-    raw = jnp.concatenate([piece[...].astype(F32) for piece in pieces], axis=0).astype(BF16)
-    me = lax.axis_index("seq")
-    per = tokens // len(order)
-    row = lax.broadcasted_iota(jnp.int32, (tokens, tokens), 0)
-    col = lax.broadcasted_iota(jnp.int32, (tokens, tokens), 1)
-    place = col // per
-    bits = jnp.zeros_like(place)
-    for k, value in enumerate(order):
-        bits = jnp.where(place == k, value, bits)
-    hit = ((row // per) ^ me == bits) & (row % per == col % per)
-    return jnp.dot(jnp.where(hit, 1.0, 0.0).astype(BF16), raw, preferred_element_type=F32)
+def place_rows(pieces, owners, out_ref):
+    per = out_ref.shape[1]
+    shards = [
+        piece[...].astype(F32)[i : i + per]
+        for piece in pieces
+        for i in range(0, piece.shape[0], per)
+    ]
+    for shard, bits in zip(shards, owners, strict=True):
+        out_ref[lax.axis_index("seq") ^ bits] = shard
 
 
 PUSH = 128
@@ -158,12 +155,13 @@
 
 
 def partner_kernel(*refs, owners):
-    pieces, refs = refs[:-8], refs[-8:]
-    gain_ref, w_ref, wo_ref, out_ref, xg_ref, xt_ref, load_ref, sem = refs
+    pieces, refs = refs[:-9], refs[-9:]
+    gain_ref, w_ref, wo_ref, out_ref, xg_ref, xt_ref, load_ref, raw_ref, sem = refs
     load = pltpu.make_async_copy(wo_ref.at[pl.ds(0, load_ref.shape[0])], load_ref, sem)
     load.start()
     tokens = out_ref.shape[0]
-    values = ordered(pieces, owners, tokens)
+    place_rows(pieces, owners, raw_ref)
+    values = jnp.concatenate([raw_ref[i] for i in range(raw_ref.shape[0])], axis=0)
     squares = jnp.sum(values * values, axis=1, keepdims=True)
     out_ref[:, -LANES:] = jnp.broadcast_to(squares, (tokens, LANES))
     gained = (values * gain_ref[...]).astype(BF16)
@@ -200,7 +198,10 @@
         ),
         in_specs=[VMEM] * (2 + len(pieces)) + [ANY],
         out_specs=(VMEM,) * 4,
-        scratch_shapes=[pltpu.SemaphoreType.DMA],
+        scratch_shapes=[
+            pltpu.VMEM((len(owners), tokens // len(owners), half), F32),
+            pltpu.SemaphoreType.DMA,
+        ],
         compiler_params=params(8),
         cost_estimate=work,
         name="project_partner",

time: 36.7 us -> 36.5 us (level)
  no operation moved by 1% of the time
where the time goes in v6:
time: 36.5 us; the launch traced here: 36.3 us
  starting transfers between devices  15.3 us (42%)
  Pallas kernels  12 us (33%)
  waiting for transfers between devices  8.86 us (24%)
    ppermute x9, starting transfers between devices, swap(): return lax.ppermute(x, 'seq', [(i, i ^ bits) for i in range(count)])  15.2 us
    ppermute x9, waiting for transfers between devices, swap(): return lax.ppermute(x, 'seq', [(i, i ^ bits) for i in range(count)])  7.52 us
    pallas_call x1, Pallas kernels, project(): pl.pallas_call(functools.partial(partner_kernel, owners=owners), out_shap...  3.5 us
    pallas_call x1, Pallas kernels, project(): pl.pallas_call(own_kernel, out_shape=(jax.ShapeDtypeStruct((tokens, 3 * c...  3.36 us
    pallas_call x3, Pallas kernels, project_out(): pl.pallas_call(functools.partial(out_kernel, count=len(pieces), owners=ow...  2.76 us
    ppermute x1, waiting for transfers between devices, per_device(): other = lax.ppermute(partial_out, 'mdl', [(0, 1), (1, 0)])  1.33 us
    pallas_call x1, Pallas kernels, prepare(): pl.pallas_call(prepare_kernel, out_shape=(jax.ShapeDtypeStruct(x.shape, x...  1.3 us
  transfers between devices with their start and end apart: 11, of which 7 were waited for; matrix products, arithmetic and copies ran while one was open for 0% of the time, Pallas kernels for 18%

profile of v6, /device:TPU:0, one launch (start us, length us, event | category | flops | bytes accessed | tf_op | source)
XLA Modules:
  0.0 36.3 jit_solution(15466471726338723952)
XLA Ops:
  0.0 2.9 %collective-permute-start = (bf16[4,4096]{1,0:T(4,128)(2,1)}, bf16[4,4096]{1,0:T(4,128)(2,1)S(1)}, u32[]{:S(2)}, u32[]{:S(2)}) collective-permute-start(bf16[4,4096]{1,0:T(4,128)(2,1)} %x_ref.1), channel_id=1, source_target_pairs={{0,2},{2,0},{4,6},{6,4},{8,10},{10,8},{12,14},{14,12},{1,3},{3,1},... | collective-permute-start | bytes 98312 | tf_op jit(solution)/shard_map/ppermute | solution.py:34
  2.9 1.3 %prepare.1 = (bf16[4,4096]{1,0:T(4,128)(2,1)S(1)}, f32[32,512]{1,0:T(8,128)S(1)}) custom-call(bf16[4,4096]{1,0:T(4,128)(2,1)} %x_ref.1, f32[512,128]{1,0:T(8,128)} %taps_ref.1), custom_call_target="tpu_custom_call" | custom-call | flops 12000000000 | bytes 4194304 | tf_op jit(solution)/shard_map/prepare/pallas_call | solution.py:104
  4.3 0.8 %collective-permute-done.refs_1_ = bf16[4,4096]{1,0:T(4,128)(2,1)S(1)} collective-permute-done((bf16[4,4096]{1,0:T(4,128)(2,1)}, bf16[4,4096]{1,0:T(4,128)(2,1)S(1)}, u32[]{:S(2)}, u32[]{:S(2)}) %collective-permute-start) | collective-permute-done | bytes 32800 | tf_op jit(solution)/shard_map/ppermute | solution.py:34
  5.1 4.2 %collective-permute-start.1 = (bf16[8,4096]{1,0:T(8,128)(2,1)S(1)}, bf16[8,4096]{1,0:T(8,128)(2,1)S(1)}, u32[]{:S(2)}, u32[]{:S(2)}) collective-permute-start(bf16[8,4096]{1,0:T(8,128)(2,1)S(1)} %stack.3.refs_0_), channel_id=1, source_target_pairs={{0,12},{2,14},{4,8},{6,10},{8,4},{10,6},{12,0},{14,2},{1,13},{3,15... | collective-permute-start | bytes 196616 | tf_op jit(solution)/shard_map/ppermute | solution.py:34
  9.3 0.0 collective-permute-start.2
  9.3 0.6 %collective-permute-start.3 = (bf16[8,4096]{1,0:T(8,128)(2,1)S(1)}, bf16[8,4096]{1,0:T(8,128)(2,1)S(1)}, u32[]{:S(2)}, u32[]{:S(2)}) collective-permute-start(bf16[8,4096]{1,0:T(8,128)(2,1)S(1)} %stack.3.refs_0_), channel_id=1, source_target_pairs={{0,4},{2,6},{4,0},{6,2},{8,12},{10,14},{12,8},{14,10},{1,5},{3,7},... | collective-permute-start | bytes 196616 | tf_op jit(solution)/shard_map/ppermute | solution.py:34
  9.9 1.8 %collective-permute-done.1.refs_1_ = bf16[8,4096]{1,0:T(8,128)(2,1)S(1)} collective-permute-done((bf16[8,4096]{1,0:T(8,128)(2,1)S(1)}, bf16[8,4096]{1,0:T(8,128)(2,1)S(1)}, u32[]{:S(2)}, u32[]{:S(2)}) %collective-permute-start.1) | collective-permute-done | bytes 65568 | tf_op jit(solution)/shard_map/ppermute | solution.py:34
  11.7 2.8 %collective-permute-done.2.refs_2_ = bf16[8,4096]{1,0:T(8,128)(2,1)S(1)} collective-permute-done((bf16[8,4096]{1,0:T(8,128)(2,1)S(1)}, bf16[8,4096]{1,0:T(8,128)(2,1)S(1)}, u32[]{:S(2)}, u32[]{:S(2)}) %collective-permute-start.2) | collective-permute-done | bytes 65568 | tf_op jit(solution)/shard_map/ppermute | solution.py:34
  14.5 0.0 collective-permute-done.3.refs_3_
  14.5 3.5 %project_partner.1 = (f32[32,1664]{1,0:T(8,128)S(1)}, bf16[32,4096]{1,0:T(8,128)(2,1)S(1)}, bf16[4096,32]{1,0:T(8,128)(2,1)S(1)}, bf16[512,4096]{1,0:T(8,128)(2,1)S(1)}) custom-call(bf16[8,4096]{1,0:T(8,128)(2,1)S(1)} %stack.3.refs_0_, bf16[8,4096]{1,0:T(8,128)(2,1)S(1)} %collective-permute-done.1.refs_1_, ...), custom_call_target="tpu_custom_call" | custom-call | flops 402653184 | bytes 12582912 | tf_op jit(solution)/shard_map/project_partner/pallas_call | solution.py:191
  18.0 0.1 collective-permute-start.4
  18.1 0.0 copy-start.1
  18.1 0.0 copy-start.3
  18.1 3.4 %project_own.1 = (f32[32,1536]{1,0:T(8,128)S(1)}, bf16[512,4096]{1,0:T(8,128)(2,1)S(1)}) custom-call(bf16[32,4096]{1,0:T(8,128)(2,1)S(1)} %get-tuple-element.14.xg_ref, bf16[4096,32]{1,0:T(8,128)(2,1)S(1)} %get-tuple-element.15.xt_ref, bf16[1,3,1024,4096]{3,2,1,0:T(8,128)(2,1)S(1)} %copy-done, bf16[1024,4096]{1,0:T(8,128)(2,1)} %bitcast.8), custom_call_target="tpu_custom_call" | custom-call | flops 402653184 | bytes 12582912 | tf_op jit(solution)/shard_map/project_own/pallas_call | solution.py:210
  21.4 0.0 collective-permute-done.4.refs_1_
  21.5 0.4 %mix.1.refs_0_ = bf16[32,512]{1,0:T(8,128)(2,1)S(1)} custom-call(f32[32,1536]{1,0:T(8,128)S(1)} %get-tuple-element.16.refs_0_, f32[32,1664]{1,0:T(8,128)S(1)} %collective-permute-done.4.refs_1_, f32[32,1664]{1,0:T(8,128)S(1)} %get-tuple-element.17.refs_2_, f32[3,7,1024]{2,1,0:T(8,128)S(1)} %bitcast.4, f32[1,1024]{1,0:T(1,128)S(1)} %bitcast.6, ...), custom_call_target="tpu_custom_call" | custom-call | tf_op jit(solution)/shard_map/mix/pallas_call | solution.py:262
  21.9 2.2 %collective-permute-start.8 = (bf16[32,512]{1,0:T(8,128)(2,1)S(1)}, bf16[32,512]{1,0:T(8,128)(2,1)S(1)}, u32[]{:S(2)}, u32[]{:S(2)}) collective-permute-start(bf16[32,512]{1,0:T(8,128)(2,1)S(1)} %mix.1.refs_0_), channel_id=1, source_target_pairs={{0,12},{2,14},{4,8},{6,10},{8,4},{10,6},{12,0},{14,2},{1,13},{3,15... | collective-permute-start | bytes 98312 | tf_op jit(solution)/shard_map/ppermute | solution.py:34
  24.1 0.0 collective-permute-start.5
  24.1 2.3 %collective-permute-start.6 = (bf16[32,512]{1,0:T(8,128)(2,1)S(1)}, bf16[32,512]{1,0:T(8,128)(2,1)S(1)}, u32[]{:S(2)}, u32[]{:S(2)}) collective-permute-start(bf16[32,512]{1,0:T(8,128)(2,1)S(1)} %mix.1.refs_0_), channel_id=1, source_target_pairs={{0,4},{2,6},{4,0},{6,2},{8,12},{10,14},{12,8},{14,10},{1,5},{3,7},... | collective-permute-start | bytes 98312 | tf_op jit(solution)/shard_map/ppermute | solution.py:34
  26.3 1.4 %collective-permute-done.8.refs_1_ = bf16[32,512]{1,0:T(8,128)(2,1)S(1)} collective-permute-done((bf16[32,512]{1,0:T(8,128)(2,1)S(1)}, bf16[32,512]{1,0:T(8,128)(2,1)S(1)}, u32[]{:S(2)}, u32[]{:S(2)}) %collective-permute-start.8) | collective-permute-done | bytes 32800 | tf_op jit(solution)/shard_map/ppermute | solution.py:34
  27.7 1.5 %collective-permute-start.9 = (bf16[64,512]{1,0:T(8,128)(2,1)S(1)}, bf16[64,512]{1,0:T(8,128)(2,1)S(1)}, u32[]{:S(2)}, u32[]{:S(2)}) collective-permute-start(bf16[64,512]{1,0:T(8,128)(2,1)S(1)} %stack.5.refs_0_), channel_id=1, source_target_pairs={{0,2},{2,0},{4,6},{6,4},{8,10},{10,8},{12,14},{14,12},{1,3},{3,1},... | collective-permute-start | bytes 196616 | tf_op jit(solution)/shard_map/ppermute | solution.py:34
  29.2 0.0 collective-permute-done.5.refs_0_
  29.2 0.0 collective-permute-done.6.refs_1_
  29.2 1.5 %collective-permute-start.7 = (bf16[64,512]{1,0:T(8,128)(2,1)S(1)}, bf16[64,512]{1,0:T(8,128)(2,1)S(1)}, u32[]{:S(2)}, u32[]{:S(2)}) collective-permute-start(bf16[64,512]{1,0:T(8,128)(2,1)S(1)} %stack.4.refs_1_), channel_id=1, source_target_pairs={{0,2},{2,0},{4,6},{6,4},{8,10},{10,8},{12,14},{14,12},{1,3},{3,1},... | collective-permute-start | bytes 196616 | tf_op jit(solution)/shard_map/ppermute | solution.py:34
  30.7 1.3 %project_out.3.refs_3_ = f32[32,1024]{1,0:T(8,128)S(1)} custom-call(bf16[64,512]{1,0:T(8,128)(2,1)S(1)} %stack.5.refs_0_, bf16[64,512]{1,0:T(8,128)(2,1)S(1)} %stack.4.refs_1_, bf16[512,4096]{1,0:T(8,128)(2,1)S(1)} %get-tuple-element.19.refs_2_.refs_1_, bf16[512,4096]{1,0:T(8,128)(2,1)S(1)} %get-tuple-element.20.refs_3_.refs_2_), custom_call_target="tpu_custom_call" | custom-call | flops 134217728 | bytes 4194304 | tf_op jit(solution)/shard_map/project_out/pallas_call | solution.py:297
  32.0 0.3 collective-permute-done.9.refs_0_
  32.3 0.7 %project_out.4.refs_3_ = f32[32,1024]{1,0:T(8,128)S(1)} custom-call(bf16[64,512]{1,0:T(8,128)(2,1)S(1)} %collective-permute-done.9.refs_0_, bf16[512,4096]{1,0:T(8,128)(2,1)S(1)} %get-tuple-element.19.refs_2_.refs_1_, bf16[512,4096]{1,0:T(8,128)(2,1)S(1)} %get-tuple-element.20.refs_3_.refs_2_, f32[32,1024]{1,0:T(8,128)S(1)} %project_out.3.refs_3_), custom_call_target="tpu_custom_call" | custom-call | flops 67108864 | bytes 2097152 | tf_op jit(solution)/shard_map/project_out/pallas_call | solution.py:297
  33.0 0.5 %collective-permute-done.7.refs_0_ = bf16[64,512]{1,0:T(8,128)(2,1)S(1)} collective-permute-done((bf16[64,512]{1,0:T(8,128)(2,1)S(1)}, bf16[64,512]{1,0:T(8,128)(2,1)S(1)}, u32[]{:S(2)}, u32[]{:S(2)}) %collective-permute-start.7) | collective-permute-done | bytes 65568 | tf_op jit(solution)/shard_map/ppermute | solution.py:34
  33.6 0.7 %project_out.5.a_ref = f32[32,1024]{1,0:T(8,128)S(1)} custom-call(bf16[64,512]{1,0:T(8,128)(2,1)S(1)} %collective-permute-done.7.refs_0_, bf16[512,4096]{1,0:T(8,128)(2,1)S(1)} %get-tuple-element.19.refs_2_.refs_1_, bf16[512,4096]{1,0:T(8,128)(2,1)S(1)} %get-tuple-element.20.refs_3_.refs_2_, f32[32,1024]{1,0:T(8,128)S(1)} %project_out.4.refs_3_), custom_call_target="tpu_custom_call" | custom-call | flops 67108864 | bytes 2097152 | tf_op jit(solution)/shard_map/project_out/pallas_call | solution.py:297
  34.3 0.1 collective-permute-start.10
  34.3 1.3 %collective-permute-done.10.b_ref = f32[32,1024]{1,0:T(8,128)S(1)} collective-permute-done((f32[32,1024]{1,0:T(8,128)S(1)}, f32[32,1024]{1,0:T(8,128)S(1)}, u32[]{:S(2)}, u32[]{:S(2)}) %collective-permute-start.10) | collective-permute-done | bytes 131104 | tf_op jit(solution)/shard_map/ppermute | solution.py:321
  35.7 0.6 %add.1 = bf16[32,1024]{1,0:T(8,128)(2,1)} custom-call(f32[32,1024]{1,0:T(8,128)S(1)} %project_out.5.a_ref, f32[32,1024]{1,0:T(8,128)S(1)} %collective-permute-done.10.b_ref), custom_call_target="tpu_custom_call" | custom-call | tf_op jit(solution)/shard_map/add/pallas_call | solution.py:322
  (9 shorter events, 0.0 us)
Async XLA Ops:
  0.0 14.5 %copy-start.2 = (f32[4096]{0:T(1024)S(1)}, f32[4096]{0:T(1024)}, u32[]{:S(2)}) copy-start(f32[4096]{0:T(1024)} %param.8) | copy-start | bytes 49156
  0.0 5.0 %collective-permute-start = (bf16[4,4096]{1,0:T(4,128)(2,1)}, bf16[4,4096]{1,0:T(4,128)(2,1)S(1)}, u32[]{:S(2)}, u32[]{:S(2)}) collective-permute-start(bf16[4,4096]{1,0:T(4,128)(2,1)} %x_ref.1), channel_id=1, source_target_pairs={{0,2},{2,0},{4,6},{6,4},{8,10},{10,8},{12,14},{14,12},{1,3},{3,1},... | collective-permute-start | bytes 98312 | tf_op jit(solution)/shard_map/ppermute | solution.py:34
  2.9 11.5 %copy-start = (bf16[1,3,1024,4096]{3,2,1,0:T(8,128)(2,1)S(1)}, bf16[1,3,1024,4096]{3,2,1,0:T(8,128)(2,1)}, u32[]{:S(2)}) copy-start(bf16[1,3,1024,4096]{3,2,1,0:T(8,128)(2,1)} %w_ref.1) | copy-start | bytes 75497472
  5.1 6.6 %collective-permute-start.1 = (bf16[8,4096]{1,0:T(8,128)(2,1)S(1)}, bf16[8,4096]{1,0:T(8,128)(2,1)S(1)}, u32[]{:S(2)}, u32[]{:S(2)}) collective-permute-start(bf16[8,4096]{1,0:T(8,128)(2,1)S(1)} %stack.3.refs_0_), channel_id=1, source_target_pairs={{0,12},{2,14},{4,8},{6,10},{8,4},{10,6},{12,0},{14,2},{1,13},{3,15... | collective-permute-start | bytes 196616 | tf_op jit(solution)/shard_map/ppermute | solution.py:34
  9.3 5.2 %collective-permute-start.2 = (bf16[8,4096]{1,0:T(8,128)(2,1)S(1)}, bf16[8,4096]{1,0:T(8,128)(2,1)S(1)}, u32[]{:S(2)}, u32[]{:S(2)}) collective-permute-start(bf16[8,4096]{1,0:T(8,128)(2,1)S(1)} %stack.3.refs_0_), channel_id=1, source_target_pairs={{0,8},{2,10},{4,12},{6,14},{8,0},{10,2},{12,4},{14,6},{1,9},{3,11}... | collective-permute-start | bytes 196616 | tf_op jit(solution)/shard_map/ppermute | solution.py:34
  9.3 5.2 %collective-permute-start.3 = (bf16[8,4096]{1,0:T(8,128)(2,1)S(1)}, bf16[8,4096]{1,0:T(8,128)(2,1)S(1)}, u32[]{:S(2)}, u32[]{:S(2)}) collective-permute-start(bf16[8,4096]{1,0:T(8,128)(2,1)S(1)} %stack.3.refs_0_), channel_id=1, source_target_pairs={{0,4},{2,6},{4,0},{6,2},{8,12},{10,14},{12,8},{14,10},{1,5},{3,7},... | collective-permute-start | bytes 196616 | tf_op jit(solution)/shard_map/ppermute | solution.py:34
  18.0 3.5 %collective-permute-start.4 = (f32[32,1664]{1,0:T(8,128)S(1)}, f32[32,1664]{1,0:T(8,128)S(1)}, u32[]{:S(2)}, u32[]{:S(2)}) collective-permute-start(f32[32,1664]{1,0:T(8,128)S(1)} %get-tuple-element.17.refs_2_), channel_id=1, source_target_pairs={{0,1},{1,0},{2,3},{3,2},{4,5},{5,4},{6,7},{7,6},{8,9},{9,8},{10,11... | collective-permute-start | bytes 638984 | tf_op jit(solution)/shard_map/ppermute | solution.py:209
  18.1 3.4 %copy-start.1 = (f32[7,3,1024]{2,0,1:T(8,128)S(1)}, f32[7,3,1024]{2,0,1:T(8,128)}, u32[]{:S(2)}) copy-start(f32[7,3,1024]{2,0,1:T(8,128)} %param.10) | copy-start | bytes 258052
  18.1 3.4 %copy-start.3 = (f32[1024]{0:T(1024)S(1)}, f32[1024]{0:T(1024)}, u32[]{:S(2)}) copy-start(f32[1024]{0:T(1024)} %param.12) | copy-start | bytes 12292
  21.9 5.8 %collective-permute-start.8 = (bf16[32,512]{1,0:T(8,128)(2,1)S(1)}, bf16[32,512]{1,0:T(8,128)(2,1)S(1)}, u32[]{:S(2)}, u32[]{:S(2)}) collective-permute-start(bf16[32,512]{1,0:T(8,128)(2,1)S(1)} %mix.1.refs_0_), channel_id=1, source_target_pairs={{0,12},{2,14},{4,8},{6,10},{8,4},{10,6},{12,0},{14,2},{1,13},{3,15... | collective-permute-start | bytes 98312 | tf_op jit(solution)/shard_map/ppermute | solution.py:34
  24.1 5.1 %collective-permute-start.5 = (bf16[32,512]{1,0:T(8,128)(2,1)S(1)}, bf16[32,512]{1,0:T(8,128)(2,1)S(1)}, u32[]{:S(2)}, u32[]{:S(2)}) collective-permute-start(bf16[32,512]{1,0:T(8,128)(2,1)S(1)} %mix.1.refs_0_), channel_id=1, source_target_pairs={{0,8},{2,10},{4,12},{6,14},{8,0},{10,2},{12,4},{14,6},{1,9},{3,11}... | collective-permute-start | bytes 98312 | tf_op jit(solution)/shard_map/ppermute | solution.py:34
  24.1 5.1 %collective-permute-start.6 = (bf16[32,512]{1,0:T(8,128)(2,1)S(1)}, bf16[32,512]{1,0:T(8,128)(2,1)S(1)}, u32[]{:S(2)}, u32[]{:S(2)}) collective-permute-start(bf16[32,512]{1,0:T(8,128)(2,1)S(1)} %mix.1.refs_0_), channel_id=1, source_target_pairs={{0,4},{2,6},{4,0},{6,2},{8,12},{10,14},{12,8},{14,10},{1,5},{3,7},... | collective-permute-start | bytes 98312 | tf_op jit(solution)/shard_map/ppermute | solution.py:34
  27.7 4.6 %collective-permute-start.9 = (bf16[64,512]{1,0:T(8,128)(2,1)S(1)}, bf16[64,512]{1,0:T(8,128)(2,1)S(1)}, u32[]{:S(2)}, u32[]{:S(2)}) collective-permute-start(bf16[64,512]{1,0:T(8,128)(2,1)S(1)} %stack.5.refs_0_), channel_id=1, source_target_pairs={{0,2},{2,0},{4,6},{6,4},{8,10},{10,8},{12,14},{14,12},{1,3},{3,1},... | collective-permute-start | bytes 196616 | tf_op jit(solution)/shard_map/ppermute | solution.py:34
  29.2 4.3 %collective-permute-start.7 = (bf16[64,512]{1,0:T(8,128)(2,1)S(1)}, bf16[64,512]{1,0:T(8,128)(2,1)S(1)}, u32[]{:S(2)}, u32[]{:S(2)}) collective-permute-start(bf16[64,512]{1,0:T(8,128)(2,1)S(1)} %stack.4.refs_1_), channel_id=1, source_target_pairs={{0,2},{2,0},{4,6},{6,4},{8,10},{10,8},{12,14},{14,12},{1,3},{3,1},... | collective-permute-start | bytes 196616 | tf_op jit(solution)/shard_map/ppermute | solution.py:34
  34.3 1.4 %collective-permute-start.10 = (f32[32,1024]{1,0:T(8,128)S(1)}, f32[32,1024]{1,0:T(8,128)S(1)}, u32[]{:S(2)}, u32[]{:S(2)}) collective-permute-start(f32[32,1024]{1,0:T(8,128)S(1)} %project_out.5.a_ref), channel_id=1, source_target_pairs={{0,1},{1,0},{2,3},{3,2},{4,5},{5,4},{6,7},{7,6},{8,9},{9,8},{10,11... | collective-permute-start | bytes 393224 | tf_op jit(solution)/shard_map/ppermute | solution.py:321

commit v7 on v6

--- a/solution.py
+++ b/solution.py
@@ -75,15 +75,14 @@
     return pl.multiple_of((mine if which == "own" else 1 - mine) * chan, chan)
 
 
-def prepare_kernel(x_ref, taps_ref, local_ref, spread_ref, group_taps, sems):
+def prepare_kernel(x_ref, taps_ref, local_ref, spread_ref, group_taps, sem):
     chan = spread_ref.shape[1]
     groups = group_taps.shape[0]
     index = lax.axis_index("seq") * 2 + lax.axis_index("mdl")
     near = pl.ds(pl.multiple_of(index * groups, groups), groups)
-    fetch = pltpu.make_async_copy(taps_ref.at[near], group_taps, sems.at[0])
-    move = pltpu.make_async_copy(x_ref, local_ref, sems.at[1])
+    fetch = pltpu.make_async_copy(taps_ref.at[near], group_taps, sem)
     fetch.start()
-    move.start()
+    local_ref[...] = x_ref[...]
     fetch.wait()
     grp = lax.broadcasted_iota(jnp.int32, (groups, chan), 0)
     ch = lax.broadcasted_iota(jnp.int32, (groups, chan), 1)
@@ -95,7 +94,6 @@
         preferred_element_type=F32,
         precision=lax.Precision.HIGHEST,
     )[: spread_ref.shape[0]]
-    move.wait()
 
 
 def prepare(x, long_taps, tokens, chan):
@@ -107,16 +105,16 @@
             jax.ShapeDtypeStruct(x.shape, x.dtype),
             jax.ShapeDtypeStruct((reach, chan), F32),
         ),
-        in_specs=[ANY] * 2,
+        in_specs=[VMEM, ANY],
         out_specs=(VMEM,) * 2,
         scratch_shapes=[
             pltpu.VMEM((groups, long_taps.shape[1]), F32),
-            pltpu.SemaphoreType.DMA((2,)),
+            pltpu.SemaphoreType.DMA,
         ],
         compiler_params=params(4),
         cost_estimate=cost(12 * 10**9, 4 * MIB),
         name="prepare",
-    )(in_hbm(x), in_hbm(long_taps))
+    )(x, in_hbm(long_taps))
 
 
 def place_rows(pieces, owners, out_ref):

time: 36.5 us -> 36.7 us (level)
  local copies, waits for them, and re-layouts: 0.02 us -> 0.81 us
  starting transfers between devices: 15.3 us -> 14.9 us
    unnamed x8 -> x10, local copies, waits for them, and re-layouts: 0.02 us -> 0.81 us
    ppermute x9, starting transfers between devices: 15.2 us -> 14.8 us  [swap(): return lax.ppermute(x, 'seq', [(i, i ^ bits) for i in range(count)])]
  transfers between devices with their start and end apart: 11 -> 11, of which waited for: 7 -> 6; matrix products, arithmetic and copies ran while one was open for 0% -> 0% of each run, Pallas kernels for 18% -> 18%
where the time goes in v7:
time: 36.7 us; the launch traced here: 36.5 us
  starting transfers between devices  14.9 us (41%)
  Pallas kernels  12 us (33%)
  waiting for transfers between devices  8.63 us (24%)
  local copies, waits for them, and re-layouts  0.81 us (2%)
    ppermute x9, starting transfers between devices, swap(): return lax.ppermute(x, 'seq', [(i, i ^ bits) for i in range(count)])  14.8 us
    ppermute x9, waiting for transfers between devices, swap(): return lax.ppermute(x, 'seq', [(i, i ^ bits) for i in range(count)])  7.29 us
    pallas_call x1, Pallas kernels, project(): pl.pallas_call(functools.partial(partner_kernel, owners=owners), out_shap...  3.51 us
    pallas_call x1, Pallas kernels, project(): pl.pallas_call(own_kernel, out_shape=(jax.ShapeDtypeStruct((tokens, 3 * c...  3.36 us
    pallas_call x3, Pallas kernels, project_out(): pl.pallas_call(functools.partial(out_kernel, count=len(pieces), owners=ow...  2.76 us
    ppermute x1, waiting for transfers between devices, per_device(): other = lax.ppermute(partial_out, 'mdl', [(0, 1), (1, 0)])  1.33 us
    pallas_call x1, Pallas kernels, prepare(): pl.pallas_call(prepare_kernel, out_shape=(jax.ShapeDtypeStruct(x.shape, x...  1.29 us
    unnamed x10, local copies, waits for them, and re-layouts  0.81 us
  transfers between devices with their start and end apart: 11, of which 6 were waited for; matrix products, arithmetic and copies ran while one was open for 0% of the time, Pallas kernels for 18%

profile of v7, /device:TPU:0, one launch (start us, length us, event | category | flops | bytes accessed | tf_op | source)
XLA Modules:
  0.0 36.5 jit_solution(14472060430047782728)
XLA Ops:
  0.0 2.9 %collective-permute-start = (bf16[4,4096]{1,0:T(4,128)(2,1)}, bf16[4,4096]{1,0:T(4,128)(2,1)S(1)}, u32[]{:S(2)}, u32[]{:S(2)}) collective-permute-start(bf16[4,4096]{1,0:T(4,128)(2,1)} %x_ref.1), channel_id=1, source_target_pairs={{0,2},{2,0},{4,6},{6,4},{8,10},{10,8},{12,14},{14,12},{1,3},{3,1},... | collective-permute-start | bytes 98312 | tf_op jit(solution)/shard_map/ppermute | solution.py:34
  2.9 0.8 %copy-done.4 = bf16[4,4096]{1,0:T(4,128)(2,1)S(1)} copy-done((bf16[4,4096]{1,0:T(4,128)(2,1)S(1)}, bf16[4,4096]{1,0:T(4,128)(2,1)}, u32[]{:S(2)}) %copy-start.4) | copy-done | bytes 32792
  3.7 1.3 %prepare.1 = (bf16[4,4096]{1,0:T(4,128)(2,1)S(1)}, f32[32,512]{1,0:T(8,128)S(1)}) custom-call(bf16[4,4096]{1,0:T(4,128)(2,1)S(1)} %copy-done.4, f32[512,128]{1,0:T(8,128)} %taps_ref.1), custom_call_target="tpu_custom_call" | custom-call | flops 12000000000 | bytes 4194304 | tf_op jit(solution)/shard_map/prepare/pallas_call | solution.py:102
  5.0 0.0 collective-permute-done.refs_1_
  5.1 4.2 %collective-permute-start.1 = (bf16[8,4096]{1,0:T(8,128)(2,1)S(1)}, bf16[8,4096]{1,0:T(8,128)(2,1)S(1)}, u32[]{:S(2)}, u32[]{:S(2)}) collective-permute-start(bf16[8,4096]{1,0:T(8,128)(2,1)S(1)} %stack.3.refs_0_), channel_id=1, source_target_pairs={{0,12},{2,14},{4,8},{6,10},{8,4},{10,6},{12,0},{14,2},{1,13},{3,15... | collective-permute-start | bytes 196616 | tf_op jit(solution)/shard_map/ppermute | solution.py:34
  9.3 0.0 collective-permute-start.2
  9.3 0.6 %collective-permute-start.3 = (bf16[8,4096]{1,0:T(8,128)(2,1)S(1)}, bf16[8,4096]{1,0:T(8,128)(2,1)S(1)}, u32[]{:S(2)}, u32[]{:S(2)}) collective-permute-start(bf16[8,4096]{1,0:T(8,128)(2,1)S(1)} %stack.3.refs_0_), channel_id=1, source_target_pairs={{0,4},{2,6},{4,0},{6,2},{8,12},{10,14},{12,8},{14,10},{1,5},{3,7},... | collective-permute-start | bytes 196616 | tf_op jit(solution)/shard_map/ppermute | solution.py:34
  9.9 2.1 %collective-permute-done.1.refs_1_ = bf16[8,4096]{1,0:T(8,128)(2,1)S(1)} collective-permute-done((bf16[8,4096]{1,0:T(8,128)(2,1)S(1)}, bf16[8,4096]{1,0:T(8,128)(2,1)S(1)}, u32[]{:S(2)}, u32[]{:S(2)}) %collective-permute-start.1) | collective-permute-done | bytes 65568 | tf_op jit(solution)/shard_map/ppermute | solution.py:34
  12.0 2.6 %collective-permute-done.2.refs_2_ = bf16[8,4096]{1,0:T(8,128)(2,1)S(1)} collective-permute-done((bf16[8,4096]{1,0:T(8,128)(2,1)S(1)}, bf16[8,4096]{1,0:T(8,128)(2,1)S(1)}, u32[]{:S(2)}, u32[]{:S(2)}) %collective-permute-start.2) | collective-permute-done | bytes 65568 | tf_op jit(solution)/shard_map/ppermute | solution.py:34
  14.6 0.0 collective-permute-done.3.refs_3_
  14.6 3.5 %project_partner.1 = (f32[32,1664]{1,0:T(8,128)S(1)}, bf16[32,4096]{1,0:T(8,128)(2,1)S(1)}, bf16[4096,32]{1,0:T(8,128)(2,1)S(1)}, bf16[512,4096]{1,0:T(8,128)(2,1)S(1)}) custom-call(bf16[8,4096]{1,0:T(8,128)(2,1)S(1)} %stack.3.refs_0_, bf16[8,4096]{1,0:T(8,128)(2,1)S(1)} %collective-permute-done.1.refs_1_, ...), custom_call_target="tpu_custom_call" | custom-call | flops 402653184 | bytes 12582912 | tf_op jit(solution)/shard_map/project_partner/pallas_call | solution.py:189
  18.2 0.1 collective-permute-start.4
  18.2 0.0 copy-start.1
  18.2 0.0 copy-start.3
  18.3 3.4 %project_own.1 = (f32[32,1536]{1,0:T(8,128)S(1)}, bf16[512,4096]{1,0:T(8,128)(2,1)S(1)}) custom-call(bf16[32,4096]{1,0:T(8,128)(2,1)S(1)} %get-tuple-element.14.xg_ref, bf16[4096,32]{1,0:T(8,128)(2,1)S(1)} %get-tuple-element.15.xt_ref, bf16[1,3,1024,4096]{3,2,1,0:T(8,128)(2,1)S(1)} %copy-done, bf16[1024,4096]{1,0:T(8,128)(2,1)} %bitcast.8), custom_call_target="tpu_custom_call" | custom-call | flops 402653184 | bytes 12582912 | tf_op jit(solution)/shard_map/project_own/pallas_call | solution.py:208
  21.6 0.0 collective-permute-done.4.refs_1_
  21.7 0.4 %mix.1.refs_0_ = bf16[32,512]{1,0:T(8,128)(2,1)S(1)} custom-call(f32[32,1536]{1,0:T(8,128)S(1)} %get-tuple-element.16.refs_0_, f32[32,1664]{1,0:T(8,128)S(1)} %collective-permute-done.4.refs_1_, f32[32,1664]{1,0:T(8,128)S(1)} %get-tuple-element.17.refs_2_, f32[3,7,1024]{2,1,0:T(8,128)S(1)} %bitcast.4, f32[1,1024]{1,0:T(1,128)S(1)} %bitcast.6, ...), custom_call_target="tpu_custom_call" | custom-call | tf_op jit(solution)/shard_map/mix/pallas_call | solution.py:260
  22.1 2.3 %collective-permute-start.8 = (bf16[32,512]{1,0:T(8,128)(2,1)S(1)}, bf16[32,512]{1,0:T(8,128)(2,1)S(1)}, u32[]{:S(2)}, u32[]{:S(2)}) collective-permute-start(bf16[32,512]{1,0:T(8,128)(2,1)S(1)} %mix.1.refs_0_), channel_id=1, source_target_pairs={{0,12},{2,14},{4,8},{6,10},{8,4},{10,6},{12,0},{14,2},{1,13},{3,15... | collective-permute-start | bytes 98312 | tf_op jit(solution)/shard_map/ppermute | solution.py:34
  24.4 0.0 collective-permute-start.5
  24.4 2.1 %collective-permute-start.6 = (bf16[32,512]{1,0:T(8,128)(2,1)S(1)}, bf16[32,512]{1,0:T(8,128)(2,1)S(1)}, u32[]{:S(2)}, u32[]{:S(2)}) collective-permute-start(bf16[32,512]{1,0:T(8,128)(2,1)S(1)} %mix.1.refs_0_), channel_id=1, source_target_pairs={{0,4},{2,6},{4,0},{6,2},{8,12},{10,14},{12,8},{14,10},{1,5},{3,7},... | collective-permute-start | bytes 98312 | tf_op jit(solution)/shard_map/ppermute | solution.py:34
  26.5 1.5 %collective-permute-done.8.refs_1_ = bf16[32,512]{1,0:T(8,128)(2,1)S(1)} collective-permute-done((bf16[32,512]{1,0:T(8,128)(2,1)S(1)}, bf16[32,512]{1,0:T(8,128)(2,1)S(1)}, u32[]{:S(2)}, u32[]{:S(2)}) %collective-permute-start.8) | collective-permute-done | bytes 32800 | tf_op jit(solution)/shard_map/ppermute | solution.py:34
  28.1 1.2 %collective-permute-start.9 = (bf16[64,512]{1,0:T(8,128)(2,1)S(1)}, bf16[64,512]{1,0:T(8,128)(2,1)S(1)}, u32[]{:S(2)}, u32[]{:S(2)}) collective-permute-start(bf16[64,512]{1,0:T(8,128)(2,1)S(1)} %stack.5.refs_0_), channel_id=1, source_target_pairs={{0,2},{2,0},{4,6},{6,4},{8,10},{10,8},{12,14},{14,12},{1,3},{3,1},... | collective-permute-start | bytes 196616 | tf_op jit(solution)/shard_map/ppermute | solution.py:34
  29.2 0.0 collective-permute-done.5.refs_0_
  29.3 1.4 %collective-permute-start.7 = (bf16[64,512]{1,0:T(8,128)(2,1)S(1)}, bf16[64,512]{1,0:T(8,128)(2,1)S(1)}, u32[]{:S(2)}, u32[]{:S(2)}) collective-permute-start(bf16[64,512]{1,0:T(8,128)(2,1)S(1)} %stack.4.refs_1_), channel_id=1, source_target_pairs={{0,2},{2,0},{4,6},{6,4},{8,10},{10,8},{12,14},{14,12},{1,3},{3,1},... | collective-permute-start | bytes 196616 | tf_op jit(solution)/shard_map/ppermute | solution.py:34
  30.7 1.3 %project_out.3.refs_3_ = f32[32,1024]{1,0:T(8,128)S(1)} custom-call(bf16[64,512]{1,0:T(8,128)(2,1)S(1)} %stack.5.refs_0_, bf16[64,512]{1,0:T(8,128)(2,1)S(1)} %stack.4.refs_1_, bf16[512,4096]{1,0:T(8,128)(2,1)S(1)} %get-tuple-element.19.refs_2_.refs_1_, bf16[512,4096]{1,0:T(8,128)(2,1)S(1)} %get-tuple-element.20.refs_3_.refs_2_), custom_call_target="tpu_custom_call" | custom-call | flops 134217728 | bytes 4194304 | tf_op jit(solution)/shard_map/project_out/pallas_call | solution.py:295
  32.0 0.9 %collective-permute-done.9.refs_0_ = bf16[64,512]{1,0:T(8,128)(2,1)S(1)} collective-permute-done((bf16[64,512]{1,0:T(8,128)(2,1)S(1)}, bf16[64,512]{1,0:T(8,128)(2,1)S(1)}, u32[]{:S(2)}, u32[]{:S(2)}) %collective-permute-start.9) | collective-permute-done | bytes 65568 | tf_op jit(solution)/shard_map/ppermute | solution.py:34
  32.9 0.7 %project_out.4.refs_3_ = f32[32,1024]{1,0:T(8,128)S(1)} custom-call(bf16[64,512]{1,0:T(8,128)(2,1)S(1)} %collective-permute-done.9.refs_0_, bf16[512,4096]{1,0:T(8,128)(2,1)S(1)} %get-tuple-element.19.refs_2_.refs_1_, bf16[512,4096]{1,0:T(8,128)(2,1)S(1)} %get-tuple-element.20.refs_3_.refs_2_, f32[32,1024]{1,0:T(8,128)S(1)} %project_out.3.refs_3_), custom_call_target="tpu_custom_call" | custom-call | flops 67108864 | bytes 2097152 | tf_op jit(solution)/shard_map/project_out/pallas_call | solution.py:295
  33.6 0.1 collective-permute-done.7.refs_0_
  33.7 0.7 %project_out.5.a_ref = f32[32,1024]{1,0:T(8,128)S(1)} custom-call(bf16[64,512]{1,0:T(8,128)(2,1)S(1)} %collective-permute-done.7.refs_0_, bf16[512,4096]{1,0:T(8,128)(2,1)S(1)} %get-tuple-element.19.refs_2_.refs_1_, bf16[512,4096]{1,0:T(8,128)(2,1)S(1)} %get-tuple-element.20.refs_3_.refs_2_, f32[32,1024]{1,0:T(8,128)S(1)} %project_out.4.refs_3_), custom_call_target="tpu_custom_call" | custom-call | flops 67108864 | bytes 2097152 | tf_op jit(solution)/shard_map/project_out/pallas_call | solution.py:295
  34.4 0.1 collective-permute-start.10
  34.5 1.3 %collective-permute-done.10.b_ref = f32[32,1024]{1,0:T(8,128)S(1)} collective-permute-done((f32[32,1024]{1,0:T(8,128)S(1)}, f32[32,1024]{1,0:T(8,128)S(1)}, u32[]{:S(2)}, u32[]{:S(2)}) %collective-permute-start.10) | collective-permute-done | bytes 131104 | tf_op jit(solution)/shard_map/ppermute | solution.py:319
  35.8 0.6 %add.1 = bf16[32,1024]{1,0:T(8,128)(2,1)} custom-call(f32[32,1024]{1,0:T(8,128)S(1)} %project_out.5.a_ref, f32[32,1024]{1,0:T(8,128)S(1)} %collective-permute-done.10.b_ref), custom_call_target="tpu_custom_call" | custom-call | tf_op jit(solution)/shard_map/add/pallas_call | solution.py:320
  (11 shorter events, 0.0 us)
Async XLA Ops:
  0.0 14.6 %copy-start.2 = (f32[4096]{0:T(1024)S(1)}, f32[4096]{0:T(1024)}, u32[]{:S(2)}) copy-start(f32[4096]{0:T(1024)} %param.8) | copy-start | bytes 49156
  0.0 5.0 %collective-permute-start = (bf16[4,4096]{1,0:T(4,128)(2,1)}, bf16[4,4096]{1,0:T(4,128)(2,1)S(1)}, u32[]{:S(2)}, u32[]{:S(2)}) collective-permute-start(bf16[4,4096]{1,0:T(4,128)(2,1)} %x_ref.1), channel_id=1, source_target_pairs={{0,2},{2,0},{4,6},{6,4},{8,10},{10,8},{12,14},{14,12},{1,3},{3,1},... | collective-permute-start | bytes 98312 | tf_op jit(solution)/shard_map/ppermute | solution.py:34
  2.9 0.8 %copy-start.4 = (bf16[4,4096]{1,0:T(4,128)(2,1)S(1)}, bf16[4,4096]{1,0:T(4,128)(2,1)}, u32[]{:S(2)}) copy-start(bf16[4,4096]{1,0:T(4,128)(2,1)} %x_ref.1) | copy-start | bytes 98308
  3.7 10.9 %copy-start = (bf16[1,3,1024,4096]{3,2,1,0:T(8,128)(2,1)S(1)}, bf16[1,3,1024,4096]{3,2,1,0:T(8,128)(2,1)}, u32[]{:S(2)}) copy-start(bf16[1,3,1024,4096]{3,2,1,0:T(8,128)(2,1)} %w_ref.1) | copy-start | bytes 75497472
  5.1 6.9 %collective-permute-start.1 = (bf16[8,4096]{1,0:T(8,128)(2,1)S(1)}, bf16[8,4096]{1,0:T(8,128)(2,1)S(1)}, u32[]{:S(2)}, u32[]{:S(2)}) collective-permute-start(bf16[8,4096]{1,0:T(8,128)(2,1)S(1)} %stack.3.refs_0_), channel_id=1, source_target_pairs={{0,12},{2,14},{4,8},{6,10},{8,4},{10,6},{12,0},{14,2},{1,13},{3,15... | collective-permute-start | bytes 196616 | tf_op jit(solution)/shard_map/ppermute | solution.py:34
  9.3 5.4 %collective-permute-start.2 = (bf16[8,4096]{1,0:T(8,128)(2,1)S(1)}, bf16[8,4096]{1,0:T(8,128)(2,1)S(1)}, u32[]{:S(2)}, u32[]{:S(2)}) collective-permute-start(bf16[8,4096]{1,0:T(8,128)(2,1)S(1)} %stack.3.refs_0_), channel_id=1, source_target_pairs={{0,8},{2,10},{4,12},{6,14},{8,0},{10,2},{12,4},{14,6},{1,9},{3,11}... | collective-permute-start | bytes 196616 | tf_op jit(solution)/shard_map/ppermute | solution.py:34
  9.3 5.4 %collective-permute-start.3 = (bf16[8,4096]{1,0:T(8,128)(2,1)S(1)}, bf16[8,4096]{1,0:T(8,128)(2,1)S(1)}, u32[]{:S(2)}, u32[]{:S(2)}) collective-permute-start(bf16[8,4096]{1,0:T(8,128)(2,1)S(1)} %stack.3.refs_0_), channel_id=1, source_target_pairs={{0,4},{2,6},{4,0},{6,2},{8,12},{10,14},{12,8},{14,10},{1,5},{3,7},... | collective-permute-start | bytes 196616 | tf_op jit(solution)/shard_map/ppermute | solution.py:34
  18.2 3.5 %collective-permute-start.4 = (f32[32,1664]{1,0:T(8,128)S(1)}, f32[32,1664]{1,0:T(8,128)S(1)}, u32[]{:S(2)}, u32[]{:S(2)}) collective-permute-start(f32[32,1664]{1,0:T(8,128)S(1)} %get-tuple-element.17.refs_2_), channel_id=1, source_target_pairs={{0,1},{1,0},{2,3},{3,2},{4,5},{5,4},{6,7},{7,6},{8,9},{9,8},{10,11... | collective-permute-start | bytes 638984 | tf_op jit(solution)/shard_map/ppermute | solution.py:207
  18.2 3.4 %copy-start.1 = (f32[7,3,1024]{2,0,1:T(8,128)S(1)}, f32[7,3,1024]{2,0,1:T(8,128)}, u32[]{:S(2)}) copy-start(f32[7,3,1024]{2,0,1:T(8,128)} %param.10) | copy-start | bytes 258052
  18.2 3.4 %copy-start.3 = (f32[1024]{0:T(1024)S(1)}, f32[1024]{0:T(1024)}, u32[]{:S(2)}) copy-start(f32[1024]{0:T(1024)} %param.12) | copy-start | bytes 12292
  22.1 6.0 %collective-permute-start.8 = (bf16[32,512]{1,0:T(8,128)(2,1)S(1)}, bf16[32,512]{1,0:T(8,128)(2,1)S(1)}, u32[]{:S(2)}, u32[]{:S(2)}) collective-permute-start(bf16[32,512]{1,0:T(8,128)(2,1)S(1)} %mix.1.refs_0_), channel_id=1, source_target_pairs={{0,12},{2,14},{4,8},{6,10},{8,4},{10,6},{12,0},{14,2},{1,13},{3,15... | collective-permute-start | bytes 98312 | tf_op jit(solution)/shard_map/ppermute | solution.py:34
  24.4 4.8 %collective-permute-start.5 = (bf16[32,512]{1,0:T(8,128)(2,1)S(1)}, bf16[32,512]{1,0:T(8,128)(2,1)S(1)}, u32[]{:S(2)}, u32[]{:S(2)}) collective-permute-start(bf16[32,512]{1,0:T(8,128)(2,1)S(1)} %mix.1.refs_0_), channel_id=1, source_target_pairs={{0,8},{2,10},{4,12},{6,14},{8,0},{10,2},{12,4},{14,6},{1,9},{3,11}... | collective-permute-start | bytes 98312 | tf_op jit(solution)/shard_map/ppermute | solution.py:34
  24.4 4.8 %collective-permute-start.6 = (bf16[32,512]{1,0:T(8,128)(2,1)S(1)}, bf16[32,512]{1,0:T(8,128)(2,1)S(1)}, u32[]{:S(2)}, u32[]{:S(2)}) collective-permute-start(bf16[32,512]{1,0:T(8,128)(2,1)S(1)} %mix.1.refs_0_), channel_id=1, source_target_pairs={{0,4},{2,6},{4,0},{6,2},{8,12},{10,14},{12,8},{14,10},{1,5},{3,7},... | collective-permute-start | bytes 98312 | tf_op jit(solution)/shard_map/ppermute | solution.py:34
  28.1 4.9 %collective-permute-start.9 = (bf16[64,512]{1,0:T(8,128)(2,1)S(1)}, bf16[64,512]{1,0:T(8,128)(2,1)S(1)}, u32[]{:S(2)}, u32[]{:S(2)}) collective-permute-start(bf16[64,512]{1,0:T(8,128)(2,1)S(1)} %stack.5.refs_0_), channel_id=1, source_target_pairs={{0,2},{2,0},{4,6},{6,4},{8,10},{10,8},{12,14},{14,12},{1,3},{3,1},... | collective-permute-start | bytes 196616 | tf_op jit(solution)/shard_map/ppermute | solution.py:34
  29.3 4.5 %collective-permute-start.7 = (bf16[64,512]{1,0:T(8,128)(2,1)S(1)}, bf16[64,512]{1,0:T(8,128)(2,1)S(1)}, u32[]{:S(2)}, u32[]{:S(2)}) collective-permute-start(bf16[64,512]{1,0:T(8,128)(2,1)S(1)} %stack.4.refs_1_), channel_id=1, source_target_pairs={{0,2},{2,0},{4,6},{6,4},{8,10},{10,8},{12,14},{14,12},{1,3},{3,1},... | collective-permute-start | bytes 196616 | tf_op jit(solution)/shard_map/ppermute | solution.py:34
  34.4 1.4 %collective-permute-start.10 = (f32[32,1024]{1,0:T(8,128)S(1)}, f32[32,1024]{1,0:T(8,128)S(1)}, u32[]{:S(2)}, u32[]{:S(2)}) collective-permute-start(f32[32,1024]{1,0:T(8,128)S(1)} %project_out.5.a_ref), channel_id=1, source_target_pairs={{0,1},{1,0},{2,3},{3,2},{4,5},{5,4},{6,7},{7,6},{8,9},{9,8},{10,11... | collective-permute-start | bytes 393224 | tf_op jit(solution)/shard_map/ppermute | solution.py:319
